TPU v7x, 32 devices: a whole 2x2x4 slice. The times are simulated.
32 devices in a mesh: ep: 8 (over z, x), tp: 4 (over y, core).
Axes of the slice: x: 2, y: 2, z: 4, core: 2. Of those that a mesh axis runs over, the one named last changes fastest.
Arguments:
- tokens: bfloat16 [1024, 4096], P('ep', 'tp'), may hold values from -6 to 6
- out_grad: bfloat16 [1024, 4096], P('ep', 'tp'), may hold values from -6 to 6
- routes: int32 [1024, 4], P('ep'), may hold values from 0 to 7, all different within a row; in each aligned block of 128 rows (0 to 127, 128 to 255, ...) at most 128 rows name the same one
- probs: bfloat16 [1024, 4], P('ep'), may hold values from 0.019897461 to 0.59765625
- w_in: bfloat16 [8, 2, 1536, 4096], P('ep', None, 'tp'), as said below
- w_out: bfloat16 [8, 1536, 4096], P('ep', 'tp'), as said below
Outputs:
- in_grad: bfloat16 [1024, 4096], P('ep', 'tp')
- grad_in: bfloat16 [8, 2, 1536, 4096], P('ep', None, 'tp')
- grad_out: bfloat16 [8, 1536, 4096], P('ep', 'tp')
Inputs may be any that keep to these rules, and one draw needn't show every extreme that they name: `routes`: each token names 4 different copies; within the tokens of one device (aligned blocks of 128 tokens) no copy is named more than 128 times, a bound that some block reaches. `w_in`: copies c and c + 4 hold equal weights. `w_out`: copies c and c + 4 hold equal weights.
All inputs are finite; a program needn't handle non-finite values.
Results may differ from a plain program's by a relative error of at most 0.02.
Values may be sent and summed in bfloat16 or wider, within the bound.
No kernel may reach another device: no remote copies, remote signals or barrier semaphores. Data moves between devices by JAX's collectives and lax.ppermute only.
A program may use at most 128 MiB of HBM per device.

v0:
```python
import jax
import jax.numpy as jnp
from jax import lax
from jax.sharding import PartitionSpec as P


def partner(block, axis, apart):
    count = lax.axis_size(axis)
    route = []
    for low in range(count):
        high = low | 1 << apart
        if high != low and high < count:
            route += [(low, high), (high, low)]
    return lax.ppermute(block, axis, route)


def slot_tables(block_routes, copies, cap):
    flat = block_routes.reshape(-1)
    nrows = flat.shape[0]
    onehot = (flat[:, None] == jnp.arange(copies, dtype=jnp.int32)[None, :]).astype(jnp.int32)
    ranks = jnp.sum((jnp.cumsum(onehot, axis=0) - 1) * onehot, axis=1)
    slot = flat * cap + ranks
    source = (
        jnp.full((copies * cap,), nrows, jnp.int32).at[slot].set(jnp.arange(nrows, dtype=jnp.int32))
    )
    return (slot, source)


def body(tokens, out_grad, routes, probs, w_in, w_out):
    n_ep = lax.axis_size("ep")
    tok_dev, top = routes.shape
    nrows = tok_dev * top
    cap = 2 * nrows // n_ep
    slot, source = slot_tables(routes, n_ep, cap)
    valid = source < nrows
    local = jnp.minimum(source, nrows - 1)
    tok_index = local // top
    scale = jnp.where(valid, probs.reshape(-1)[local].astype(jnp.float32), 0.0)[:, None]
    full_x, full_g = (
        lax.all_gather(tokens, "tp", axis=1, tiled=True),
        lax.all_gather(out_grad, "tp", axis=1, tiled=True),
    )
    packed_x = jnp.where(valid[:, None], full_x[tok_index], jnp.zeros((), jnp.bfloat16))
    packed_g = (scale * full_g[tok_index].astype(jnp.float32)).astype(jnp.bfloat16)
    width = full_x.shape[1]
    send_x = packed_x.reshape(n_ep, cap, width)
    send_g = packed_g.reshape(n_ep, cap, width)
    recv_x, recv_g = (
        lax.all_to_all(send_x, "ep", split_axis=0, concat_axis=0, tiled=True),
        lax.all_to_all(send_g, "ep", split_axis=0, concat_axis=0, tiled=True),
    )
    width = recv_x.shape[2]
    rows_x = recv_x.reshape(n_ep * cap, width)
    rows_g = recv_g.reshape(n_ep * cap, width)
    w_gate = w_in[0, 0]
    w_up = w_in[0, 1]
    w_down = w_out[0]
    contract_last = (((1,), (1,)), ((), ()))
    a = lax.dot_general(rows_x, w_gate, contract_last, preferred_element_type=jnp.float32)
    b = lax.dot_general(rows_x, w_up, contract_last, preferred_element_type=jnp.float32)
    sig = jax.nn.sigmoid(a)
    silu = a * sig
    hidden = (silu * b).astype(jnp.bfloat16)
    dh = lax.dot_general(rows_g, w_down, contract_last, preferred_element_type=jnp.float32)
    da = (dh * b * sig * (1.0 + a * (1.0 - sig))).astype(jnp.bfloat16)
    db = (dh * silu).astype(jnp.bfloat16)
    partial_rows = jnp.dot(da, w_gate, preferred_element_type=jnp.float32)
    partial_rows = partial_rows + jnp.dot(db, w_up, preferred_element_type=jnp.float32)
    summed = lax.psum_scatter(
        partial_rows.reshape(n_ep, cap, width).astype(jnp.bfloat16),
        "tp",
        scatter_dimension=2,
        tiled=True,
    )
    back = lax.all_to_all(summed, "ep", split_axis=0, concat_axis=0, tiled=True)
    picked = back.reshape(n_ep * cap, back.shape[2])[slot]
    in_grad = jnp.sum(
        picked.astype(jnp.float32).reshape(tok_dev, top, back.shape[2]), axis=1
    ).astype(jnp.bfloat16)
    contract_rows = (((0,), (0,)), ((), ()))
    own_in = jnp.stack(
        [
            lax.dot_general(da, rows_x, contract_rows, preferred_element_type=jnp.float32),
            lax.dot_general(db, rows_x, contract_rows, preferred_element_type=jnp.float32),
        ]
    ).astype(jnp.bfloat16)[None]
    own_out = lax.dot_general(
        hidden, rows_g, contract_rows, preferred_element_type=jnp.float32
    ).astype(jnp.bfloat16)[None]
    half_bit = n_ep.bit_length() - 2
    other_in, other_out = partner((own_in, own_out), "ep", half_bit)
    grad_in = (own_in.astype(jnp.float32) + other_in.astype(jnp.float32)).astype(jnp.bfloat16)
    grad_out = (own_out.astype(jnp.float32) + other_out.astype(jnp.float32)).astype(jnp.bfloat16)
    return (in_grad, grad_in, grad_out)


def solution(mesh):
    return jax.shard_map(
        body,
        mesh=mesh,
        in_specs=(
            P("ep", "tp"),
            P("ep", "tp"),
            P("ep", None),
            P("ep", None),
            P("ep", None, "tp", None),
            P("ep", "tp", None),
        ),
        out_specs=(P("ep", "tp"), P("ep", None, "tp", None), P("ep", "tp", None)),
        check_vma=False,
    )
```

profile of v0, /device:TPU:0, one launch (start us, length us, event | category | flops | bytes accessed | tf_op | source)
XLA Modules:
  0.0 950.2 jit_solution(637954491075334123)
XLA Ops:
  15.0 6.8 gather_fusion
  21.8 7.3 all-gather.5.cloned.1.call-done
  29.1 16.4 %gather_fusion.2 = bf16[1024,4096]{1,0:T(8,128)(2,1)} fusion(bf16[128,4096]{1,0:T(8,128)(2,1)} %all-gather.5.cloned.1.call-done, s32[1024]{0:T(1024)S(1)} %get-tuple-element.8), kind=kCustom, calls=%fused_computation.2 | custom fusion | bytes 16781312 | tf_op jit(solution)/shard_map/gather | solution.py:43
  45.5 7.2 broadcast_select_fusion
  52.8 5.5 all-to-all-start.1
  59.0 18.9 %all-gather.3.cloned.1.call-done = bf16[128,4096]{1,0:T(8,128)(2,1)} async-done(((bf16[128,1024]{1,0:T(8,128)(2,1)}), bf16[128,4096]{1,0:T(8,128)(2,1)}) %all-gather.3.cloned.1.call-update) | async-done | bytes 1048592 | tf_op jit(solution)/shard_map/all_gather | solution.py:41
  77.9 16.4 %gather_fusion.1 = bf16[1024,4096]{1,0:T(8,128)(2,1)} fusion(bf16[128,4096]{1,0:T(8,128)(2,1)} %all-gather.3.cloned.1.call-done, s32[1024]{0:T(1024)S(1)} %get-tuple-element.8), kind=kCustom, calls=%fused_computation.1 | custom fusion | bytes 16781312 | tf_op jit(solution)/shard_map/gather | solution.py:44
  94.3 10.0 %fusion = bf16[8,128,4096]{2,1,0:T(8,128)(2,1)} fusion(bf16[8,128,4096]{2,1,0:T(8,128)(2,1)} %bitcast.50, f32[8,128]{1,0:T(8,128)S(1)} %get-tuple-element.3), kind=kLoop, calls=%fused_computation.6 | loop fusion | flops 12582912 | bytes 16781312 | tf_op jit(solution)/shard_map/convert_element_type | solution.py:44
  104.3 137.5 %all-to-all-done.1 = bf16[8,128,4096]{2,1,0:T(8,128)(2,1)} async-done(((bf16[8,128,4096]{2,1,0:T(8,128)(2,1)}), bf16[8,128,4096]{2,1,0:T(8,128)(2,1)}, u32[]{:S(2)}, u32[]{:S(2)}) %all-to-all-start.1) | async-done | bytes 8388640 | tf_op jit(solution)/shard_map/all_to_all | solution.py:49
  247.1 9.9 %fusion.6 = f32[1024,384]{1,0:T(8,128)} fusion(bf16[1024,4096]{1,0:T(8,128)(2,1)} %bitcast.10, bf16[1,2,384,4096]{3,2,1,0:T(8,128)(2,1)} %param.10), kind=kOutput, calls=%fused_computation.20 | convolution fusion | flops 3221225472 | bytes 13107200 | tf_op jit(solution)/shard_map/dot_general | solution.py:59
  257.0 9.9 %fusion.9 = f32[1024,384]{1,0:T(8,128)} fusion(bf16[1024,4096]{1,0:T(8,128)(2,1)} %bitcast.10, bf16[1,2,384,4096]{3,2,1,0:T(8,128)(2,1)} %param.10), kind=kOutput, calls=%fused_computation.23 | convolution fusion | flops 3221225472 | bytes 13107200 | tf_op jit(solution)/shard_map/dot_general | solution.py:60
  266.9 162.6 %all-to-all-done = bf16[8,128,4096]{2,1,0:T(8,128)(2,1)} async-done(((bf16[8,128,4096]{2,1,0:T(8,128)(2,1)}), bf16[8,128,4096]{2,1,0:T(8,128)(2,1)}, u32[]{:S(2)}, u32[]{:S(2)}) %all-to-all-start) | async-done | bytes 8388640 | tf_op jit(solution)/shard_map/all_to_all | solution.py:50
  429.5 9.2 multiply_convert_fusion.1
  438.8 10.6 %fusion.4 = f32[1024,4096]{1,0:T(8,128)} fusion(bf16[1024,384]{1,0:T(8,128)(2,1)S(1)} %get-tuple-element.6, bf16[1,2,384,4096]{3,2,1,0:T(8,128)(2,1)} %param.10), kind=kOutput, calls=%fused_computation.18 | convolution fusion | flops 3221225472 | bytes 20709376 | tf_op jit(solution)/shard_map/dot_general | solution.py:67
  449.3 11.2 %add_convert_fusion = bf16[1024,4096]{1,0:T(8,128)(2,1)} fusion(f32[1024,4096]{1,0:T(8,128)} %fusion.4, bf16[1024,384]{1,0:T(8,128)(2,1)S(1)} %get-tuple-element.5, bf16[1,2,384,4096]{3,2,1,0:T(8,128)(2,1)} %param.10), kind=kOutput, calls=%fused_computation.7 | convolution fusion | flops 3229614080 | bytes 29097984 | tf_op jit(solution)/shard_map/dot_general | solution.py:68
  460.6 7.2 fusion.1
  467.9 8.7 fusion.2
  480.9 9.4 fusion.3
  493.2 37.4 %reduce-scatter.2.cloned.1.call-done = bf16[8,128,1024]{2,1,0:T(8,128)(2,1)} async-done(((bf16[8,128,4096]{2,1,0:T(8,128)(2,1)}), bf16[8,128,1024]{2,1,0:T(8,128)(2,1)}) %reduce-scatter.2.cloned.1.call-update) | async-done | bytes 2097168 | tf_op jit(solution)/shard_map/reduce_scatter | solution.py:69
  530.6 5.8 all-to-all-start.2
  536.4 375.0 %collective-permute-done.1 = bf16[1,384,4096]{2,1,0:T(8,128)(2,1)} collective-permute-done((bf16[1,384,4096]{2,1,0:T(8,128)(2,1)}, bf16[1,384,4096]{2,1,0:T(8,128)(2,1)}, u32[]{:S(2)}, u32[]{:S(2)}) %collective-permute-start.1) | collective-permute-done | bytes 3145760 | tf_op jit(solution)/shard_map/ppermute | solution.py:14
  911.4 5.8 add_convert_fusion.2
  917.3 7.5 add_convert_fusion.1
  924.8 7.5 all-to-all-done.2
  (52 shorter events, 31.9 us)
Async XLA Ops:
  7.2 422.4 %copy-start = (bf16[1,384,4096]{2,1,0:T(8,128)(2,1)S(1)}, bf16[1,384,4096]{2,1,0:T(8,128)(2,1)}, u32[]{:S(2)}) copy-start(bf16[1,384,4096]{2,1,0:T(8,128)(2,1)} %param.11) | copy-start | bytes 9437188
  7.2 21.9 %all-gather.5.cloned.1.call-start = ((), (), s32[]{:S(2)}) async-start(), calls=%async_computation.5 | async-start | bytes 1310720 | tf_op jit(solution)/shard_map/all_gather | solution.py:40
  52.8 189.1 %all-to-all-start.1 = ((bf16[8,128,4096]{2,1,0:T(8,128)(2,1)}), bf16[8,128,4096]{2,1,0:T(8,128)(2,1)}, u32[]{:S(2)}, u32[]{:S(2)}) async-start(bf16[8,128,4096]{2,1,0:T(8,128)(2,1)} %broadcast_select_fusion), calls=%async_computation.1 | async-start | bytes 16777216 | tf_op jit(solution)/shard_map/all_to_all | solution.py:49
  58.3 19.6 %all-gather.3.cloned.1.call-start = ((), (), s32[]{:S(2)}) async-start(), calls=%async_computation.4 | async-start | bytes 1310720 | tf_op jit(solution)/shard_map/all_gather | solution.py:41
  241.8 187.7 %all-to-all-start = ((bf16[8,128,4096]{2,1,0:T(8,128)(2,1)}), bf16[8,128,4096]{2,1,0:T(8,128)(2,1)}, u32[]{:S(2)}, u32[]{:S(2)}) async-start(bf16[8,128,4096]{2,1,0:T(8,128)(2,1)} %fusion), calls=%async_computation | async-start | bytes 16777216 | tf_op jit(solution)/shard_map/all_to_all | solution.py:50
  246.9 283.7 %reduce-scatter.2.cloned.1.call-start = ((), (), s32[]{:S(2)}) async-start(), calls=%async_computation.6 | async-start | bytes 10485760 | tf_op jit(solution)/shard_map/reduce_scatter | solution.py:69
  438.8 10.6 %copy-start.6 = (bf16[1024,384]{1,0:T(8,128)(2,1)}, bf16[1024,384]{1,0:T(8,128)(2,1)S(1)}, u32[]{:S(2)}) copy-start(bf16[1024,384]{1,0:T(8,128)(2,1)S(1)} %get-tuple-element.6) | copy-start | bytes 2359300
  438.8 10.6 %copy-start.4 = (bf16[1024,384]{1,0:T(8,128)(2,1)}, bf16[1024,384]{1,0:T(8,128)(2,1)S(1)}, u32[]{:S(2)}) copy-start(bf16[1024,384]{1,0:T(8,128)(2,1)S(1)} %get-tuple-element.5) | copy-start | bytes 2359300
  460.6 7.3 copy-start.5
  476.6 4.3 copy-start.2
  476.6 4.3 copy-start.7
  476.6 4.3 copy-start.8
  480.9 436.4 %collective-permute-start = (bf16[1,2,384,4096]{3,2,1,0:T(8,128)(2,1)}, bf16[1,2,384,4096]{3,2,1,0:T(8,128)(2,1)}, u32[]{:S(2)}, u32[]{:S(2)}) collective-permute-start(bf16[1,2,384,4096]{3,2,1,0:T(8,128)(2,1)} %pad_maximum_fusion), channel_id=1, source_target_pairs={{0,16},{16,0},{4,20},{20,4},{8,24},{24,8},{12,28},{28,12},{1,17},{... | collective-permute-start | bytes 18874376 | tf_op jit(solution)/shard_map/ppermute | solution.py:14
  490.3 421.2 %collective-permute-start.1 = (bf16[1,384,4096]{2,1,0:T(8,128)(2,1)}, bf16[1,384,4096]{2,1,0:T(8,128)(2,1)}, u32[]{:S(2)}, u32[]{:S(2)}) collective-permute-start(bf16[1,384,4096]{2,1,0:T(8,128)(2,1)} %fusion.3), channel_id=1, source_target_pairs={{0,16},{16,0},{4,20},{20,4},{8,24},{24,8},{12,28},{28,12},{1,17},{... | collective-permute-start | bytes 9437192 | tf_op jit(solution)/shard_map/ppermute | solution.py:14
  530.6 401.7 %all-to-all-start.2 = ((bf16[8,128,1024]{2,1,0:T(8,128)(2,1)}), bf16[8,128,1024]{2,1,0:T(8,128)(2,1)}, u32[]{:S(2)}, u32[]{:S(2)}) async-start(bf16[8,128,1024]{2,1,0:T(8,128)(2,1)} %reduce-scatter.2.cloned.1.call-done), calls=%async_computation.3 | async-start | bytes 4194304 | tf_op jit(solution)/shard_map/all_to_all | solution.py:75
  536.4 380.9 %copy-start.3 = (bf16[1,1,384,4096]{3,2,1,0:T(8,128)(2,1)S(1)}, bf16[1,1,384,4096]{3,2,1,0:T(8,128)(2,1)}, u32[]{:S(2)}) copy-start(bf16[1,1,384,4096]{3,2,1,0:T(8,128)(2,1)} %copy-done.2) | copy-start | bytes 9437188
  932.3 10.9 %copy-start.1 = (bf16[1,384,4096]{2,1,0:T(8,128)(2,1)S(1)}, bf16[1,384,4096]{2,1,0:T(8,128)(2,1)}, u32[]{:S(2)}) copy-start(bf16[1,384,4096]{2,1,0:T(8,128)(2,1)} %param.11) | copy-start | bytes 9437188
Sparse Core Ops, SparseCore 0:
  9.6 19.4 all-gather.4
  60.7 17.1 all-gather.2
  460.7 69.8 reduce-scatter.1
where the time goes:
time: 958 us; the launch traced here: 950 us
  waiting for transfers between devices  748 us (78%)
  matrix products  76.2 us (8%)
  local copies, waits for them, and re-layouts  53.1 us (6%)
  other arithmetic  39.4 us (4%)
  starting transfers between devices  19.6 us (2%)
  between operations  14.4 us (2%)
    ppermute x2, waiting for transfers between devices, partner(): return lax.ppermute(block, axis, route)  375 us
    all_to_all x1, waiting for transfers between devices, body(): lax.all_to_all(send_g, 'ep', split_axis=0, concat_axis=0, tiled=True)  163 us
    all_to_all x1, waiting for transfers between devices, body(): lax.all_to_all(send_x, 'ep', split_axis=0, concat_axis=0, tiled=True)  138 us
    reduce_scatter x1, waiting for transfers between devices, body(): lax.psum_scatter(partial_rows.reshape(n_ep, cap, width).astype(jnp.bfloat...  37.4 us
  transfers between devices with their start and end apart: 8, of which 7 were waited for; matrix products, arithmetic and copies ran while one was open for 11% of the time, Pallas kernels for 0%

commit v1 on v0

v1 whole, which is shorter than its diff:
```python
import functools

import jax
import jax.numpy as jnp
from jax import lax
from jax.experimental import pallas as pl
from jax.experimental.pallas import tpu as pltpu
from jax.sharding import PartitionSpec as P

BF16 = jnp.bfloat16
F32 = jnp.float32
VMEM_LIMIT = 40 * 1024 * 1024
SHRINK = 1.0 / 64.0


def hop(block, axis, bit):
    count = lax.axis_size(axis)
    return lax.ppermute(block, axis, [(i, i ^ bit) for i in range(count)])


def after(value, *others):
    return lax.optimization_barrier((value,) + others)[0] if others else value


def bits_of(number, letter, skip=0):
    return [f"{letter}{i}" for i in range(skip, number.bit_length() - 1)]


class Lanes:
    def __init__(self, depth):
        self.depth = depth
        self.sent = {}

    def send(self, block, bit, *others):
        queue = self.sent.setdefault(bit, [])
        ready = list(others) + queue[-self.depth : len(queue) - self.depth + 1]
        axis = "ep" if bit[0] == "e" else "tp"
        queue.append(hop(after(block, *ready), axis, 1 << int(bit[1:])))
        return queue[-1]


def gather_plan(n_ep, n_tp):
    if (n_ep, n_tp) == (8, 4):
        x, n, f, y = "e0", "e1", "e2", "t1"
        return [
            ((x,), x, 2), ((y,), y, 2), ((n,), n, 2), ((f,), f, 2),
            ((x, y), x, 0), ((x, y), y, 1), ((x, n), x, 2), ((y, n), y, 2),
            ((x, y, n), n, 2), ((n, f), n, 2), ((x, f), x, 2), ((y, f), y, 2),
            ((x, y, f), x, 0), ((x, y, f), y, 1), ((x, y, n, f), n, 2),
            ((x, n, f), x, 2), ((y, n, f), y, 2),
        ]
    bits = bits_of(n_ep, "e") + bits_of(n_tp, "t", 1)
    plan = []
    for i, bit in enumerate(bits):
        for low in range(1 << i):
            below = tuple(b for j, b in enumerate(bits[:i]) if low >> j & 1)
            plan.append((below + (bit,), bit, 2))
    return plan


def name_of(ep, tp):
    names = [f"e{i}" for i in range(ep.bit_length()) if ep >> i & 1]
    names += [f"t{i + 1}" for i in range(tp.bit_length()) if tp >> i & 1]
    return frozenset(names)


def rows_kernel(n_tp, part, t_ref, p_ref, a_ref, b_ref, win_ref, wout_ref, *rest):
    if part:
        dadb_ref, hid_ref, part_ref, xs, gs, wi, wo, acc, sems = rest
    else:
        dadb_ref, hid_ref, xs, gs, wi, wo, acc, sems = rest
    width = xs.shape[2]
    tok = xs.shape[1] // 2
    ffl = hid_ref.shape[0]
    pairs = n_tp // 2
    copies = []
    for d in range(n_tp):
        src = (a_ref, b_ref)[d % 2]
        column = pl.ds(pl.multiple_of((t_ref[0] ^ d) * width, width), width)
        mine = [
            pltpu.make_async_copy(win_ref.at[:, column], wi.at[d], sems.at[d, 0]),
            pltpu.make_async_copy(wout_ref.at[:, column], wo.at[d], sems.at[d, 1]),
        ]
        for j in range(2):
            for k, dst in enumerate((xs, gs)):
                mine.append(
                    pltpu.make_async_copy(
                        src.at[j * pairs + d // 2, k],
                        dst.at[d, pl.ds(j * tok, tok)],
                        sems.at[d, 2 + 2 * j + k],
                    )
                )
        for copy in mine:
            copy.start()
        copies.append(mine)
    last = (((1,), (1,)), ((), ()))
    for d in range(n_tp):
        for copy in copies[d]:
            copy.wait()
        ab = lax.dot_general(wi[d], xs[d], last, preferred_element_type=F32)
        small = gs[d] * jnp.asarray(SHRINK, BF16)
        h = lax.dot_general(wo[d], small, last, preferred_element_type=F32)
        if d == 0:
            acc[pl.ds(0, 2 * ffl)] = ab
            acc[pl.ds(2 * ffl, ffl)] = h
        else:
            acc[pl.ds(0, 2 * ffl)] += ab
            acc[pl.ds(2 * ffl, ffl)] += h
    a = acc[pl.ds(0, ffl)]
    b = acc[pl.ds(ffl, ffl)]
    scale = p_ref[...]
    named = scale > 0.0
    dh = acc[pl.ds(2 * ffl, ffl)] * (scale * (1.0 / SHRINK))
    sig = jax.nn.sigmoid(a)
    silu = a * sig
    da = dh * b * sig * (1.0 + a * (1.0 - sig))
    dadb_ref[pl.ds(0, ffl)] = jnp.where(named, da, 0.0).astype(BF16)
    dadb_ref[pl.ds(ffl, ffl)] = jnp.where(named, dh * silu, 0.0).astype(BF16)
    hid_ref[...] = jnp.where(named, (0.5 * scale) * (silu * b), 0.0).astype(BF16)
    if part:
        rows = dadb_ref[...].T
        for d in range(n_tp):
            out = jnp.dot(rows, wi[d], preferred_element_type=F32).astype(BF16)
            for j in range(2):
                part_ref[d % 2, j * pairs + d // 2] = out[j * tok : (j + 1) * tok]


def rows_call(part, t, p, a, b, w_in, w_out, n_tp):
    tok, width = a.shape[2:]
    ffl = w_out.shape[0]
    rows = 2 * tok
    outs = [
        jax.ShapeDtypeStruct((2 * ffl, rows), BF16),
        jax.ShapeDtypeStruct((ffl, rows), BF16),
    ]
    if part:
        outs.append(jax.ShapeDtypeStruct((2, n_tp, tok, width), BF16))
    flops = 2 * rows * ffl * n_tp * width * (5 if part else 3)
    vmem = pl.BlockSpec(memory_space=pltpu.VMEM)
    hbm = pl.BlockSpec(memory_space=pl.ANY)
    return pl.pallas_call(
        functools.partial(rows_kernel, n_tp, part),
        out_shape=outs,
        in_specs=[pl.BlockSpec(memory_space=pltpu.SMEM), vmem, hbm, hbm, hbm, hbm],
        out_specs=[vmem] * len(outs),
        scratch_shapes=[
            pltpu.VMEM((n_tp, rows, width), BF16),
            pltpu.VMEM((n_tp, rows, width), BF16),
            pltpu.VMEM((n_tp, 2 * ffl, width), BF16),
            pltpu.VMEM((n_tp, ffl, width), BF16),
            pltpu.VMEM((3 * ffl, rows), F32),
            pltpu.SemaphoreType.DMA((n_tp, 6)),
        ],
        compiler_params=pltpu.CompilerParams(vmem_limit_bytes=VMEM_LIMIT),
        cost_estimate=pl.CostEstimate(
            flops=flops,
            bytes_accessed=2 * (3 * ffl + 2 * rows) * n_tp * width,
            transcendentals=rows * ffl,
        ),
        name="rows",
    )(t, p, a, b, w_in, w_out)


def grads_kernel(n_tp, chunks, t_ref, *refs):
    dadb_refs, hid_refs = refs[:chunks], refs[chunks : 2 * chunks]
    a_refs, b_refs = refs[2 * chunks : 3 * chunks], refs[3 * chunks : 4 * chunks]
    gin_ref, gout_ref, lhs, xs, gs, oi, oo, sems, osems = refs[4 * chunks :]
    width = xs.shape[2]
    pairs = n_tp // 2
    tok = xs.shape[1] // (2 * chunks)
    ffl = oo.shape[1]

    def fetch(d):
        copies = []
        for c in range(chunks):
            src = (a_refs, b_refs)[d % 2][c]
            for j in range(2):
                for k, dst in enumerate((xs, gs)):
                    copies.append(
                        pltpu.make_async_copy(
                            src.at[j * pairs + d // 2, k],
                            dst.at[d % 2, pl.ds((2 * c + j) * tok, tok)],
                            sems.at[d % 2, 2 * c + j, k],
                        )
                    )
        for copy in copies:
            copy.start()
        return copies

    coming = fetch(0)
    for c in range(chunks):
        lhs[pl.ds(0, 2 * ffl), pl.ds(2 * c * tok, 2 * tok)] = dadb_refs[c][...]
        lhs[pl.ds(2 * ffl, ffl), pl.ds(2 * c * tok, 2 * tok)] = hid_refs[c][...]
    leaving = {}
    tile = min(256, width)
    for d in range(n_tp):
        slot = d % 2
        for copy in coming:
            copy.wait()
        if d + 1 < n_tp:
            coming = fetch(d + 1)
        for copy in leaving.pop(d - 2, ()):
            copy.wait()

        def step(i, _, slot=slot):
            cols = pl.ds(pl.multiple_of(i * tile, tile), tile)
            gi = jnp.dot(lhs[pl.ds(0, 2 * ffl)], xs[slot, :, cols], preferred_element_type=F32)
            oi[slot, :, cols] = gi.astype(BF16)
            go = jnp.dot(lhs[pl.ds(2 * ffl, ffl)], gs[slot, :, cols], preferred_element_type=F32)
            oo[slot, :, cols] = (2.0 * go).astype(BF16)
            return 0

        lax.fori_loop(0, width // tile, step, 0)
        column = pl.ds(pl.multiple_of((t_ref[0] ^ d) * width, width), width)
        leaving[d] = (
            pltpu.make_async_copy(oi.at[slot], gin_ref.at[:, column], osems.at[slot, 0]),
            pltpu.make_async_copy(oo.at[slot], gout_ref.at[:, column], osems.at[slot, 1]),
        )
        for copy in leaving[d]:
            copy.start()
    for copies in leaving.values():
        for copy in copies:
            copy.wait()


def grads_call(t, dadb, hid, a, b, n_tp):
    chunks = len(dadb)
    tok, width = a[0].shape[2:]
    ffl = hid[0].shape[0]
    rows = 2 * tok * chunks
    depth = n_tp * width
    vmem = pl.BlockSpec(memory_space=pltpu.VMEM)
    hbm = pl.BlockSpec(memory_space=pl.ANY)
    return pl.pallas_call(
        functools.partial(grads_kernel, n_tp, chunks),
        out_shape=[
            jax.ShapeDtypeStruct((2 * ffl, depth), BF16),
            jax.ShapeDtypeStruct((ffl, depth), BF16),
        ],
        in_specs=[pl.BlockSpec(memory_space=pltpu.SMEM)]
        + [vmem] * (2 * chunks)
        + [hbm] * (2 * chunks),
        out_specs=[hbm, hbm],
        scratch_shapes=[
            pltpu.VMEM((3 * ffl, rows), BF16),
            pltpu.VMEM((2, rows, width), BF16),
            pltpu.VMEM((2, rows, width), BF16),
            pltpu.VMEM((2, 2 * ffl, width), BF16),
            pltpu.VMEM((2, ffl, width), BF16),
            pltpu.SemaphoreType.DMA((2, 2 * chunks, 2)),
            pltpu.SemaphoreType.DMA((2, 2)),
        ],
        compiler_params=pltpu.CompilerParams(vmem_limit_bytes=VMEM_LIMIT),
        cost_estimate=pl.CostEstimate(
            flops=6 * rows * ffl * depth,
            bytes_accessed=2 * (3 * ffl + 2 * rows) * depth,
            transcendentals=0,
        ),
        name="grads",
    )(t, *dadb, *hid, *a, *b)


def scales(routes, probs, n_ep):
    experts = n_ep // 2
    hit = (routes % experts)[None] == jnp.arange(experts, dtype=jnp.int32)[:, None, None]
    own = jnp.sum(jnp.where(hit, probs.astype(F32)[None], 0.0), axis=2)
    every = lax.all_gather(own, "ep", axis=0)
    me = lax.axis_index("ep")
    order = jnp.arange(n_ep, dtype=jnp.int32)
    block = (order[:, None] ^ me) == order[None, :]
    expert = jnp.arange(experts, dtype=jnp.int32) == me % experts
    pick = block[:, :, None, None] & expert[None, None, :, None]
    return jnp.sum(jnp.where(pick, every[None], 0.0), axis=(1, 2))


def body(tokens, out_grad, routes, probs, w_in, w_out):
    n_ep, n_tp = lax.axis_size("ep"), lax.axis_size("tp")
    pairs = n_tp // 2
    chunks = n_ep // 2
    ffl = w_out.shape[1]
    w_in = w_in.reshape(2 * ffl, w_in.shape[3])
    w_out = w_out[0]
    t = lax.axis_index("tp").astype(jnp.int32).reshape(1)
    p = scales(routes, probs, n_ep)

    lanes = Lanes(2)
    have = {frozenset(): {2: jnp.stack([tokens, out_grad])}}

    def held(name, part):
        parts = have[name]
        if part in parts:
            return parts[part]
        if part < 2:
            return parts[2][part]
        parts[2] = jnp.stack([parts[0], parts[1]])
        return parts[2]

    chunk_of = {}
    for c in range(chunks):
        names = [name_of(2 * c + j, y) for j in range(2) for y in range(pairs)]
        chunk_of.update({name: (c, names) for name in names})
    missing = {c: 2 * pairs * 2 for c in range(chunks)}
    missing[0] -= 2
    a, b = {}, {}
    for target, bit, part in gather_plan(n_ep, n_tp):
        target = frozenset(target)
        source = target - {bit}
        have.setdefault(target, {})[part] = lanes.send(held(source, part), bit)
        c, names = chunk_of[target]
        missing[c] -= 2 if part == 2 else 1
        if not missing[c]:
            a[c] = jnp.stack([held(name, 2) for name in names])
            b[c] = lanes.send(a[c], "t0")

    dadb, hid, parts = {}, {}, {}
    for c in range(chunks):
        near = c < chunks // 2
        scale = p[2 * c : 2 * c + 2].reshape(1, -1)
        out = rows_call(near, t, scale, a[c], b[c], w_in, w_out, n_tp)
        dadb[c], hid[c] = out[:2]
        if near:
            parts[c] = out[2]

    terms = {}
    for c in range(chunks // 2):
        far = lanes.send(parts[c][1], "t0")
        both = (parts[c][0].astype(F32) + far.astype(F32)).astype(BF16)
        for j in range(2):
            for y in range(pairs):
                terms[name_of(2 * c + j, y)] = both[j * pairs + y]
    for target, bit, part in reversed(gather_plan(n_ep, n_tp)):
        target = frozenset(target)
        if target not in terms:
            continue
        half = terms[target].shape[0] // 2
        rows = slice(0, None) if part == 2 else slice(part * half, (part + 1) * half)
        come = lanes.send(terms[target][rows], bit)
        into = terms[target - {bit}]
        if part == 2:
            total = (into.astype(F32) + come.astype(F32)).astype(BF16)
        else:
            total = (into[rows].astype(F32) + come.astype(F32)).astype(BF16)
            halves = [into[:half], into[half:]]
            halves[part] = total
            total = jnp.concatenate(halves)
        terms[target - {bit}] = total
    in_grad = terms[frozenset()]

    order = range(chunks)
    grad_in, grad_out = grads_call(
        t, [dadb[c] for c in order], [hid[c] for c in order],
        [a[c] for c in order], [b[c] for c in order], n_tp,
    )
    return in_grad, grad_in.reshape(1, 2, ffl, -1), grad_out[None]


def solution(mesh):
    return jax.shard_map(
        body,
        mesh=mesh,
        in_specs=(
            P("ep", "tp"),
            P("ep", "tp"),
            P("ep", None),
            P("ep", None),
            P("ep", None, "tp", None),
            P("ep", "tp", None),
        ),
        out_specs=(P("ep", "tp"), P("ep", None, "tp", None), P("ep", "tp", None)),
        check_vma=False,
    )
```

time: 958 us -> 187 us (0.20)
  waiting for transfers between devices: 748 us -> 66 us
  matrix products: 76.2 us -> 0 us
  Pallas kernels: 0 us -> 44.7 us
  local copies, waits for them, and re-layouts: 53.1 us -> 9.63 us
  other arithmetic: 39.4 us -> 8.63 us
  blocking collectives: 0 us -> 27.5 us
  between operations: 14.4 us -> 1.03 us
    ppermute x2 -> x31, waiting for transfers between devices: 375 us -> 66 us  [hop(): return lax.ppermute(block, axis, [(i, i ^ bit) for i in range(count)])]
    all_to_all x3 -> x0, waiting for transfers between devices: 308 us -> none  [the longest x1 163 us: body(): lax.all_to_all(send_g, 'ep', split_axis=0, concat_axis=0, tiled=True)]
    dot_general x8 -> x0, matrix products: 76.2 us -> none  [the longest x1 11.2 us: body(): jnp.dot(db, w_up, preferred_element_type=jnp.float32)]
    gather x5 -> x0, local copies, waits for them, and re-layouts: 47.4 us -> none  [the longest x1 16.4 us: body(): full_g[tok_index].astype(jnp.float32)]
    pallas_call x0 -> x5, Pallas kernels: none -> 44.7 us  [the longest x4 28.1 us: rows_call(): pl.pallas_call(functools.partial(rows_kernel, n_tp, part), out_shape=outs...]
    reduce_scatter x1 -> x0, waiting for transfers between devices: 37.4 us -> none  [body(): lax.psum_scatter(partial_rows.reshape(n_ep, cap, width).astype(jnp.bfloat...]
    all_gather x0 -> x1, blocking collectives: none -> 27.5 us  [scales(): every = lax.all_gather(own, 'ep', axis=0)]
    all_gather x2 -> x0, waiting for transfers between devices: 26.2 us -> none  [the longest x1 18.9 us: body(): lax.all_gather(out_grad, 'tp', axis=1, tiled=True)]
  transfers between devices with their start and end apart: 8 -> 31, of which waited for: 7 -> 14; matrix products, arithmetic and copies ran while one was open for 11% -> 4% of each run, Pallas kernels for 0% -> 24%
where the time goes in v1:
time: 187 us; the launch traced here: 186 us
  waiting for transfers between devices  66 us (35%)
  Pallas kernels  44.7 us (24%)
  starting transfers between devices  28.9 us (15%)
  blocking collectives  27.5 us (15%)
  local copies, waits for them, and re-layouts  9.63 us (5%)
  other arithmetic  8.63 us (5%)
    ppermute x31, waiting for transfers between devices, hop(): return lax.ppermute(block, axis, [(i, i ^ bit) for i in range(count)])  66 us
    ppermute x31, starting transfers between devices, hop(): return lax.ppermute(block, axis, [(i, i ^ bit) for i in range(count)])  28.9 us
    pallas_call x4, Pallas kernels, rows_call(): pl.pallas_call(functools.partial(rows_kernel, n_tp, part), out_shape=outs...  28.1 us
    all_gather x1, blocking collectives, scales(): every = lax.all_gather(own, 'ep', axis=0)  27.5 us
    pallas_call x1, Pallas kernels, grads_call(): pl.pallas_call(functools.partial(grads_kernel, n_tp, chunks), out_shape=[...  16.5 us
    unnamed x36, local copies, waits for them, and re-layouts  9.3 us
    another operation x7, other arithmetic, body(): a[c] = jnp.stack([held(name, 2) for name in names])  6.34 us
  transfers between devices with their start and end apart: 31, of which 14 were waited for; matrix products, arithmetic and copies ran while one was open for 4% of the time, Pallas kernels for 24%

profile of v1, /device:TPU:0, one launch (start us, length us, event | category | flops | bytes accessed | tf_op | source)
XLA Modules:
  0.0 186.4 jit_solution(11738733427935590337)
XLA Ops:
  1.7 3.0 %collective-permute-start.1 = (bf16[2,128,1024]{2,1,0:T(8,128)(2,1)S(1)}, bf16[2,128,1024]{2,1,0:T(8,128)(2,1)S(1)}, u32[]{:S(2)}, u32[]{:S(2)}) collective-permute-start(bf16[2,128,1024]{2,1,0:T(8,128)(2,1)S(1)} %get-tuple-element.81), channel_id=1, source_target_pairs={{0,4},{4,0},{8,12},{12,8},{16,20},{20,16},{24,28},{28,24},{1,5},{5... | collective-permute-start | bytes 1572872 | tf_op jit(solution)/shard_map/ppermute | solution.py:18
  7.8 8.8 %collective-permute-done.1 = bf16[2,128,1024]{2,1,0:T(8,128)(2,1)S(1)} collective-permute-done((bf16[2,128,1024]{2,1,0:T(8,128)(2,1)S(1)}, bf16[2,128,1024]{2,1,0:T(8,128)(2,1)S(1)}, u32[]{:S(2)}, u32[]{:S(2)}) %collective-permute-start.1) | collective-permute-done | bytes 524320 | tf_op jit(solution)/shard_map/ppermute | solution.py:18
  16.7 1.8 collective-permute-start.3
  20.1 2.6 %collective-permute-start.5 = (bf16[2,128,1024]{2,1,0:T(8,128)(2,1)S(1)}, bf16[2,128,1024]{2,1,0:T(8,128)(2,1)S(1)}, u32[]{:S(2)}, u32[]{:S(2)}) collective-permute-start(bf16[2,128,1024]{2,1,0:T(8,128)(2,1)S(1)} %get-tuple-element.81), channel_id=1, source_target_pairs={{0,16},{4,20},{8,24},{12,28},{16,0},{20,4},{24,8},{28,12},{1,17},{... | collective-permute-start | bytes 1572872 | tf_op jit(solution)/shard_map/ppermute | solution.py:18
  24.7 2.8 %collective-permute-done.2 = bf16[128,1024]{1,0:T(8,128)(2,1)S(1)} collective-permute-done((bf16[128,1024]{1,0:T(8,128)(2,1)S(1)}, bf16[128,1024]{1,0:T(8,128)(2,1)S(1)}, u32[]{:S(2)}, u32[]{:S(2)}) %collective-permute-start.2) | collective-permute-done | bytes 262176 | tf_op jit(solution)/shard_map/ppermute | solution.py:18
  27.6 1.6 collective-permute-start.15
  29.3 15.3 %collective-permute-done.5 = bf16[2,128,1024]{2,1,0:T(8,128)(2,1)S(1)} collective-permute-done((bf16[2,128,1024]{2,1,0:T(8,128)(2,1)S(1)}, bf16[2,128,1024]{2,1,0:T(8,128)(2,1)S(1)}, u32[]{:S(2)}, u32[]{:S(2)}) %collective-permute-start.5) | collective-permute-done | bytes 524320 | tf_op jit(solution)/shard_map/ppermute | solution.py:18
  45.1 2.2 %collective-permute-done.15 = bf16[2,128,1024]{2,1,0:T(8,128)(2,1)S(1)} collective-permute-done((bf16[2,128,1024]{2,1,0:T(8,128)(2,1)S(1)}, bf16[2,128,1024]{2,1,0:T(8,128)(2,1)S(1)}, u32[]{:S(2)}, u32[]{:S(2)}) %collective-permute-start.15) | collective-permute-done | bytes 524320 | tf_op jit(solution)/shard_map/ppermute | solution.py:18
  48.8 1.6 pad_maximum_fusion.a_ref.refs_8_
  50.6 6.7 %collective-permute-done.7 = bf16[2,128,1024]{2,1,0:T(8,128)(2,1)S(1)} collective-permute-done((bf16[2,128,1024]{2,1,0:T(8,128)(2,1)S(1)}, bf16[2,128,1024]{2,1,0:T(8,128)(2,1)S(1)}, u32[]{:S(2)}, u32[]{:S(2)}) %collective-permute-start.7) | collective-permute-done | bytes 524320 | tf_op jit(solution)/shard_map/ppermute | solution.py:18
  57.9 4.6 %collective-permute-done.6 = bf16[2,128,1024]{2,1,0:T(8,128)(2,1)S(1)} collective-permute-done((bf16[2,128,1024]{2,1,0:T(8,128)(2,1)S(1)}, bf16[2,128,1024]{2,1,0:T(8,128)(2,1)S(1)}, u32[]{:S(2)}, u32[]{:S(2)}) %collective-permute-start.6) | collective-permute-done | bytes 524320 | tf_op jit(solution)/shard_map/ppermute | solution.py:18
  64.6 3.0 %collective-permute-done.12 = bf16[128,1024]{1,0:T(8,128)(2,1)S(1)} collective-permute-done((bf16[128,1024]{1,0:T(8,128)(2,1)S(1)}, bf16[128,1024]{1,0:T(8,128)(2,1)S(1)}, u32[]{:S(2)}, u32[]{:S(2)}) %collective-permute-start.12) | collective-permute-done | bytes 262176 | tf_op jit(solution)/shard_map/ppermute | solution.py:18
  68.7 3.1 %collective-permute-done.10 = bf16[128,1024]{1,0:T(8,128)(2,1)S(1)} collective-permute-done((bf16[128,1024]{1,0:T(8,128)(2,1)S(1)}, bf16[128,1024]{1,0:T(8,128)(2,1)S(1)}, u32[]{:S(2)}, u32[]{:S(2)}) %collective-permute-start.10) | collective-permute-done | bytes 262176 | tf_op jit(solution)/shard_map/ppermute | solution.py:18
  72.0 9.3 %collective-permute-done.19 = bf16[2,128,1024]{2,1,0:T(8,128)(2,1)S(1)} collective-permute-done((bf16[2,128,1024]{2,1,0:T(8,128)(2,1)S(1)}, bf16[2,128,1024]{2,1,0:T(8,128)(2,1)S(1)}, u32[]{:S(2)}, u32[]{:S(2)}) %collective-permute-start.19) | collective-permute-done | bytes 524320 | tf_op jit(solution)/shard_map/ppermute | solution.py:18
  85.3 27.5 %all-gather.1 = f32[8,4,128]{2,1,0:T(4,128)S(1)} all-gather(f32[1,4,128]{2,1,0:T(4,128)S(1)} %bitcast.121), channel_id=2, replica_groups=mesh['ep'=8,'tp'=4] {'ep'}, dimensions={0}, use_global_device_ids=true | all-gather | bytes 18432 | tf_op jit(solution)/shard_map/all_gather | solution.py:267
  112.8 1.6 pad_maximum_fusion.1.a_ref.refs_10_
  115.5 1.6 copy-done.4
  118.6 7.9 %rows.5 = (bf16[768,256]{1,0:T(8,128)(2,1)S(1)}, bf16[384,256]{1,0:T(8,128)(2,1)S(1)}, bf16[2,4,128,1024]{3,2,1,0:T(8,128)(2,1)S(1)}) custom-call(s32[1]{0:T(128)} %bitcast.t_ref, f32[1,256]{1,0:T(1,128)S(1)} %bitcast.101, bf16[4,2,128,1024]{3,2,1,0:T(8,128)(2,1)S(1)} %copy-done.4, bf16[4,2,128,1024]{3,2,1,0:T(8,128)(2,1)S(1)} %copy-done.9, ...), custom_call_target="tpu_custom_call" | custom-call | flops 4026531840 | bytes 13631488 | tf_op jit(solution)/shard_map/rows/pallas_call | solution.py:141
  127.9 8.3 %rows.4 = (bf16[768,256]{1,0:T(8,128)(2,1)S(1)}, bf16[384,256]{1,0:T(8,128)(2,1)S(1)}, bf16[2,4,128,1024]{3,2,1,0:T(8,128)(2,1)S(1)}) custom-call(s32[1]{0:T(128)} %bitcast.t_ref, f32[1,256]{1,0:T(1,128)S(1)} %bitcast.100, bf16[4,2,128,1024]{3,2,1,0:T(8,128)(2,1)} %pad_maximum_fusion.a_ref.refs_8_, ...), custom_call_target="tpu_custom_call" | custom-call | flops 4026531840 | bytes 13631488 | tf_op jit(solution)/shard_map/rows/pallas_call | solution.py:141
  139.3 5.9 %rows.6 = (bf16[768,256]{1,0:T(8,128)(2,1)S(1)}, bf16[384,256]{1,0:T(8,128)(2,1)S(1)}) custom-call(s32[1]{0:T(128)} %bitcast.t_ref, f32[1,256]{1,0:T(1,128)S(1)} %bitcast.99, bf16[4,2,128,1024]{3,2,1,0:T(8,128)(2,1)} %pad_maximum_fusion.1.a_ref.refs_10_, bf16[4,2,128,1024]{3,2,1,0:T(8,128)(2,1)S(1)} %copy-done.7, bf16[768,4096]{1,0:T(8,128)(2,1)S(1)} %bitcast.92, ...), custom_call_target="tpu_custom_call" | custom-call | flops 2415919104 | bytes 13631488 | tf_op jit(solution)/shard_map/rows/pallas_call | solution.py:141
  145.2 6.0 %rows.7 = (bf16[768,256]{1,0:T(8,128)(2,1)S(1)}, bf16[384,256]{1,0:T(8,128)(2,1)S(1)}) custom-call(s32[1]{0:T(128)} %bitcast.t_ref, f32[1,256]{1,0:T(1,128)S(1)} %bitcast.98, bf16[4,2,128,1024]{3,2,1,0:T(8,128)(2,1)} %pad_maximum_fusion.3.a_ref.refs_11_, bf16[4,2,128,1024]{3,2,1,0:T(8,128)(2,1)} %collective-permute-done.21.b_ref.refs_15_, ...), custom_call_target="tpu_custom_call" | custom-call | flops 2415919104 | bytes 13631488 | tf_op jit(solution)/shard_map/rows/pallas_call | solution.py:141
  154.8 5.7 %collective-permute-done.26 = bf16[128,1024]{1,0:T(8,128)(2,1)S(1)} collective-permute-done((bf16[128,1024]{1,0:T(8,128)(2,1)S(1)}, bf16[128,1024]{1,0:T(8,128)(2,1)S(1)}, u32[]{:S(2)}, u32[]{:S(2)}) %collective-permute-start.26) | collective-permute-done | bytes 262176 | tf_op jit(solution)/shard_map/ppermute | solution.py:18
  164.1 1.6 collective-permute-done.27
  168.9 16.5 %grads.1 = (bf16[768,4096]{1,0:T(8,128)(2,1)}, bf16[384,4096]{1,0:T(8,128)(2,1)}) custom-call(s32[1]{0:T(128)} %bitcast.t_ref, bf16[768,256]{1,0:T(8,128)(2,1)S(1)} %get-tuple-element.61.refs_0_, bf16[768,256]{1,0:T(8,128)(2,1)S(1)} %get-tuple-element.62.refs_1_, bf16[768,256]{1,0:T(8,128)(2,1)S(1)} %get-tuple-element.63.refs_2_, ...), custom_call_target="tpu_custom_call" | custom-call | flops 9663676416 | bytes 26214400 | tf_op jit(solution)/shard_map/grads/pallas_call | solution.py:234
  (115 shorter events, 36.1 us)
Async XLA Ops:
  1.7 14.9 %collective-permute-start.1 = (bf16[2,128,1024]{2,1,0:T(8,128)(2,1)S(1)}, bf16[2,128,1024]{2,1,0:T(8,128)(2,1)S(1)}, u32[]{:S(2)}, u32[]{:S(2)}) collective-permute-start(bf16[2,128,1024]{2,1,0:T(8,128)(2,1)S(1)} %get-tuple-element.81), channel_id=1, source_target_pairs={{0,4},{4,0},{8,12},{12,8},{16,20},{20,16},{24,28},{28,24},{1,5},{5... | collective-permute-start | bytes 1572872 | tf_op jit(solution)/shard_map/ppermute | solution.py:18
  4.7 13.8 %collective-permute-start = (bf16[2,128,1024]{2,1,0:T(8,128)(2,1)S(1)}, bf16[2,128,1024]{2,1,0:T(8,128)(2,1)S(1)}, u32[]{:S(2)}, u32[]{:S(2)}) collective-permute-start(bf16[2,128,1024]{2,1,0:T(8,128)(2,1)S(1)} %get-tuple-element.81), channel_id=1, source_target_pairs={{0,2},{1,3},{2,0},{3,1},{4,6},{5,7},{6,4},{7,5},{8,10},{9,11},{10,... | collective-permute-start | bytes 1572872 | tf_op jit(solution)/shard_map/ppermute | solution.py:18
  6.3 16.4 %collective-permute-start.8 = (bf16[2,128,1024]{2,1,0:T(8,128)(2,1)S(1)}, bf16[2,128,1024]{2,1,0:T(8,128)(2,1)S(1)}, u32[]{:S(2)}, u32[]{:S(2)}) collective-permute-start(bf16[2,128,1024]{2,1,0:T(8,128)(2,1)S(1)} %get-tuple-element.81), channel_id=1, source_target_pairs={{0,8},{4,12},{8,0},{12,4},{16,24},{20,28},{24,16},{28,20},{1,9},{5... | collective-permute-start | bytes 1572872 | tf_op jit(solution)/shard_map/ppermute | solution.py:18
  20.1 24.5 %collective-permute-start.5 = (bf16[2,128,1024]{2,1,0:T(8,128)(2,1)S(1)}, bf16[2,128,1024]{2,1,0:T(8,128)(2,1)S(1)}, u32[]{:S(2)}, u32[]{:S(2)}) collective-permute-start(bf16[2,128,1024]{2,1,0:T(8,128)(2,1)S(1)} %get-tuple-element.81), channel_id=1, source_target_pairs={{0,16},{4,20},{8,24},{12,28},{16,0},{20,4},{24,8},{28,12},{1,17},{... | collective-permute-start | bytes 1572872 | tf_op jit(solution)/shard_map/ppermute | solution.py:18
  22.7 22.4 %collective-permute-start.9 = (bf16[2,128,1024]{2,1,0:T(8,128)(2,1)S(1)}, bf16[2,128,1024]{2,1,0:T(8,128)(2,1)S(1)}, u32[]{:S(2)}, u32[]{:S(2)}) collective-permute-start(bf16[2,128,1024]{2,1,0:T(8,128)(2,1)S(1)} %collective-permute-done.8), channel_id=1, source_target_pairs={{0,4},{4,0},{8,12},{12,8},{16,20},{20,16},{24,28},{28,24},{1,5},{5... | collective-permute-start | bytes 1572872 | tf_op jit(solution)/shard_map/ppermute | solution.py:18
  23.2 21.9 %collective-permute-start.11 = (bf16[2,128,1024]{2,1,0:T(8,128)(2,1)S(1)}, bf16[2,128,1024]{2,1,0:T(8,128)(2,1)S(1)}, u32[]{:S(2)}, u32[]{:S(2)}) collective-permute-start(bf16[2,128,1024]{2,1,0:T(8,128)(2,1)S(1)} %collective-permute-done.8), channel_id=1, source_target_pairs={{0,2},{1,3},{2,0},{3,1},{4,6},{5,7},{6,4},{7,5},{8,10},{9,11},{10,... | collective-permute-start | bytes 1572872 | tf_op jit(solution)/shard_map/ppermute | solution.py:18
  27.6 19.7 %collective-permute-start.15 = (bf16[2,128,1024]{2,1,0:T(8,128)(2,1)S(1)}, bf16[2,128,1024]{2,1,0:T(8,128)(2,1)S(1)}, u32[]{:S(2)}, u32[]{:S(2)}) collective-permute-start(bf16[2,128,1024]{2,1,0:T(8,128)(2,1)S(1)} %get-tuple-element.83), channel_id=1, source_target_pairs={{0,8},{4,12},{8,0},{12,4},{16,24},{20,28},{24,16},{28,20},{1,9},{5... | collective-permute-start | bytes 1572872 | tf_op jit(solution)/shard_map/ppermute | solution.py:18
  44.6 12.7 %collective-permute-start.7 = (bf16[2,128,1024]{2,1,0:T(8,128)(2,1)S(1)}, bf16[2,128,1024]{2,1,0:T(8,128)(2,1)S(1)}, u32[]{:S(2)}, u32[]{:S(2)}) collective-permute-start(bf16[2,128,1024]{2,1,0:T(8,128)(2,1)S(1)} %collective-permute-done.5), channel_id=1, source_target_pairs={{0,4},{4,0},{8,12},{12,8},{16,20},{20,16},{24,28},{28,24},{1,5},{5... | collective-permute-start | bytes 1572872 | tf_op jit(solution)/shard_map/ppermute | solution.py:18
  47.6 36.2 %collective-permute-start.16 = (bf16[4,2,128,1024]{3,2,1,0:T(8,128)(2,1)S(1)}, bf16[4,2,128,1024]{3,2,1,0:T(8,128)(2,1)S(1)}, u32[]{:S(2)}, u32[]{:S(2)}) collective-permute-start(bf16[4,2,128,1024]{3,2,1,0:T(8,128)(2,1)S(1)} %pad_maximum_fusion.2.a_ref.refs_9_), channel_id=1, source_target_pairs={{0,1},{1,0},{2,3},{3,2},{4,5},{5,4},{6,7},{7,6},{8,9},{9,8},{10,11... | collective-permute-start | bytes 6291464 | tf_op jit(solution)/shard_map/ppermute | solution.py:18
  47.7 14.8 %collective-permute-start.6 = (bf16[2,128,1024]{2,1,0:T(8,128)(2,1)S(1)}, bf16[2,128,1024]{2,1,0:T(8,128)(2,1)S(1)}, u32[]{:S(2)}, u32[]{:S(2)}) collective-permute-start(bf16[2,128,1024]{2,1,0:T(8,128)(2,1)S(1)} %collective-permute-done.5), channel_id=1, source_target_pairs={{0,2},{1,3},{2,0},{3,1},{4,6},{5,7},{6,4},{7,5},{8,10},{9,11},{10,... | collective-permute-start | bytes 1572872 | tf_op jit(solution)/shard_map/ppermute | solution.py:18
  48.8 15.3 %collective-permute-start.17 = (bf16[2,128,1024]{2,1,0:T(8,128)(2,1)S(1)}, bf16[2,128,1024]{2,1,0:T(8,128)(2,1)S(1)}, u32[]{:S(2)}, u32[]{:S(2)}) collective-permute-start(bf16[2,128,1024]{2,1,0:T(8,128)(2,1)S(1)} %collective-permute-done.5), channel_id=1, source_target_pairs={{0,8},{4,12},{8,0},{12,4},{16,24},{20,28},{24,16},{28,20},{1,9},{5... | collective-permute-start | bytes 1572872 | tf_op jit(solution)/shard_map/ppermute | solution.py:18
  50.4 64.0 %collective-permute-start.4 = (bf16[4,2,128,1024]{3,2,1,0:T(8,128)(2,1)}, bf16[4,2,128,1024]{3,2,1,0:T(8,128)(2,1)}, u32[]{:S(2)}, u32[]{:S(2)}) collective-permute-start(bf16[4,2,128,1024]{3,2,1,0:T(8,128)(2,1)} %pad_maximum_fusion.a_ref.refs_8_), channel_id=1, source_target_pairs={{0,1},{1,0},{2,3},{3,2},{4,5},{5,4},{6,7},{7,6},{8,9},{9,8},{10,11... | collective-permute-start | bytes 6291464 | tf_op jit(solution)/shard_map/ppermute | solution.py:18
  57.3 10.4 %collective-permute-start.12 = (bf16[128,1024]{1,0:T(8,128)(2,1)S(1)}, bf16[128,1024]{1,0:T(8,128)(2,1)S(1)}, u32[]{:S(2)}, u32[]{:S(2)}) collective-permute-start(bf16[128,1024]{1,0:T(8,128)(2,1)S(1)} %slice_bitcast_fusion.8), channel_id=1, source_target_pairs={{0,2},{1,3},{2,0},{3,1},{4,6},{5,7},{6,4},{7,5},{8,10},{9,11},{10,... | collective-permute-start | bytes 786440 | tf_op jit(solution)/shard_map/ppermute | solution.py:18
  64.1 17.2 %collective-permute-start.19 = (bf16[2,128,1024]{2,1,0:T(8,128)(2,1)S(1)}, bf16[2,128,1024]{2,1,0:T(8,128)(2,1)S(1)}, u32[]{:S(2)}, u32[]{:S(2)}) collective-permute-start(bf16[2,128,1024]{2,1,0:T(8,128)(2,1)S(1)} %collective-permute-done.17), channel_id=1, source_target_pairs={{0,4},{4,0},{8,12},{12,8},{16,20},{20,16},{24,28},{28,24},{1,5},{5... | collective-permute-start | bytes 1572872 | tf_op jit(solution)/shard_map/ppermute | solution.py:18
  67.7 13.6 %collective-permute-start.18 = (bf16[2,128,1024]{2,1,0:T(8,128)(2,1)S(1)}, bf16[2,128,1024]{2,1,0:T(8,128)(2,1)S(1)}, u32[]{:S(2)}, u32[]{:S(2)}) collective-permute-start(bf16[2,128,1024]{2,1,0:T(8,128)(2,1)S(1)} %collective-permute-done.17), channel_id=1, source_target_pairs={{0,2},{1,3},{2,0},{3,1},{4,6},{5,7},{6,4},{7,5},{8,10},{9,11},{10,... | collective-permute-start | bytes 1572872 | tf_op jit(solution)/shard_map/ppermute | solution.py:18
  71.9 10.4 %collective-permute-start.20 = (bf16[2,128,1024]{2,1,0:T(8,128)(2,1)S(1)}, bf16[2,128,1024]{2,1,0:T(8,128)(2,1)S(1)}, u32[]{:S(2)}, u32[]{:S(2)}) collective-permute-start(bf16[2,128,1024]{2,1,0:T(8,128)(2,1)S(1)} %get-tuple-element.50), channel_id=1, source_target_pairs={{0,8},{4,12},{8,0},{12,4},{16,24},{20,28},{24,16},{28,20},{1,9},{5... | collective-permute-start | bytes 1572872 | tf_op jit(solution)/shard_map/ppermute | solution.py:18
  85.2 41.5 %collective-permute-start.21 = (bf16[4,2,128,1024]{3,2,1,0:T(8,128)(2,1)}, bf16[4,2,128,1024]{3,2,1,0:T(8,128)(2,1)}, u32[]{:S(2)}, u32[]{:S(2)}) collective-permute-start(bf16[4,2,128,1024]{3,2,1,0:T(8,128)(2,1)} %pad_maximum_fusion.3.a_ref.refs_11_), channel_id=1, source_target_pairs={{0,1},{1,0},{2,3},{3,2},{4,5},{5,4},{6,7},{7,6},{8,9},{9,8},{10,11... | collective-permute-start | bytes 6291464 | tf_op jit(solution)/shard_map/ppermute | solution.py:18
  114.5 21.9 %collective-permute-start.13 = (bf16[4,2,128,1024]{3,2,1,0:T(8,128)(2,1)}, bf16[4,2,128,1024]{3,2,1,0:T(8,128)(2,1)S(1)}, u32[]{:S(2)}, u32[]{:S(2)}) collective-permute-start(bf16[4,2,128,1024]{3,2,1,0:T(8,128)(2,1)} %pad_maximum_fusion.1.a_ref.refs_10_), channel_id=1, source_target_pairs={{0,1},{1,0},{2,3},{3,2},{4,5},{5,4},{6,7},{7,6},{8,9},{9,8},{10,11... | collective-permute-start | bytes 6291464 | tf_op jit(solution)/shard_map/ppermute | solution.py:18
  126.7 24.5 %collective-permute-start.22 = (bf16[4,128,1024]{2,1,0:T(8,128)(2,1)S(1)}, bf16[4,128,1024]{2,1,0:T(8,128)(2,1)S(1)}, u32[]{:S(2)}, u32[]{:S(2)}) collective-permute-start(bf16[4,128,1024]{2,1,0:T(8,128)(2,1)S(1)} %slice_bitcast_fusion), channel_id=1, source_target_pairs={{0,1},{1,0},{2,3},{3,2},{4,5},{5,4},{6,7},{7,6},{8,9},{9,8},{10,11... | collective-permute-start | bytes 3145736 | tf_op jit(solution)/shard_map/ppermute | solution.py:18
  137.7 14.3 %collective-permute-start.14 = (bf16[4,128,1024]{2,1,0:T(8,128)(2,1)S(1)}, bf16[4,128,1024]{2,1,0:T(8,128)(2,1)S(1)}, u32[]{:S(2)}, u32[]{:S(2)}) collective-permute-start(bf16[4,128,1024]{2,1,0:T(8,128)(2,1)S(1)} %slice_bitcast_fusion.1), channel_id=1, source_target_pairs={{0,1},{1,0},{2,3},{3,2},{4,5},{5,4},{6,7},{7,6},{8,9},{9,8},{10,11... | collective-permute-start | bytes 3145736 | tf_op jit(solution)/shard_map/ppermute | solution.py:18
  152.4 10.5 %collective-permute-start.24 = (bf16[128,1024]{1,0:T(8,128)(2,1)S(1)}, bf16[128,1024]{1,0:T(8,128)(2,1)S(1)}, u32[]{:S(2)}, u32[]{:S(2)}) collective-permute-start(bf16[128,1024]{1,0:T(8,128)(2,1)S(1)} %get-tuple-element.54), channel_id=1, source_target_pairs={{0,4},{4,0},{8,12},{12,8},{16,20},{20,16},{24,28},{28,24},{1,5},{5... | collective-permute-start | bytes 786440 | tf_op jit(solution)/shard_map/ppermute | solution.py:18
  163.0 22.4 %collective-permute-start.25 = (bf16[128,1024]{1,0:T(8,128)(2,1)S(1)}, bf16[128,1024]{1,0:T(8,128)(2,1)S(1)}, u32[]{:S(2)}, u32[]{:S(2)}) collective-permute-start(bf16[128,1024]{1,0:T(8,128)(2,1)S(1)} %add_convert_fusion.2), channel_id=1, source_target_pairs={{0,8},{4,12},{8,0},{12,4},{16,24},{20,28},{24,16},{28,20},{1,9},{5... | collective-permute-start | bytes 786440 | tf_op jit(solution)/shard_map/ppermute | solution.py:18
  167.2 18.3 %collective-permute-start.30 = (bf16[128,1024]{1,0:T(8,128)(2,1)S(1)}, bf16[128,1024]{1,0:T(8,128)(2,1)S(1)}, u32[]{:S(2)}, u32[]{:S(2)}) collective-permute-start(bf16[128,1024]{1,0:T(8,128)(2,1)S(1)} %pad_maximum_fusion.8), channel_id=1, source_target_pairs={{0,4},{4,0},{8,12},{12,8},{16,20},{20,16},{24,28},{28,24},{1,5},{5... | collective-permute-start | bytes 786440 | tf_op jit(solution)/shard_map/ppermute | solution.py:18
  167.8 17.7 %collective-permute-start.28 = (bf16[128,1024]{1,0:T(8,128)(2,1)S(1)}, bf16[128,1024]{1,0:T(8,128)(2,1)S(1)}, u32[]{:S(2)}, u32[]{:S(2)}) collective-permute-start(bf16[128,1024]{1,0:T(8,128)(2,1)S(1)} %pad_maximum_fusion.7), channel_id=1, source_target_pairs={{0,2},{1,3},{2,0},{3,1},{4,6},{5,7},{6,4},{7,5},{8,10},{9,11},{10,... | collective-permute-start | bytes 786440 | tf_op jit(solution)/shard_map/ppermute | solution.py:18
  (25 other events, 155.8 us)

commit v2 on v1

v2 whole, which is shorter than its diff:
```python
import functools

import jax
import jax.numpy as jnp
from jax import lax
from jax.experimental import pallas as pl
from jax.experimental.pallas import tpu as pltpu
from jax.sharding import PartitionSpec as P

BF16 = jnp.bfloat16
F32 = jnp.float32
VMEM_LIMIT = 58 * 1024 * 1024
SLOTS = 3
SHRINK = 1.0 / 64.0


def hop(block, axis, bit):
    count = lax.axis_size(axis)
    return lax.ppermute(block, axis, [(i, i ^ bit) for i in range(count)])


def leap(block, ep, tp):
    wide, count = lax.axis_size("tp"), lax.axis_size("ep") * lax.axis_size("tp")
    apart = ep * wide + tp
    return lax.ppermute(block, ("ep", "tp"), [(i, i ^ apart) for i in range(count)])


def after(value, *others):
    return lax.optimization_barrier((value,) + others)[0] if others else value


def bits_of(number, letter, skip=0):
    return [f"{letter}{i}" for i in range(skip, number.bit_length() - 1)]


class Lanes:
    def __init__(self, depth):
        self.depth = depth
        self.sent = {}

    def send(self, block, bit, *others):
        queue = self.sent.setdefault(bit, [])
        ready = list(others)
        if bit != "t0":
            ready += queue[-self.depth : len(queue) - self.depth + 1]
        axis = "ep" if bit[0] == "e" else "tp"
        queue.append(hop(after(block, *ready), axis, 1 << int(bit[1:])))
        return queue[-1]


def gather_plan(n_ep, n_tp):
    if (n_ep, n_tp) == (8, 4):
        x, n, f, y = "e0", "e1", "e2", "t1"
        near = (x, n), (y, n), (x, y, n)
        far = (x, f), (y, f), (n, f)
        return [
            ((x,), x, 2), ((y,), y, 2), ((n,), n, 2), ((f,), f, 2),
            ((x, y), x, 0), ((x, y), y, 1),
            ((x, n), x, 2, (f,)), ((y, n), y, 2, (f,)), ((x, y, n), n, 2, (f,)),
            ((x, f), x, 2, *near), ((y, f), y, 2, *near), ((n, f), n, 2, *near),
            ((x, y, f), x, 2, *far, 0), ((y, n, f), y, 2, *far, 0), ((x, n, f), n, 2, *far, 0),
            ((x, y, n, f), x, 0, 1), ((x, y, n, f), y, 1, 1),
        ]
    bits = bits_of(n_ep, "e") + bits_of(n_tp, "t", 1)
    plan = []
    for i, bit in enumerate(bits):
        for low in range(1 << i):
            below = tuple(b for j, b in enumerate(bits[:i]) if low >> j & 1)
            plan.append((below + (bit,), bit, 2))
    return plan


def name_of(ep, tp):
    names = [f"e{i}" for i in range(ep.bit_length()) if ep >> i & 1]
    names += [f"t{i + 1}" for i in range(tp.bit_length()) if tp >> i & 1]
    return frozenset(names)


def rows_of(refs, tok):
    if len(refs) == 1:
        return refs[0].at[0:tok], refs[0].at[tok : 2 * tok], refs[0].at[2 * tok : 2 * tok + 16]
    return refs[0], refs[1].at[0:tok], refs[1].at[tok : tok + 16]


def weights_row(ref, expert, tok):
    width = ref.shape[1]
    per = width // tok
    table = ref[...].astype(F32)
    lines = lax.broadcasted_iota(jnp.int32, table.shape, 0)
    lanes = lax.broadcasted_iota(jnp.int32, table.shape, 1)
    table = jnp.where((lines == expert // per) & (lanes // tok == expert % per), table, 0.0)
    line = jnp.sum(table, axis=0, keepdims=True)
    return functools.reduce(jnp.add, [line[:, i * tok : (i + 1) * tok] for i in range(per)])


def rows_kernel(n_tp, sizes, part, where_ref, win_ref, wout_ref, *refs):
    blocks = len(sizes) // n_tp
    pieces = [[] for _ in range(blocks)]
    for k, size in enumerate(sizes):
        pieces[k // n_tp].append(refs[:size])
        refs = refs[size:]
    if part:
        dadb_ref, hid_ref, part_ref, *refs = refs
    else:
        dadb_ref, hid_ref, *refs = refs
    xs, gs, ps, wi, wo, acc, sems, psems, wsems = refs
    ffl = hid_ref.shape[0]
    tok = hid_ref.shape[1] // blocks
    width = wout_ref.shape[1] // n_tp

    def column(d):
        return pl.ds(pl.multiple_of((where_ref[0] ^ d) * width, width), width)

    copies = []
    for d in range(n_tp):
        mine = []
        for j in range(blocks):
            x, g, _ = rows_of(pieces[j][d], tok)
            into = pl.ds(j * tok, tok)
            mine.append(pltpu.make_async_copy(x, xs.at[d, into], sems.at[d, j, 0]))
            mine.append(pltpu.make_async_copy(g, gs.at[d, into], sems.at[d, j, 1]))
        mine.append(pltpu.make_async_copy(win_ref.at[:, column(d)], wi.at[d], wsems.at[d, 0]))
        mine.append(pltpu.make_async_copy(wout_ref.at[:, column(d)], wo.at[d], wsems.at[d, 1]))
        copies.append(mine)
    tables = []
    for j in range(blocks):
        table = rows_of(pieces[j][0], tok)[2]
        tables.append(pltpu.make_async_copy(table, ps.at[j], psems.at[j]))
        tables[j].start()

    for copy in copies[0] + copies[1]:
        copy.start()
    last = (((1,), (1,)), ((), ()))
    for d in range(n_tp):
        for copy in copies[d]:
            copy.wait()
        for copy in copies[d + 2] if d + 2 < n_tp else ():
            copy.start()
        x = xs[d]
        g = gs[d] * jnp.asarray(SHRINK, BF16)
        ab = lax.dot_general(wi[d], x, last, preferred_element_type=F32)
        h = lax.dot_general(wo[d], g, last, preferred_element_type=F32)
        if d == 0:
            acc[pl.ds(0, 2 * ffl)] = ab
            acc[pl.ds(2 * ffl, ffl)] = h
        else:
            acc[pl.ds(0, 2 * ffl)] += ab
            acc[pl.ds(2 * ffl, ffl)] += h
    scale = []
    for j in range(blocks):
        tables[j].wait()
        first = weights_row(ps.at[j], where_ref[1], tok)
        scale.append(first + weights_row(ps.at[j], where_ref[2], tok))
    scale = jnp.concatenate(scale, axis=1)
    a = acc[pl.ds(0, ffl)]
    b = acc[pl.ds(ffl, ffl)]
    named = scale > 0.0
    dh = acc[pl.ds(2 * ffl, ffl)] * (scale * (1.0 / SHRINK))
    sig = jax.nn.sigmoid(a)
    silu = a * sig
    da = dh * b * sig * (1.0 + a * (1.0 - sig))
    dadb_ref[pl.ds(0, ffl)] = jnp.where(named, da, 0.0).astype(BF16)
    dadb_ref[pl.ds(ffl, ffl)] = jnp.where(named, dh * silu, 0.0).astype(BF16)
    hid_ref[...] = jnp.where(named, (0.5 * scale) * (silu * b), 0.0).astype(BF16)
    if part:
        lhs = dadb_ref[...].T
        for d in range(n_tp):
            out = jnp.dot(lhs, wi[d], preferred_element_type=F32).astype(BF16)
            for j in range(blocks):
                part_ref[d % 2, j * (n_tp // 2) + d // 2] = out[j * tok : (j + 1) * tok]


def rows_call(part, where, pieces, w_in, w_out, tok):
    n_tp = len(pieces[0])
    flat = [piece for block in pieces for piece in block]
    sizes = [len(piece) for piece in flat]
    arrays = [array for piece in flat for array in piece]
    blocks = len(pieces)
    rows, width = blocks * tok, arrays[0].shape[1]
    ffl = w_out.shape[0]
    outs = [
        jax.ShapeDtypeStruct((2 * ffl, rows), BF16),
        jax.ShapeDtypeStruct((ffl, rows), BF16),
    ]
    if part:
        outs.append(jax.ShapeDtypeStruct((2, blocks * n_tp // 2, tok, width), BF16))
    vmem = pl.BlockSpec(memory_space=pltpu.VMEM)
    hbm = pl.BlockSpec(memory_space=pltpu.HBM)
    return pl.pallas_call(
        functools.partial(rows_kernel, n_tp, sizes, part),
        out_shape=outs,
        in_specs=[pl.BlockSpec(memory_space=pltpu.SMEM)] + [hbm] * (2 + len(arrays)),
        out_specs=[vmem] * len(outs),
        scratch_shapes=[
            pltpu.VMEM((n_tp, rows, width), BF16),
            pltpu.VMEM((n_tp, rows, width), BF16),
            pltpu.VMEM((blocks, 16, width), BF16),
            pltpu.VMEM((n_tp, 2 * ffl, width), BF16),
            pltpu.VMEM((n_tp, ffl, width), BF16),
            pltpu.VMEM((3 * ffl, rows), F32),
            pltpu.SemaphoreType.DMA((n_tp, blocks, 2)),
            pltpu.SemaphoreType.DMA((blocks,)),
            pltpu.SemaphoreType.DMA((n_tp, 2)),
        ],
        compiler_params=pltpu.CompilerParams(vmem_limit_bytes=VMEM_LIMIT),
        cost_estimate=pl.CostEstimate(
            flops=2 * rows * ffl * n_tp * width * (5 if part else 3),
            bytes_accessed=2 * (3 * ffl + 2 * rows) * n_tp * width,
            transcendentals=rows * ffl,
        ),
        name="rows",
    )(where, w_in, w_out, *arrays)


def grads_kernel(steps, sizes, added, filled, where_ref, dadb_ref, hid_ref, *refs):
    pieces = []
    tok = hid_ref.shape[1] * len(steps) // len(sizes)
    for size in sizes:
        pieces.append(rows_of(refs[:size], tok))
        refs = refs[size:]
    base, refs = (refs[:2], refs[2:]) if added else ((), refs)
    gin_ref, gout_ref, xs, gs, oi, oo, bi, bo, sems, bsems, osems = refs[2 if filled else 0 :]
    width = pieces[0][0].shape[1]
    slots, _, tile = xs.shape
    tiles = width // tile
    total = len(steps) * tiles

    def column(k):
        start = (where_ref[0] ^ steps[k // tiles]) * width + k % tiles * tile
        return pl.ds(pl.multiple_of(start, tile), tile)

    def fetch(k):
        slot, cols = k % slots, pl.ds(k % tiles * tile, tile)
        copies = []
        for i, (x, g, _) in enumerate(pieces[k // tiles :: len(steps)]):
            into = pl.ds(i * tok, tok)
            copies.append(pltpu.make_async_copy(x.at[:, cols], xs.at[slot, into], sems.at[slot, i, 0]))
            copies.append(pltpu.make_async_copy(g.at[:, cols], gs.at[slot, into], sems.at[slot, i, 1]))
        for i, (src, dst) in enumerate(zip(base, (bi, bo))):
            copies.append(pltpu.make_async_copy(src.at[:, column(k)], dst.at[slot], bsems.at[slot, i]))
        for copy in copies:
            copy.start()
        return copies

    coming = [fetch(k) for k in range(min(slots - 1, total))]
    leaving = {}
    for k in range(total):
        slot = k % slots
        if k + slots - 1 < total:
            coming.append(fetch(k + slots - 1))
        for copy in coming[k]:
            copy.wait()
        for copy in leaving.pop(k - slots, ()):
            copy.wait()
        gi = jnp.dot(dadb_ref[...], xs[slot], preferred_element_type=F32)
        go = 2.0 * jnp.dot(hid_ref[...], gs[slot], preferred_element_type=F32)
        if added:
            gi = gi + bi[slot].astype(F32)
            go = go + bo[slot].astype(F32)
        oi[slot] = gi.astype(BF16)
        oo[slot] = go.astype(BF16)
        leaving[k] = (
            pltpu.make_async_copy(oi.at[slot], gin_ref.at[:, column(k)], osems.at[slot, 0]),
            pltpu.make_async_copy(oo.at[slot], gout_ref.at[:, column(k)], osems.at[slot, 1]),
        )
        for copy in leaving[k]:
            copy.start()
    for copies in leaving.values():
        for copy in copies:
            copy.wait()


def grads_call(where, dadb, hid, pieces, steps, base=(), filled=()):
    n_tp = len(pieces[0])
    flat = [block[d] for block in pieces for d in steps]
    sizes = [len(piece) for piece in flat]
    arrays = [array for piece in flat for array in piece]
    width = arrays[0].shape[1]
    ffl, rows = hid.shape
    depth = n_tp * width
    tile = min(512, width)
    vmem = pl.BlockSpec(memory_space=pltpu.VMEM)
    hbm = pl.BlockSpec(memory_space=pltpu.HBM)
    operands = [where, dadb, hid, *arrays, *base, *filled]
    return pl.pallas_call(
        functools.partial(grads_kernel, steps, sizes, len(base) > 0, len(filled) > 0),
        out_shape=[
            jax.ShapeDtypeStruct((2 * ffl, depth), BF16),
            jax.ShapeDtypeStruct((ffl, depth), BF16),
        ],
        in_specs=[pl.BlockSpec(memory_space=pltpu.SMEM), vmem, vmem]
        + [hbm] * (len(operands) - 3),
        out_specs=[hbm, hbm],
        input_output_aliases={len(operands) - 2: 0, len(operands) - 1: 1} if filled else {},
        scratch_shapes=[
            pltpu.VMEM((SLOTS, rows, tile), BF16),
            pltpu.VMEM((SLOTS, rows, tile), BF16),
            pltpu.VMEM((SLOTS, 2 * ffl, tile), BF16),
            pltpu.VMEM((SLOTS, ffl, tile), BF16),
            pltpu.VMEM((SLOTS, 2 * ffl, tile), BF16),
            pltpu.VMEM((SLOTS, ffl, tile), BF16),
            pltpu.SemaphoreType.DMA((SLOTS, len(pieces), 2)),
            pltpu.SemaphoreType.DMA((SLOTS, 2)),
            pltpu.SemaphoreType.DMA((SLOTS, 2)),
        ],
        compiler_params=pltpu.CompilerParams(vmem_limit_bytes=VMEM_LIMIT),
        cost_estimate=pl.CostEstimate(
            flops=6 * rows * ffl * len(steps) * width,
            bytes_accessed=2 * (3 * ffl + 2 * rows) * len(steps) * width,
            transcendentals=0,
        ),
        name="grads",
    )(*operands)


def own_rows(tokens, out_grad, routes, probs, n_ep):
    tok, width = tokens.shape
    copies = jnp.arange(n_ep, dtype=jnp.int32)[:, None, None]
    table = jnp.sum(jnp.where(routes[None] == copies, probs[None], 0), axis=2).astype(BF16)
    table = table.reshape(n_ep * tok // width, width)
    table = jnp.pad(table, ((0, 16 - table.shape[0]), (0, 0)))
    return jnp.concatenate([tokens, out_grad, table])


def body(tokens, out_grad, routes, probs, w_in, w_out):
    n_ep, n_tp = lax.axis_size("ep"), lax.axis_size("tp")
    pairs = n_tp // 2
    ffl = w_out.shape[1]
    w_in = w_in.reshape(2 * ffl, w_in.shape[3])
    w_out = w_out[0]
    tok = tokens.shape[0]
    expert = lax.axis_index("ep") % (n_ep // 2)
    where = jnp.stack([lax.axis_index("tp"), expert, expert + n_ep // 2]).astype(jnp.int32)

    lanes = Lanes(1)
    have = {frozenset(): {2: own_rows(tokens, out_grad, routes, probs, n_ep)}}

    def held(name, part):
        parts = have[name]
        if part not in parts:
            if part == 2:
                parts[2] = jnp.concatenate([parts[0], parts[1]])
            else:
                parts[part] = parts[2][:tok] if part == 0 else parts[2][tok:]
        return parts[part]

    def arrays(name):
        parts = have[name]
        return (parts[2],) if 2 in parts else (parts[0], parts[1])

    names = [[name_of(e, y) for y in range(pairs)] for e in range(n_ep)]
    half_of = {name: 2 * e // n_ep for e in range(n_ep) for name in names[e]}
    missing = [n_ep * pairs - 2, n_ep * pairs]
    pieces = [None] * n_ep
    done = []
    terms = {}
    other = {frozenset(): (lanes.send(have[frozenset()][2], "t0"),)}
    for target, bit, part, *first in gather_plan(n_ep, n_tp):
        target = frozenset(target)
        before = []
        for what in first:
            before.append(done[what] if isinstance(what, int) else have[frozenset(what)][2])
        have.setdefault(target, {})[part] = lanes.send(held(target - {bit}, part), bit, *before)
        if 2 in have[target] or len(have[target]) == 2:
            other[target] = tuple(lanes.send(array, "t0") for array in arrays(target))
        half = half_of[target]
        missing[half] -= 2 if part == 2 else 1
        if missing[half]:
            continue
        blocks = range(half * n_ep // 2, (half + 1) * n_ep // 2)
        for e in blocks:
            pieces[e] = [
                arrays(names[e][d // 2]) if d % 2 == 0 else other[names[e][d // 2]]
                for d in range(n_tp)
            ]
        mine = pieces[blocks[0] : blocks[-1] + 1]
        out = rows_call(half == 0, where, mine, w_in, w_out, tok)
        if half == 0:
            count = len(blocks) * pairs
            step = max(1, count // 2)
            for i in range(0, count, step):
                come = lanes.send(out[2][1, i : i + step], "t0")
                total = (out[2][0, i : i + step].astype(F32) + come.astype(F32)).astype(BF16)
                for k in range(step):
                    terms[names[(i + k) // pairs][(i + k) % pairs]] = total[k]
            near = grads_call(where, out[0], out[1], mine, list(range(n_tp)))
            done += [out[1], hop(near[1][:16, :128], "tp", 1)]
        else:
            last = out[1]
            grads = grads_call(where, out[0], out[1], mine, list(range(n_tp)), near)

    keep = {}
    for e in range(n_ep // 2):
        for y in range(pairs):
            keep[e, y] = terms[names[e][y]].astype(F32)
    top = n_ep // 4
    for e in range(n_ep // 2 - 1, top, -1):
        for y in range(pairs):
            if y and e > top:
                keep[e - top, y] += hop(keep[e, y].astype(BF16), "ep", top).astype(F32)
            elif e > top:
                keep[top, 0] += hop(keep[e, y].astype(BF16), "ep", e - top).astype(F32)
    for y in range(1, pairs):
        keep[top, 0] += hop(keep[top, y].astype(BF16), "tp", 2 * y).astype(F32)
    total = keep[0, 0]
    for e in range(top + 1):
        for y in range(pairs if e < top else 1):
            if e or y:
                sums = keep[e, y].astype(BF16)
                total = total + leap(after(sums, last) if True else sums, e, 2 * y).astype(F32)
    in_grad = total.astype(BF16)

    grad_in, grad_out = grads
    return in_grad, grad_in.reshape(1, 2, ffl, -1), grad_out[None]


def solution(mesh):
    return jax.shard_map(
        body,
        mesh=mesh,
        in_specs=(
            P("ep", "tp"),
            P("ep", "tp"),
            P("ep", None),
            P("ep", None),
            P("ep", None, "tp", None),
            P("ep", "tp", None),
        ),
        out_specs=(P("ep", "tp"), P("ep", None, "tp", None), P("ep", "tp", None)),
        check_vma=False,
    )
```

time: 187 us -> 138 us (0.74)
  blocking collectives: 27.5 us -> 0 us
  waiting for transfers between devices: 66 us -> 44.4 us
  local copies, waits for them, and re-layouts: 9.63 us -> 4.69 us
  Pallas kernels: 44.7 us -> 49.3 us
  starting transfers between devices: 28.9 us -> 33.3 us
  other arithmetic: 8.63 us -> 5.39 us
    all_gather x1 -> x0, blocking collectives: 27.5 us -> none  [scales(): every = lax.all_gather(own, 'ep', axis=0)]
    ppermute x31 -> x41, waiting for transfers between devices: 66 us -> 44.3 us  [hop(): return lax.ppermute(block, axis, [(i, i ^ bit) for i in range(count)])]
    unnamed x36 -> x50, local copies, waits for them, and re-layouts: 9.3 us -> 2.68 us
    another operation x7 -> x1, other arithmetic: 6.34 us -> 0.62 us  [body(): jnp.stack([lax.axis_index('tp'), expert, expert + n_ep // 2])]
    ppermute x0 -> x4, starting transfers between devices: none -> 4.92 us  [leap(): lax.ppermute(block, ('ep', 'tp'), [(i, i ^ apart) for i in range(count)])]
    pallas_call x5 -> x4, Pallas kernels: 44.7 us -> 49.3 us  [the longest x2 26.4 us: rows_call(): pl.pallas_call(functools.partial(rows_kernel, n_tp, sizes, part), out_sha...]
    ppermute x31 -> x41, starting transfers between devices: 28.9 us -> 28.4 us  [hop(): return lax.ppermute(block, axis, [(i, i ^ bit) for i in range(count)])]
  transfers between devices with their start and end apart: 31 -> 45, of which waited for: 14 -> 13; matrix products, arithmetic and copies ran while one was open for 4% -> 3% of each run, Pallas kernels for 24% -> 36%
where the time goes in v2:
time: 138 us
  Pallas kernels  49.3 us (36%)
  waiting for transfers between devices  44.4 us (32%)
  starting transfers between devices  33.3 us (24%)
  other arithmetic  5.39 us (4%)
  local copies, waits for them, and re-layouts  4.69 us (3%)
    ppermute x41, waiting for transfers between devices, hop(): return lax.ppermute(block, axis, [(i, i ^ bit) for i in range(count)])  44.3 us
    ppermute x41, starting transfers between devices, hop(): return lax.ppermute(block, axis, [(i, i ^ bit) for i in range(count)])  28.4 us
    pallas_call x2, Pallas kernels, rows_call(): pl.pallas_call(functools.partial(rows_kernel, n_tp, sizes, part), out_sha...  26.4 us
    pallas_call x2, Pallas kernels, grads_call(): pl.pallas_call(functools.partial(grads_kernel, steps, sizes, len(base) >...  22.9 us
    ppermute x4, starting transfers between devices, leap(): lax.ppermute(block, ('ep', 'tp'), [(i, i ^ apart) for i in range(count)])  4.92 us
  transfers between devices with their start and end apart: 45, of which 13 were waited for; matrix products, arithmetic and copies ran while one was open for 3% of the time, Pallas kernels for 36%

profile of v2, /device:TPU:0, one launch (start us, length us, event | category | flops | bytes accessed | tf_op | source)
XLA Modules:
  0.0 138.1 jit_solution(10686888726363823277)
XLA Ops:
  2.4 3.0 %collective-permute-start.1 = (bf16[272,1024]{1,0:T(8,128)(2,1)S(1)}, bf16[272,1024]{1,0:T(8,128)(2,1)S(1)}, u32[]{:S(2)}, u32[]{:S(2)}) collective-permute-start(bf16[272,1024]{1,0:T(8,128)(2,1)S(1)} %fusion.3.refs_0_), channel_id=1, source_target_pairs={{0,2},{1,3},{2,0},{3,1},{4,6},{5,7},{6,4},{7,5},{8,10},{9,11},{10,... | collective-permute-start | bytes 1671176 | tf_op jit(solution)/shard_map/ppermute | solution.py:19
  5.5 1.5 %collective-permute-start.3 = (bf16[272,1024]{1,0:T(8,128)(2,1)S(1)}, bf16[272,1024]{1,0:T(8,128)(2,1)S(1)}, u32[]{:S(2)}, u32[]{:S(2)}) collective-permute-start(bf16[272,1024]{1,0:T(8,128)(2,1)S(1)} %fusion.3.refs_0_), channel_id=1, source_target_pairs={{0,4},{4,0},{8,12},{12,8},{16,20},{20,16},{24,28},{28,24},{1,5},{5... | collective-permute-start | bytes 1671176 | tf_op jit(solution)/shard_map/ppermute | solution.py:19
  7.0 1.6 %collective-permute-start.9 = (bf16[272,1024]{1,0:T(8,128)(2,1)S(1)}, bf16[272,1024]{1,0:T(8,128)(2,1)S(1)}, u32[]{:S(2)}, u32[]{:S(2)}) collective-permute-start(bf16[272,1024]{1,0:T(8,128)(2,1)S(1)} %fusion.3.refs_0_), channel_id=1, source_target_pairs={{0,8},{4,12},{8,0},{12,4},{16,24},{20,28},{24,16},{28,20},{1,9},{5... | collective-permute-start | bytes 1671176 | tf_op jit(solution)/shard_map/ppermute | solution.py:19
  8.5 2.6 %collective-permute-start.11 = (bf16[272,1024]{1,0:T(8,128)(2,1)S(1)}, bf16[272,1024]{1,0:T(8,128)(2,1)}, u32[]{:S(2)}, u32[]{:S(2)}) collective-permute-start(bf16[272,1024]{1,0:T(8,128)(2,1)S(1)} %fusion.3.refs_0_), channel_id=1, source_target_pairs={{0,16},{4,20},{8,24},{12,28},{16,0},{20,4},{24,8},{28,12},{1,17},{... | collective-permute-start | bytes 1671176 | tf_op jit(solution)/shard_map/ppermute | solution.py:19
  11.1 7.0 %collective-permute-done.1.refs_2_ = bf16[272,1024]{1,0:T(8,128)(2,1)S(1)} collective-permute-done((bf16[272,1024]{1,0:T(8,128)(2,1)S(1)}, bf16[272,1024]{1,0:T(8,128)(2,1)S(1)}, u32[]{:S(2)}, u32[]{:S(2)}) %collective-permute-start.1) | collective-permute-done | bytes 557088 | tf_op jit(solution)/shard_map/ppermute | solution.py:19
  19.5 1.5 %collective-permute-start.5 = (bf16[128,1024]{1,0:T(8,128)(2,1)S(1)}, bf16[128,1024]{1,0:T(8,128)(2,1)S(1)}, u32[]{:S(2)}, u32[]{:S(2)}) collective-permute-start(bf16[128,1024]{1,0:T(8,128)(2,1)S(1)} %slice.68), channel_id=1, source_target_pairs={{0,4},{4,0},{8,12},{12,8},{16,20},{20,16},{24,28},{28,24},{1,5},{5... | collective-permute-start | bytes 786440 | tf_op jit(solution)/shard_map/ppermute | solution.py:19
  21.6 10.9 %collective-permute-done.9.refs_9_ = bf16[272,1024]{1,0:T(8,128)(2,1)S(1)} collective-permute-done((bf16[272,1024]{1,0:T(8,128)(2,1)S(1)}, bf16[272,1024]{1,0:T(8,128)(2,1)S(1)}, u32[]{:S(2)}, u32[]{:S(2)}) %collective-permute-start.9) | collective-permute-done | bytes 557088 | tf_op jit(solution)/shard_map/ppermute | solution.py:19
  32.6 2.5 %collective-permute-done.11.refs_0_ = bf16[272,1024]{1,0:T(8,128)(2,1)} collective-permute-done((bf16[272,1024]{1,0:T(8,128)(2,1)S(1)}, bf16[272,1024]{1,0:T(8,128)(2,1)}, u32[]{:S(2)}, u32[]{:S(2)}) %collective-permute-start.11) | collective-permute-done | bytes 557088 | tf_op jit(solution)/shard_map/ppermute | solution.py:19
  37.6 10.1 %collective-permute-done.14.refs_13_ = bf16[272,1024]{1,0:T(8,128)(2,1)} collective-permute-done((bf16[272,1024]{1,0:T(8,128)(2,1)S(1)}, bf16[272,1024]{1,0:T(8,128)(2,1)}, u32[]{:S(2)}, u32[]{:S(2)}) %collective-permute-start.14) | collective-permute-done | bytes 557088 | tf_op jit(solution)/shard_map/ppermute | solution.py:19
  47.7 3.1 %collective-permute-done.12.refs_11_ = bf16[272,1024]{1,0:T(8,128)(2,1)} collective-permute-done((bf16[272,1024]{1,0:T(8,128)(2,1)S(1)}, bf16[272,1024]{1,0:T(8,128)(2,1)}, u32[]{:S(2)}, u32[]{:S(2)}) %collective-permute-start.12) | collective-permute-done | bytes 557088 | tf_op jit(solution)/shard_map/ppermute | solution.py:19
  53.6 1.4 %collective-permute-start.20 = (bf16[272,1024]{1,0:T(8,128)(2,1)}, bf16[272,1024]{1,0:T(8,128)(2,1)}, u32[]{:S(2)}, u32[]{:S(2)}) collective-permute-start(bf16[272,1024]{1,0:T(8,128)(2,1)} %collective-permute-done.11.refs_0_), channel_id=1, source_target_pairs={{0,2},{1,3},{2,0},{3,1},{4,6},{5,7},{6,4},{7,5},{8,10},{9,11},{10,... | collective-permute-start | bytes 1671176 | tf_op jit(solution)/shard_map/ppermute | solution.py:19
  55.1 1.5 %collective-permute-start.22 = (bf16[272,1024]{1,0:T(8,128)(2,1)}, bf16[272,1024]{1,0:T(8,128)(2,1)}, u32[]{:S(2)}, u32[]{:S(2)}) collective-permute-start(bf16[272,1024]{1,0:T(8,128)(2,1)} %collective-permute-done.11.refs_0_), channel_id=1, source_target_pairs={{0,4},{4,0},{8,12},{12,8},{16,20},{20,16},{24,28},{28,24},{1,5},{5... | collective-permute-start | bytes 1671176 | tf_op jit(solution)/shard_map/ppermute | solution.py:19
  57.1 15.4 %rows.2 = (bf16[768,512]{1,0:T(8,128)(2,1)}, bf16[384,512]{1,0:T(8,128)(2,1)}, bf16[2,8,128,1024]{3,2,1,0:T(8,128)(2,1)}) custom-call(s32[3]{0:T(128)} %pad_add_fusion.where_ref, bf16[768,4096]{1,0:T(8,128)(2,1)} %bitcast.47, bf16[384,4096]{1,0:T(8,128)(2,1)} %bitcast.49, bf16[272,1024]{1,0:T(8,128)(2,1)} %copy-done.14, bf16[272,1024]{1,0:T(8,128)(2,1)} %copy-done.19, ...), custom_call_target="tpu_custom_call" | custom-call | flops 8053063680 | bytes 17825792 | tf_op jit(solution)/shard_map/rows/pallas_call | solution.py:189
  73.7 1.6 %collective-permute-start.30 = (bf16[272,1024]{1,0:T(8,128)(2,1)}, bf16[272,1024]{1,0:T(8,128)(2,1)S(1)}, u32[]{:S(2)}, u32[]{:S(2)}) collective-permute-start(bf16[272,1024]{1,0:T(8,128)(2,1)} %collective-permute-done.22.refs_4_), channel_id=1, source_target_pairs={{0,8},{4,12},{8,0},{12,4},{16,24},{20,28},{24,16},{28,20},{1,9},{5... | collective-permute-start | bytes 1671176 | tf_op jit(solution)/shard_map/ppermute | solution.py:19
  75.3 10.6 %grads.2 = (bf16[768,4096]{1,0:T(8,128)(2,1)}, bf16[384,4096]{1,0:T(8,128)(2,1)}) custom-call(s32[3]{0:T(128)} %pad_add_fusion.where_ref, bf16[768,512]{1,0:T(8,128)(2,1)} %get-tuple-element.42.dadb_ref, bf16[384,512]{1,0:T(8,128)(2,1)} %get-tuple-element.38.hid_ref, bf16[272,1024]{1,0:T(8,128)(2,1)} %copy-done.14, bf16[272,1024]{1,0:T(8,128)(2,1)} %copy-done.19, ...), custom_call_target="tpu_custom_call" | custom-call | flops 4831838208 | bytes 17825792 | tf_op jit(solution)/shard_map/grads/pallas_call | solution.py:285
  89.7 1.7 %collective-permute-done.21.refs_3_ = bf16[272,1024]{1,0:T(8,128)(2,1)S(1)} collective-permute-done((bf16[272,1024]{1,0:T(8,128)(2,1)}, bf16[272,1024]{1,0:T(8,128)(2,1)S(1)}, u32[]{:S(2)}, u32[]{:S(2)}) %collective-permute-start.21) | collective-permute-done | bytes 557088 | tf_op jit(solution)/shard_map/ppermute | solution.py:19
  91.4 1.5 %collective-permute-start.33 = (bf16[128,1024]{1,0:T(8,128)(2,1)S(1)}, bf16[128,1024]{1,0:T(8,128)(2,1)S(1)}, u32[]{:S(2)}, u32[]{:S(2)}) collective-permute-start(bf16[128,1024]{1,0:T(8,128)(2,1)S(1)} %slice.72), channel_id=1, source_target_pairs={{0,4},{4,0},{8,12},{12,8},{16,20},{20,16},{24,28},{28,24},{1,5},{5... | collective-permute-start | bytes 786440 | tf_op jit(solution)/shard_map/ppermute | solution.py:19
  96.2 3.8 %collective-permute-done.33.refs_14_ = bf16[128,1024]{1,0:T(8,128)(2,1)S(1)} collective-permute-done((bf16[128,1024]{1,0:T(8,128)(2,1)S(1)}, bf16[128,1024]{1,0:T(8,128)(2,1)S(1)}, u32[]{:S(2)}, u32[]{:S(2)}) %collective-permute-start.33) | collective-permute-done | bytes 262176 | tf_op jit(solution)/shard_map/ppermute | solution.py:19
  100.0 2.2 %collective-permute-done.34.refs_15_ = bf16[144,1024]{1,0:T(8,128)(2,1)S(1)} collective-permute-done((bf16[144,1024]{1,0:T(8,128)(2,1)S(1)}, bf16[144,1024]{1,0:T(8,128)(2,1)S(1)}, u32[]{:S(2)}, u32[]{:S(2)}) %collective-permute-start.34) | collective-permute-done | bytes 294944 | tf_op jit(solution)/shard_map/ppermute | solution.py:19
  102.3 1.5 %collective-permute-start.43 = (bf16[128,1024]{1,0:T(8,128)(2,1)S(1)}, bf16[128,1024]{1,0:T(8,128)(2,1)S(1)}, u32[]{:S(2)}, u32[]{:S(2)}) collective-permute-start(bf16[128,1024]{1,0:T(8,128)(2,1)S(1)} %get-tuple-element.62), channel_id=1, source_target_pairs={{0,2},{1,3},{2,0},{3,1},{4,6},{5,7},{6,4},{7,5},{8,10},{9,11},{10,... | collective-permute-start | bytes 786440 | tf_op jit(solution)/shard_map/ppermute | solution.py:19
  103.8 1.5 %collective-permute-start.42 = (bf16[128,1024]{1,0:T(8,128)(2,1)S(1)}, bf16[128,1024]{1,0:T(8,128)(2,1)S(1)}, u32[]{:S(2)}, u32[]{:S(2)}) collective-permute-start(bf16[128,1024]{1,0:T(8,128)(2,1)S(1)} %get-tuple-element.63), channel_id=1, source_target_pairs={{0,4},{4,0},{8,12},{12,8},{16,20},{20,16},{24,28},{28,24},{1,5},{5... | collective-permute-start | bytes 786440 | tf_op jit(solution)/shard_map/ppermute | solution.py:19
  107.6 11.0 %rows.3 = (bf16[768,512]{1,0:T(8,128)(2,1)}, bf16[384,512]{1,0:T(8,128)(2,1)}) custom-call(s32[3]{0:T(128)} %pad_add_fusion.where_ref, bf16[768,4096]{1,0:T(8,128)(2,1)} %bitcast.48, bf16[384,4096]{1,0:T(8,128)(2,1)} %bitcast.50, bf16[272,1024]{1,0:T(8,128)(2,1)} %collective-permute-done.11.refs_0_, bf16[272,1024]{1,0:T(8,128)(2,1)} %copy-done.3, ...), custom_call_target="tpu_custom_call" | custom-call | flops 4831838208 | bytes 17825792 | tf_op jit(solution)/shard_map/rows/pallas_call | solution.py:189
  122.4 2.4 %collective-permute-start.41 = (bf16[128,1024]{1,0:T(8,128)(2,1)S(1)}, bf16[128,1024]{1,0:T(8,128)(2,1)S(1)}, u32[]{:S(2)}, u32[]{:S(2)}) collective-permute-start(bf16[128,1024]{1,0:T(8,128)(2,1)S(1)} %fusion.6), channel_id=1, source_target_pairs={{0,6},{1,7},{2,4},{3,5},{4,2},{5,3},{6,0},{7,1},{8,14},{9,15},{10,... | collective-permute-start | bytes 786440 | tf_op jit(solution)/shard_map/ppermute | solution.py:25
  124.8 12.4 %grads.3 = (bf16[768,4096]{1,0:T(8,128)(2,1)}, bf16[384,4096]{1,0:T(8,128)(2,1)}) custom-call(s32[3]{0:T(128)} %pad_add_fusion.where_ref, bf16[768,512]{1,0:T(8,128)(2,1)} %get-tuple-element.51.dadb_ref, bf16[384,512]{1,0:T(8,128)(2,1)} %get-tuple-element.46.hid_ref, bf16[272,1024]{1,0:T(8,128)(2,1)} %collective-permute-done.11.refs_0_, ...), custom_call_target="tpu_custom_call" | custom-call | flops 4831838208 | bytes 17825792 | tf_op jit(solution)/shard_map/grads/pallas_call | solution.py:285
  (136 shorter events, 25.0 us)
Async XLA Ops:
  2.4 15.7 %collective-permute-start.1 = (bf16[272,1024]{1,0:T(8,128)(2,1)S(1)}, bf16[272,1024]{1,0:T(8,128)(2,1)S(1)}, u32[]{:S(2)}, u32[]{:S(2)}) collective-permute-start(bf16[272,1024]{1,0:T(8,128)(2,1)S(1)} %fusion.3.refs_0_), channel_id=1, source_target_pairs={{0,2},{1,3},{2,0},{3,1},{4,6},{5,7},{6,4},{7,5},{8,10},{9,11},{10,... | collective-permute-start | bytes 1671176 | tf_op jit(solution)/shard_map/ppermute | solution.py:19
  7.0 25.6 %collective-permute-start.9 = (bf16[272,1024]{1,0:T(8,128)(2,1)S(1)}, bf16[272,1024]{1,0:T(8,128)(2,1)S(1)}, u32[]{:S(2)}, u32[]{:S(2)}) collective-permute-start(bf16[272,1024]{1,0:T(8,128)(2,1)S(1)} %fusion.3.refs_0_), channel_id=1, source_target_pairs={{0,8},{4,12},{8,0},{12,4},{16,24},{20,28},{24,16},{28,20},{1,9},{5... | collective-permute-start | bytes 1671176 | tf_op jit(solution)/shard_map/ppermute | solution.py:19
  8.5 26.5 %collective-permute-start.11 = (bf16[272,1024]{1,0:T(8,128)(2,1)S(1)}, bf16[272,1024]{1,0:T(8,128)(2,1)}, u32[]{:S(2)}, u32[]{:S(2)}) collective-permute-start(bf16[272,1024]{1,0:T(8,128)(2,1)S(1)} %fusion.3.refs_0_), channel_id=1, source_target_pairs={{0,16},{4,20},{8,24},{12,28},{16,0},{20,4},{24,8},{28,12},{1,17},{... | collective-permute-start | bytes 1671176 | tf_op jit(solution)/shard_map/ppermute | solution.py:19
  11.1 25.1 %collective-permute-start = (bf16[272,1024]{1,0:T(8,128)(2,1)S(1)}, bf16[272,1024]{1,0:T(8,128)(2,1)S(1)}, u32[]{:S(2)}, u32[]{:S(2)}) collective-permute-start(bf16[272,1024]{1,0:T(8,128)(2,1)S(1)} %fusion.3.refs_0_), channel_id=1, source_target_pairs={{0,1},{1,0},{2,3},{3,2},{4,5},{5,4},{6,7},{7,6},{8,9},{9,8},{10,11... | collective-permute-start | bytes 1671176 | tf_op jit(solution)/shard_map/ppermute | solution.py:19
  19.5 15.5 %collective-permute-start.5 = (bf16[128,1024]{1,0:T(8,128)(2,1)S(1)}, bf16[128,1024]{1,0:T(8,128)(2,1)S(1)}, u32[]{:S(2)}, u32[]{:S(2)}) collective-permute-start(bf16[128,1024]{1,0:T(8,128)(2,1)S(1)} %slice.68), channel_id=1, source_target_pairs={{0,4},{4,0},{8,12},{12,8},{16,20},{20,16},{24,28},{28,24},{1,5},{5... | collective-permute-start | bytes 786440 | tf_op jit(solution)/shard_map/ppermute | solution.py:19
  21.1 14.5 %collective-permute-start.6 = (bf16[144,1024]{1,0:T(8,128)(2,1)S(1)}, bf16[144,1024]{1,0:T(8,128)(2,1)S(1)}, u32[]{:S(2)}, u32[]{:S(2)}) collective-permute-start(bf16[144,1024]{1,0:T(8,128)(2,1)S(1)} %slice.69), channel_id=1, source_target_pairs={{0,2},{1,3},{2,0},{3,1},{4,6},{5,7},{6,4},{7,5},{8,10},{9,11},{10,... | collective-permute-start | bytes 884744 | tf_op jit(solution)/shard_map/ppermute | solution.py:19
  35.6 15.2 %collective-permute-start.12 = (bf16[272,1024]{1,0:T(8,128)(2,1)S(1)}, bf16[272,1024]{1,0:T(8,128)(2,1)}, u32[]{:S(2)}, u32[]{:S(2)}) collective-permute-start(bf16[272,1024]{1,0:T(8,128)(2,1)S(1)} %collective-permute-done.9.refs_9_), channel_id=1, source_target_pairs={{0,2},{1,3},{2,0},{3,1},{4,6},{5,7},{6,4},{7,5},{8,10},{9,11},{10,... | collective-permute-start | bytes 1671176 | tf_op jit(solution)/shard_map/ppermute | solution.py:19
  36.2 14.9 %collective-permute-start.16 = (bf16[272,1024]{1,0:T(8,128)(2,1)S(1)}, bf16[272,1024]{1,0:T(8,128)(2,1)}, u32[]{:S(2)}, u32[]{:S(2)}) collective-permute-start(bf16[272,1024]{1,0:T(8,128)(2,1)S(1)} %constant_dynamic-update-slice_fusion.refs_6_), channel_id=1, source_target_pairs={{0,8},{4,12},{8,0},{12,4},{16,24},{20,28},{24,16},{28,20},{1,9},{5... | collective-permute-start | bytes 1671176 | tf_op jit(solution)/shard_map/ppermute | solution.py:19
  37.1 14.2 %collective-permute-start.4 = (bf16[272,1024]{1,0:T(8,128)(2,1)S(1)}, bf16[272,1024]{1,0:T(8,128)(2,1)S(1)}, u32[]{:S(2)}, u32[]{:S(2)}) collective-permute-start(bf16[272,1024]{1,0:T(8,128)(2,1)S(1)} %collective-permute-done.3.refs_4_), channel_id=1, source_target_pairs={{0,1},{1,0},{2,3},{3,2},{4,5},{5,4},{6,7},{7,6},{8,9},{9,8},{10,11... | collective-permute-start | bytes 1671176 | tf_op jit(solution)/shard_map/ppermute | solution.py:19
  37.3 15.5 %collective-permute-start.10 = (bf16[272,1024]{1,0:T(8,128)(2,1)S(1)}, bf16[272,1024]{1,0:T(8,128)(2,1)}, u32[]{:S(2)}, u32[]{:S(2)}) collective-permute-start(bf16[272,1024]{1,0:T(8,128)(2,1)S(1)} %collective-permute-done.9.refs_9_), channel_id=1, source_target_pairs={{0,1},{1,0},{2,3},{3,2},{4,5},{5,4},{6,7},{7,6},{8,9},{9,8},{10,11... | collective-permute-start | bytes 1671176 | tf_op jit(solution)/shard_map/ppermute | solution.py:19
  52.8 33.9 %collective-permute-start.19 = (bf16[272,1024]{1,0:T(8,128)(2,1)}, bf16[272,1024]{1,0:T(8,128)(2,1)S(1)}, u32[]{:S(2)}, u32[]{:S(2)}) collective-permute-start(bf16[272,1024]{1,0:T(8,128)(2,1)} %collective-permute-done.11.refs_0_), channel_id=1, source_target_pairs={{0,1},{1,0},{2,3},{3,2},{4,5},{5,4},{6,7},{7,6},{8,9},{9,8},{10,11... | collective-permute-start | bytes 1671176 | tf_op jit(solution)/shard_map/ppermute | solution.py:19
  53.6 18.8 %collective-permute-start.20 = (bf16[272,1024]{1,0:T(8,128)(2,1)}, bf16[272,1024]{1,0:T(8,128)(2,1)}, u32[]{:S(2)}, u32[]{:S(2)}) collective-permute-start(bf16[272,1024]{1,0:T(8,128)(2,1)} %collective-permute-done.11.refs_0_), channel_id=1, source_target_pairs={{0,2},{1,3},{2,0},{3,1},{4,6},{5,7},{6,4},{7,5},{8,10},{9,11},{10,... | collective-permute-start | bytes 1671176 | tf_op jit(solution)/shard_map/ppermute | solution.py:19
  55.1 17.4 %collective-permute-start.22 = (bf16[272,1024]{1,0:T(8,128)(2,1)}, bf16[272,1024]{1,0:T(8,128)(2,1)}, u32[]{:S(2)}, u32[]{:S(2)}) collective-permute-start(bf16[272,1024]{1,0:T(8,128)(2,1)} %collective-permute-done.11.refs_0_), channel_id=1, source_target_pairs={{0,4},{4,0},{8,12},{12,8},{16,20},{20,16},{24,28},{28,24},{1,5},{5... | collective-permute-start | bytes 1671176 | tf_op jit(solution)/shard_map/ppermute | solution.py:19
  56.6 15.9 %collective-permute-start.24 = (bf16[272,1024]{1,0:T(8,128)(2,1)}, bf16[272,1024]{1,0:T(8,128)(2,1)}, u32[]{:S(2)}, u32[]{:S(2)}) collective-permute-start(bf16[272,1024]{1,0:T(8,128)(2,1)} %collective-permute-done.11.refs_0_), channel_id=1, source_target_pairs={{0,8},{4,12},{8,0},{12,4},{16,24},{20,28},{24,16},{28,20},{1,9},{5... | collective-permute-start | bytes 1671176 | tf_op jit(solution)/shard_map/ppermute | solution.py:19
  72.5 15.4 %collective-permute-start.25 = (bf16[272,1024]{1,0:T(8,128)(2,1)}, bf16[272,1024]{1,0:T(8,128)(2,1)}, u32[]{:S(2)}, u32[]{:S(2)}) collective-permute-start(bf16[272,1024]{1,0:T(8,128)(2,1)} %collective-permute-done.20.refs_2_), channel_id=1, source_target_pairs={{0,4},{4,0},{8,12},{12,8},{16,20},{20,16},{24,28},{28,24},{1,5},{5... | collective-permute-start | bytes 1671176 | tf_op jit(solution)/shard_map/ppermute | solution.py:19
  73.1 15.1 %collective-permute-start.28 = (bf16[272,1024]{1,0:T(8,128)(2,1)}, bf16[272,1024]{1,0:T(8,128)(2,1)}, u32[]{:S(2)}, u32[]{:S(2)}) collective-permute-start(bf16[272,1024]{1,0:T(8,128)(2,1)} %collective-permute-done.24.refs_8_), channel_id=1, source_target_pairs={{0,2},{1,3},{2,0},{3,1},{4,6},{5,7},{6,4},{7,5},{8,10},{9,11},{10,... | collective-permute-start | bytes 1671176 | tf_op jit(solution)/shard_map/ppermute | solution.py:19
  73.7 14.7 %collective-permute-start.30 = (bf16[272,1024]{1,0:T(8,128)(2,1)}, bf16[272,1024]{1,0:T(8,128)(2,1)S(1)}, u32[]{:S(2)}, u32[]{:S(2)}) collective-permute-start(bf16[272,1024]{1,0:T(8,128)(2,1)} %collective-permute-done.22.refs_4_), channel_id=1, source_target_pairs={{0,8},{4,12},{8,0},{12,4},{16,24},{20,28},{24,16},{28,20},{1,9},{5... | collective-permute-start | bytes 1671176 | tf_op jit(solution)/shard_map/ppermute | solution.py:19
  102.3 17.6 %collective-permute-start.43 = (bf16[128,1024]{1,0:T(8,128)(2,1)S(1)}, bf16[128,1024]{1,0:T(8,128)(2,1)S(1)}, u32[]{:S(2)}, u32[]{:S(2)}) collective-permute-start(bf16[128,1024]{1,0:T(8,128)(2,1)S(1)} %get-tuple-element.62), channel_id=1, source_target_pairs={{0,2},{1,3},{2,0},{3,1},{4,6},{5,7},{6,4},{7,5},{8,10},{9,11},{10,... | collective-permute-start | bytes 786440 | tf_op jit(solution)/shard_map/ppermute | solution.py:19
  103.8 16.1 %collective-permute-start.42 = (bf16[128,1024]{1,0:T(8,128)(2,1)S(1)}, bf16[128,1024]{1,0:T(8,128)(2,1)S(1)}, u32[]{:S(2)}, u32[]{:S(2)}) collective-permute-start(bf16[128,1024]{1,0:T(8,128)(2,1)S(1)} %get-tuple-element.63), channel_id=1, source_target_pairs={{0,4},{4,0},{8,12},{12,8},{16,20},{20,16},{24,28},{28,24},{1,5},{5... | collective-permute-start | bytes 786440 | tf_op jit(solution)/shard_map/ppermute | solution.py:19
  105.3 17.0 %collective-permute-start.40 = (bf16[128,1024]{1,0:T(8,128)(2,1)S(1)}, bf16[128,1024]{1,0:T(8,128)(2,1)S(1)}, u32[]{:S(2)}, u32[]{:S(2)}) collective-permute-start(bf16[128,1024]{1,0:T(8,128)(2,1)S(1)} %get-tuple-element.61), channel_id=1, source_target_pairs={{0,8},{4,12},{8,0},{12,4},{16,24},{20,28},{24,16},{28,20},{1,9},{5... | collective-permute-start | bytes 786440 | tf_op jit(solution)/shard_map/ppermute | solution.py:19
  118.7 18.5 %collective-permute-start.38 = (bf16[128,1024]{1,0:T(8,128)(2,1)S(1)}, bf16[128,1024]{1,0:T(8,128)(2,1)S(1)}, u32[]{:S(2)}, u32[]{:S(2)}) collective-permute-start(bf16[128,1024]{1,0:T(8,128)(2,1)S(1)} %get-tuple-element.48), channel_id=1, source_target_pairs={{0,4},{1,5},{2,6},{3,7},{4,0},{5,1},{6,2},{7,3},{8,12},{9,13},{10,... | collective-permute-start | bytes 786440 | tf_op jit(solution)/shard_map/ppermute | solution.py:25
  119.3 17.9 %collective-permute-start.37 = (bf16[128,1024]{1,0:T(8,128)(2,1)S(1)}, bf16[128,1024]{1,0:T(8,128)(2,1)S(1)}, u32[]{:S(2)}, u32[]{:S(2)}) collective-permute-start(bf16[128,1024]{1,0:T(8,128)(2,1)S(1)} %get-tuple-element.47), channel_id=1, source_target_pairs={{0,2},{1,3},{2,0},{3,1},{4,6},{5,7},{6,4},{7,5},{8,10},{9,11},{10,... | collective-permute-start | bytes 786440 | tf_op jit(solution)/shard_map/ppermute | solution.py:25
  121.0 16.2 %collective-permute-start.44 = (bf16[128,1024]{1,0:T(8,128)(2,1)S(1)}, bf16[128,1024]{1,0:T(8,128)(2,1)S(1)}, u32[]{:S(2)}, u32[]{:S(2)}) collective-permute-start(bf16[128,1024]{1,0:T(8,128)(2,1)S(1)} %fusion.5), channel_id=1, source_target_pairs={{0,8},{1,9},{2,10},{3,11},{4,12},{5,13},{6,14},{7,15},{8,0},{9,1},... | collective-permute-start | bytes 786440 | tf_op jit(solution)/shard_map/ppermute | solution.py:25
  122.4 14.8 %collective-permute-start.41 = (bf16[128,1024]{1,0:T(8,128)(2,1)S(1)}, bf16[128,1024]{1,0:T(8,128)(2,1)S(1)}, u32[]{:S(2)}, u32[]{:S(2)}) collective-permute-start(bf16[128,1024]{1,0:T(8,128)(2,1)S(1)} %fusion.6), channel_id=1, source_target_pairs={{0,6},{1,7},{2,4},{3,5},{4,2},{5,3},{6,0},{7,1},{8,14},{9,15},{10,... | collective-permute-start | bytes 786440 | tf_op jit(solution)/shard_map/ppermute | solution.py:25
  (45 other events, 424.2 us)

commit v3 on v2

--- a/solution.py
+++ b/solution.py
@@ -59,7 +59,7 @@
             ((x, n), x, 2, (f,)), ((y, n), y, 2, (f,)), ((x, y, n), n, 2, (f,)),
             ((x, f), x, 2, *near), ((y, f), y, 2, *near), ((n, f), n, 2, *near),
             ((x, y, f), x, 2, *far, 0), ((y, n, f), y, 2, *far, 0), ((x, n, f), n, 2, *far, 0),
-            ((x, y, n, f), x, 0, 1), ((x, y, n, f), y, 1, 1),
+            ((x, y, n, f), x, 0), ((x, y, n, f), y, 1),
         ]
     bits = bits_of(n_ep, "e") + bits_of(n_tp, "t", 1)
     plan = []
@@ -100,7 +100,8 @@
         pieces[k // n_tp].append(refs[:size])
         refs = refs[size:]
     if part:
-        dadb_ref, hid_ref, part_ref, *refs = refs
+        dadb_ref, hid_ref, *part_refs = refs[:5]
+        refs = refs[5:]
     else:
         dadb_ref, hid_ref, *refs = refs
     xs, gs, ps, wi, wo, acc, sems, psems, wsems = refs
@@ -167,7 +168,9 @@
         for d in range(n_tp):
             out = jnp.dot(lhs, wi[d], preferred_element_type=F32).astype(BF16)
             for j in range(blocks):
-                part_ref[d % 2, j * (n_tp // 2) + d // 2] = out[j * tok : (j + 1) * tok]
+                piece, half = j * (n_tp // 2) + d // 2, blocks * n_tp // 4
+                into = part_refs[1 + piece // half] if d % 2 else part_refs[0]
+                into[piece % half if d % 2 else piece] = out[j * tok : (j + 1) * tok]
 
 
 def rows_call(part, where, pieces, w_in, w_out, tok):
@@ -183,7 +186,9 @@
         jax.ShapeDtypeStruct((ffl, rows), BF16),
     ]
     if part:
-        outs.append(jax.ShapeDtypeStruct((2, blocks * n_tp // 2, tok, width), BF16))
+        outs += [
+            jax.ShapeDtypeStruct((blocks * n_tp // k, tok, width), BF16) for k in (2, 4, 4)
+        ]
     vmem = pl.BlockSpec(memory_space=pltpu.VMEM)
     hbm = pl.BlockSpec(memory_space=pltpu.HBM)
     return pl.pallas_call(
@@ -210,6 +215,151 @@
         ),
         name="rows",
     )(where, w_in, w_out, *arrays)
+
+
+def far_kernel(n_tp, sizes, where_ref, win_ref, wout_ref, *refs):
+    blocks = len(sizes) // n_tp
+    pieces = [[] for _ in range(blocks)]
+    for k, size in enumerate(sizes):
+        pieces[k // n_tp].append(refs[:size])
+        refs = refs[size:]
+    base, refs = refs[:2], refs[2:]
+    gin_ref, gout_ref, xs, gs, ps, wi, wo, acc, dadb_ref, hid_ref, bi, bo, oi, oo, *refs = refs
+    sems, psems, wsems, bsems, osems = refs
+    ffl = hid_ref.shape[0]
+    tok = hid_ref.shape[1] // blocks
+    width = wout_ref.shape[1] // n_tp
+
+    def column(d):
+        return pl.ds(pl.multiple_of((where_ref[0] ^ d) * width, width), width)
+
+    copies = []
+    for d in range(n_tp):
+        mine = []
+        for j in range(blocks):
+            x, g, _ = rows_of(pieces[j][d], tok)
+            into = pl.ds(j * tok, tok)
+            mine.append(pltpu.make_async_copy(x, xs.at[d, into], sems.at[d, j, 0]))
+            mine.append(pltpu.make_async_copy(g, gs.at[d, into], sems.at[d, j, 1]))
+        mine.append(pltpu.make_async_copy(win_ref.at[:, column(d)], wi.at[d], wsems.at[d, 0]))
+        mine.append(pltpu.make_async_copy(wout_ref.at[:, column(d)], wo.at[d], wsems.at[d, 1]))
+        copies.append(mine)
+    tables = []
+    for j in range(blocks):
+        table = rows_of(pieces[j][0], tok)[2]
+        tables.append(pltpu.make_async_copy(table, ps.at[j], psems.at[j]))
+        tables[j].start()
+
+    for copy in copies[0] + copies[1]:
+        copy.start()
+    last = (((1,), (1,)), ((), ()))
+    for d in range(n_tp):
+        for copy in copies[d]:
+            copy.wait()
+        for copy in copies[d + 2] if d + 2 < n_tp else ():
+            copy.start()
+        if d == n_tp - 2:
+            added = [pltpu.make_async_copy(base[0], bi, bsems.at[0])]
+            added.append(pltpu.make_async_copy(base[1], bo, bsems.at[1]))
+            for copy in added:
+                copy.start()
+        x = xs[d]
+        g = gs[d] * jnp.asarray(SHRINK, BF16)
+        ab = lax.dot_general(wi[d], x, last, preferred_element_type=F32)
+        h = lax.dot_general(wo[d], g, last, preferred_element_type=F32)
+        if d == 0:
+            acc[pl.ds(0, 2 * ffl)] = ab
+            acc[pl.ds(2 * ffl, ffl)] = h
+        else:
+            acc[pl.ds(0, 2 * ffl)] += ab
+            acc[pl.ds(2 * ffl, ffl)] += h
+    scale = []
+    for j in range(blocks):
+        tables[j].wait()
+        first = weights_row(ps.at[j], where_ref[1], tok)
+        scale.append(first + weights_row(ps.at[j], where_ref[2], tok))
+    scale = jnp.concatenate(scale, axis=1)
+    a = acc[pl.ds(0, ffl)]
+    b = acc[pl.ds(ffl, ffl)]
+    named = scale > 0.0
+    dh = acc[pl.ds(2 * ffl, ffl)] * (scale * (1.0 / SHRINK))
+    sig = jax.nn.sigmoid(a)
+    silu = a * sig
+    da = dh * b * sig * (1.0 + a * (1.0 - sig))
+    dadb_ref[pl.ds(0, ffl)] = jnp.where(named, da, 0.0).astype(BF16)
+    dadb_ref[pl.ds(ffl, ffl)] = jnp.where(named, dh * silu, 0.0).astype(BF16)
+    hid_ref[...] = jnp.where(named, (0.5 * scale) * (silu * b), 0.0).astype(BF16)
+    for copy in added:
+        copy.wait()
+    tile = oi.shape[2]
+    tiles = width // tile
+    leaving = {}
+    for k in range(n_tp * tiles):
+        slot, d, cols = k % 2, k // tiles, pl.ds(k % tiles * tile, tile)
+        start = (where_ref[0] ^ d) * width + k % tiles * tile
+        here = pl.ds(pl.multiple_of(start, tile), tile)
+        for copy in leaving.pop(k - 2, ()):
+            copy.wait()
+        gi = jnp.dot(dadb_ref[...], xs[d, :, cols], preferred_element_type=F32)
+        go = 2.0 * jnp.dot(hid_ref[...], gs[d, :, cols], preferred_element_type=F32)
+        oi[slot] = (gi + bi[:, here].astype(F32)).astype(BF16)
+        oo[slot] = (go + bo[:, here].astype(F32)).astype(BF16)
+        leaving[k] = (
+            pltpu.make_async_copy(oi.at[slot], gin_ref.at[:, here], osems.at[slot, 0]),
+            pltpu.make_async_copy(oo.at[slot], gout_ref.at[:, here], osems.at[slot, 1]),
+        )
+        for copy in leaving[k]:
+            copy.start()
+    for copies in leaving.values():
+        for copy in copies:
+            copy.wait()
+
+
+def far_call(where, pieces, w_in, w_out, tok, base):
+    n_tp = len(pieces[0])
+    flat = [piece for block in pieces for piece in block]
+    sizes = [len(piece) for piece in flat]
+    arrays = [array for piece in flat for array in piece]
+    blocks = len(pieces)
+    rows, width = blocks * tok, arrays[0].shape[1]
+    ffl, depth = w_out.shape
+    tile = min(512, width)
+    hbm = pl.BlockSpec(memory_space=pltpu.HBM)
+    return pl.pallas_call(
+        functools.partial(far_kernel, n_tp, sizes),
+        out_shape=[
+            jax.ShapeDtypeStruct((2 * ffl, depth), BF16),
+            jax.ShapeDtypeStruct((ffl, depth), BF16),
+        ],
+        in_specs=[pl.BlockSpec(memory_space=pltpu.SMEM)] + [hbm] * (4 + len(arrays)),
+        out_specs=[hbm, hbm],
+        scratch_shapes=[
+            pltpu.VMEM((n_tp, rows, width), BF16),
+            pltpu.VMEM((n_tp, rows, width), BF16),
+            pltpu.VMEM((blocks, 16, width), BF16),
+            pltpu.VMEM((n_tp, 2 * ffl, width), BF16),
+            pltpu.VMEM((n_tp, ffl, width), BF16),
+            pltpu.VMEM((3 * ffl, rows), F32),
+            pltpu.VMEM((2 * ffl, rows), BF16),
+            pltpu.VMEM((ffl, rows), BF16),
+            pltpu.VMEM((2 * ffl, depth), BF16),
+            pltpu.VMEM((ffl, depth), BF16),
+            pltpu.VMEM((2, 2 * ffl, tile), BF16),
+            pltpu.VMEM((2, ffl, tile), BF16),
+            pltpu.SemaphoreType.DMA((n_tp, blocks, 2)),
+            pltpu.SemaphoreType.DMA((blocks,)),
+            pltpu.SemaphoreType.DMA((n_tp, 2)),
+            pltpu.SemaphoreType.DMA((2,)),
+            pltpu.SemaphoreType.DMA((2, 2)),
+        ],
+        compiler_params=pltpu.CompilerParams(vmem_limit_bytes=VMEM_LIMIT),
+        cost_estimate=pl.CostEstimate(
+            flops=12 * rows * ffl * depth,
+            bytes_accessed=2 * (9 * ffl + 2 * rows) * depth,
+            transcendentals=rows * ffl,
+        ),
+        name="far",
+    )(where, w_in, w_out, *arrays, *base)
 
 
 def grads_kernel(steps, sizes, added, filled, where_ref, dadb_ref, hid_ref, *refs):
@@ -355,7 +505,8 @@
     done = []
     terms = {}
     other = {frozenset(): (lanes.send(have[frozenset()][2], "t0"),)}
-    for target, bit, part, *first in gather_plan(n_ep, n_tp):
+    plan = gather_plan(n_ep, n_tp)
+    for target, bit, part, *first in plan:
         target = frozenset(target)
         before = []
         for what in first:
@@ -374,20 +525,20 @@
                 for d in range(n_tp)
             ]
         mine = pieces[blocks[0] : blocks[-1] + 1]
-        out = rows_call(half == 0, where, mine, w_in, w_out, tok)
         if half == 0:
-            count = len(blocks) * pairs
-            step = max(1, count // 2)
-            for i in range(0, count, step):
-                come = lanes.send(out[2][1, i : i + step], "t0")
-                total = (out[2][0, i : i + step].astype(F32) + come.astype(F32)).astype(BF16)
-                for k in range(step):
-                    terms[names[(i + k) // pairs][(i + k) % pairs]] = total[k]
+            out = rows_call(True, where, mine, w_in, w_out, tok)
             near = grads_call(where, out[0], out[1], mine, list(range(n_tp)))
             done += [out[1], hop(near[1][:16, :128], "tp", 1)]
-        else:
-            last = out[1]
-            grads = grads_call(where, out[0], out[1], mine, list(range(n_tp)), near)
+
+    kept, leaving = out[2], out[3:]
+    half_way = leaving[0].shape[0]
+    for i, mine in enumerate(leaving):
+        come = hop(mine, "tp", 1)
+        total = kept[i * half_way : (i + 1) * half_way].astype(F32) + come.astype(F32)
+        total = total.astype(BF16)
+        for m in range(half_way):
+            k = i * half_way + m
+            terms[names[k // pairs][k % pairs]] = total[m]
 
     keep = {}
     for e in range(n_ep // 2):
@@ -407,10 +558,10 @@
         for y in range(pairs if e < top else 1):
             if e or y:
                 sums = keep[e, y].astype(BF16)
-                total = total + leap(after(sums, last) if True else sums, e, 2 * y).astype(F32)
+                total = total + leap(sums, e, 2 * y).astype(F32)
     in_grad = total.astype(BF16)
 
-    grad_in, grad_out = grads
+    grad_in, grad_out = far_call(where, pieces[n_ep // 2 :], w_in, w_out, tok, near)
     return in_grad, grad_in.reshape(1, 2, ffl, -1), grad_out[None]
 
 

time: 138 us -> 135 us (0.978)
  waiting for transfers between devices: 44.4 us -> 50.2 us
  Pallas kernels: 49.3 us -> 43.5 us
  local copies, waits for them, and re-layouts: 4.69 us -> 1.48 us
    pallas_call x0 -> x1, Pallas kernels: none -> 18.5 us  [far_call(): pl.pallas_call(functools.partial(far_kernel, n_tp, sizes), out_shape=[jax...]
    pallas_call x2 -> x1, Pallas kernels: 22.9 us -> 10.3 us  [grads_call(): pl.pallas_call(functools.partial(grads_kernel, steps, sizes, len(base) >...]
    pallas_call x2 -> x1, Pallas kernels: 26.4 us -> 14.7 us  [rows_call(): pl.pallas_call(functools.partial(rows_kernel, n_tp, sizes, part), out_sha...]
    ppermute x41 -> x40, waiting for transfers between devices: 44.3 us -> 50.2 us  [hop(): return lax.ppermute(block, axis, [(i, i ^ bit) for i in range(count)])]
    convert_element_type x1, other arithmetic: 0.94 us -> 2.51 us  [body(): total = total.astype(BF16)]
    unnamed x50 -> x48, local copies, waits for them, and re-layouts: 2.68 us -> 1.3 us
    ppermute x41 -> x40, starting transfers between devices: 28.4 us -> 27.9 us  [hop(): return lax.ppermute(block, axis, [(i, i ^ bit) for i in range(count)])]
  transfers between devices with their start and end apart: 45 -> 44, of which waited for: 13 -> 12; matrix products, arithmetic and copies ran while one was open for 3% -> 3% of each run, Pallas kernels for 36% -> 32%
where the time goes in v3:
time: 135 us; the launch traced here: 134 us
  waiting for transfers between devices  50.2 us (37%)
  Pallas kernels  43.5 us (32%)
  starting transfers between devices  32.2 us (24%)
  other arithmetic  6.04 us (4%)
  local copies, waits for them, and re-layouts  1.48 us (1%)
    ppermute x40, waiting for transfers between devices, hop(): return lax.ppermute(block, axis, [(i, i ^ bit) for i in range(count)])  50.2 us
    ppermute x40, starting transfers between devices, hop(): return lax.ppermute(block, axis, [(i, i ^ bit) for i in range(count)])  27.9 us
    pallas_call x1, Pallas kernels, far_call(): pl.pallas_call(functools.partial(far_kernel, n_tp, sizes), out_shape=[jax...  18.5 us
    pallas_call x1, Pallas kernels, rows_call(): pl.pallas_call(functools.partial(rows_kernel, n_tp, sizes, part), out_sha...  14.7 us
    pallas_call x1, Pallas kernels, grads_call(): pl.pallas_call(functools.partial(grads_kernel, steps, sizes, len(base) >...  10.3 us
    ppermute x4, starting transfers between devices, leap(): lax.ppermute(block, ('ep', 'tp'), [(i, i ^ apart) for i in range(count)])  4.33 us
  transfers between devices with their start and end apart: 44, of which 12 were waited for; matrix products, arithmetic and copies ran while one was open for 3% of the time, Pallas kernels for 32%

profile of v3, /device:TPU:0, one launch (start us, length us, event | category | flops | bytes accessed | tf_op | source)
XLA Modules:
  0.0 134.4 jit_solution(17792396535918011240)
XLA Ops:
  2.4 3.0 %collective-permute-start.1 = (bf16[272,1024]{1,0:T(8,128)(2,1)S(1)}, bf16[272,1024]{1,0:T(8,128)(2,1)S(1)}, u32[]{:S(2)}, u32[]{:S(2)}) collective-permute-start(bf16[272,1024]{1,0:T(8,128)(2,1)S(1)} %fusion.1.refs_0_), channel_id=1, source_target_pairs={{0,2},{1,3},{2,0},{3,1},{4,6},{5,7},{6,4},{7,5},{8,10},{9,11},{10,... | collective-permute-start | bytes 1671176 | tf_op jit(solution)/shard_map/ppermute | solution.py:19
  5.5 1.5 %collective-permute-start.3 = (bf16[272,1024]{1,0:T(8,128)(2,1)S(1)}, bf16[272,1024]{1,0:T(8,128)(2,1)S(1)}, u32[]{:S(2)}, u32[]{:S(2)}) collective-permute-start(bf16[272,1024]{1,0:T(8,128)(2,1)S(1)} %fusion.1.refs_0_), channel_id=1, source_target_pairs={{0,4},{4,0},{8,12},{12,8},{16,20},{20,16},{24,28},{28,24},{1,5},{5... | collective-permute-start | bytes 1671176 | tf_op jit(solution)/shard_map/ppermute | solution.py:19
  7.0 1.6 %collective-permute-start.9 = (bf16[272,1024]{1,0:T(8,128)(2,1)S(1)}, bf16[272,1024]{1,0:T(8,128)(2,1)S(1)}, u32[]{:S(2)}, u32[]{:S(2)}) collective-permute-start(bf16[272,1024]{1,0:T(8,128)(2,1)S(1)} %fusion.1.refs_0_), channel_id=1, source_target_pairs={{0,8},{4,12},{8,0},{12,4},{16,24},{20,28},{24,16},{28,20},{1,9},{5... | collective-permute-start | bytes 1671176 | tf_op jit(solution)/shard_map/ppermute | solution.py:19
  8.5 2.6 %collective-permute-start.11 = (bf16[272,1024]{1,0:T(8,128)(2,1)S(1)}, bf16[272,1024]{1,0:T(8,128)(2,1)}, u32[]{:S(2)}, u32[]{:S(2)}) collective-permute-start(bf16[272,1024]{1,0:T(8,128)(2,1)S(1)} %fusion.1.refs_0_), channel_id=1, source_target_pairs={{0,16},{4,20},{8,24},{12,28},{16,0},{20,4},{24,8},{28,12},{1,17},{... | collective-permute-start | bytes 1671176 | tf_op jit(solution)/shard_map/ppermute | solution.py:19
  11.1 7.0 %collective-permute-done.1.refs_2_ = bf16[272,1024]{1,0:T(8,128)(2,1)S(1)} collective-permute-done((bf16[272,1024]{1,0:T(8,128)(2,1)S(1)}, bf16[272,1024]{1,0:T(8,128)(2,1)S(1)}, u32[]{:S(2)}, u32[]{:S(2)}) %collective-permute-start.1) | collective-permute-done | bytes 557088 | tf_op jit(solution)/shard_map/ppermute | solution.py:19
  18.1 1.4 %collective-permute-done.3.refs_4_ = bf16[272,1024]{1,0:T(8,128)(2,1)S(1)} collective-permute-done((bf16[272,1024]{1,0:T(8,128)(2,1)S(1)}, bf16[272,1024]{1,0:T(8,128)(2,1)S(1)}, u32[]{:S(2)}, u32[]{:S(2)}) %collective-permute-start.3) | collective-permute-done | bytes 557088 | tf_op jit(solution)/shard_map/ppermute | solution.py:19
  19.5 1.5 %collective-permute-start.5 = (bf16[128,1024]{1,0:T(8,128)(2,1)S(1)}, bf16[128,1024]{1,0:T(8,128)(2,1)S(1)}, u32[]{:S(2)}, u32[]{:S(2)}) collective-permute-start(bf16[128,1024]{1,0:T(8,128)(2,1)S(1)} %slice.56), channel_id=1, source_target_pairs={{0,4},{4,0},{8,12},{12,8},{16,20},{20,16},{24,28},{28,24},{1,5},{5... | collective-permute-start | bytes 786440 | tf_op jit(solution)/shard_map/ppermute | solution.py:19
  21.6 10.9 %collective-permute-done.9.refs_9_ = bf16[272,1024]{1,0:T(8,128)(2,1)S(1)} collective-permute-done((bf16[272,1024]{1,0:T(8,128)(2,1)S(1)}, bf16[272,1024]{1,0:T(8,128)(2,1)S(1)}, u32[]{:S(2)}, u32[]{:S(2)}) %collective-permute-start.9) | collective-permute-done | bytes 557088 | tf_op jit(solution)/shard_map/ppermute | solution.py:19
  32.6 2.5 %collective-permute-done.11.refs_0_ = bf16[272,1024]{1,0:T(8,128)(2,1)} collective-permute-done((bf16[272,1024]{1,0:T(8,128)(2,1)S(1)}, bf16[272,1024]{1,0:T(8,128)(2,1)}, u32[]{:S(2)}, u32[]{:S(2)}) %collective-permute-start.11) | collective-permute-done | bytes 557088 | tf_op jit(solution)/shard_map/ppermute | solution.py:19
  37.6 10.1 %collective-permute-done.14.refs_13_ = bf16[272,1024]{1,0:T(8,128)(2,1)} collective-permute-done((bf16[272,1024]{1,0:T(8,128)(2,1)S(1)}, bf16[272,1024]{1,0:T(8,128)(2,1)}, u32[]{:S(2)}, u32[]{:S(2)}) %collective-permute-start.14) | collective-permute-done | bytes 557088 | tf_op jit(solution)/shard_map/ppermute | solution.py:19
  47.7 3.1 %collective-permute-done.12.refs_11_ = bf16[272,1024]{1,0:T(8,128)(2,1)} collective-permute-done((bf16[272,1024]{1,0:T(8,128)(2,1)S(1)}, bf16[272,1024]{1,0:T(8,128)(2,1)}, u32[]{:S(2)}, u32[]{:S(2)}) %collective-permute-start.12) | collective-permute-done | bytes 557088 | tf_op jit(solution)/shard_map/ppermute | solution.py:19
  52.8 1.4 %collective-permute-start.28 = (bf16[272,1024]{1,0:T(8,128)(2,1)}, bf16[272,1024]{1,0:T(8,128)(2,1)}, u32[]{:S(2)}, u32[]{:S(2)}) collective-permute-start(bf16[272,1024]{1,0:T(8,128)(2,1)} %collective-permute-done.11.refs_0_), channel_id=1, source_target_pairs={{0,2},{1,3},{2,0},{3,1},{4,6},{5,7},{6,4},{7,5},{8,10},{9,11},{10,... | collective-permute-start | bytes 1671176 | tf_op jit(solution)/shard_map/ppermute | solution.py:19
  54.2 1.5 %collective-permute-start.30 = (bf16[272,1024]{1,0:T(8,128)(2,1)}, bf16[272,1024]{1,0:T(8,128)(2,1)}, u32[]{:S(2)}, u32[]{:S(2)}) collective-permute-start(bf16[272,1024]{1,0:T(8,128)(2,1)} %collective-permute-done.11.refs_0_), channel_id=1, source_target_pairs={{0,4},{4,0},{8,12},{12,8},{16,20},{20,16},{24,28},{28,24},{1,5},{5... | collective-permute-start | bytes 1671176 | tf_op jit(solution)/shard_map/ppermute | solution.py:19
  56.2 14.7 %rows.1 = (bf16[768,512]{1,0:T(8,128)(2,1)}, bf16[384,512]{1,0:T(8,128)(2,1)}, bf16[8,128,1024]{2,1,0:T(8,128)(2,1)}, bf16[4,128,1024]{2,1,0:T(8,128)(2,1)}, bf16[4,128,1024]{2,1,0:T(8,128)(2,1)}) custom-call(s32[3]{0:T(128)} %pad_add_fusion.where_ref, bf16[768,4096]{1,0:T(8,128)(2,1)} %bitcast.39, bf16[384,4096]{1,0:T(8,128)(2,1)} %bitcast.41, ...), custom_call_target="tpu_custom_call" | custom-call | flops 8053063680 | bytes 17825792 | tf_op jit(solution)/shard_map/rows/pallas_call | solution.py:194
  72.9 1.6 %collective-permute-start.38 = (bf16[272,1024]{1,0:T(8,128)(2,1)}, bf16[272,1024]{1,0:T(8,128)(2,1)S(1)}, u32[]{:S(2)}, u32[]{:S(2)}) collective-permute-start(bf16[272,1024]{1,0:T(8,128)(2,1)} %collective-permute-done.30.refs_4_), channel_id=1, source_target_pairs={{0,8},{4,12},{8,0},{12,4},{16,24},{20,28},{24,16},{28,20},{1,9},{5... | collective-permute-start | bytes 1671176 | tf_op jit(solution)/shard_map/ppermute | solution.py:19
  74.5 11.8 %collective-permute-done.36.refs_10_ = bf16[272,1024]{1,0:T(8,128)(2,1)S(1)} collective-permute-done((bf16[272,1024]{1,0:T(8,128)(2,1)}, bf16[272,1024]{1,0:T(8,128)(2,1)S(1)}, u32[]{:S(2)}, u32[]{:S(2)}) %collective-permute-start.36) | collective-permute-done | bytes 557088 | tf_op jit(solution)/shard_map/ppermute | solution.py:19
  87.8 1.5 %collective-permute-start.40 = (bf16[128,1024]{1,0:T(8,128)(2,1)S(1)}, bf16[128,1024]{1,0:T(8,128)(2,1)}, u32[]{:S(2)}, u32[]{:S(2)}) collective-permute-start(bf16[128,1024]{1,0:T(8,128)(2,1)S(1)} %slice.66), channel_id=1, source_target_pairs={{0,4},{4,0},{8,12},{12,8},{16,20},{20,16},{24,28},{28,24},{1,5},{5... | collective-permute-start | bytes 786440 | tf_op jit(solution)/shard_map/ppermute | solution.py:19
  89.3 2.5 %add_convert_fusion.1 = (bf16[4,128,1024]{2,1,0:T(8,128)(2,1)S(1)}, bf16[4,128,1024]{2,1,0:T(8,128)(2,1)S(1)}) fusion(bf16[4,128,1024]{2,1,0:T(8,128)(2,1)S(1)} %collective-permute-done.18, bf16[8,128,1024]{2,1,0:T(8,128)(2,1)} %get-tuple-element.30, bf16[4,128,1024]{2,1,0:T(8,128)(2,1)S(1)} %collective-permute-done.21), kind=kLoop, calls=%fused_computation.1 | loop fusion | flops 4194304 | bytes 6291456 | tf_op jit(solution)/shard_map/convert_element_type | solution.py:538
  91.9 1.2 collective-permute-start.41
  94.6 1.6 %collective-permute-start.22 = (bf16[128,1024]{1,0:T(8,128)(2,1)S(1)}, bf16[128,1024]{1,0:T(8,128)(2,1)S(1)}, u32[]{:S(2)}, u32[]{:S(2)}) collective-permute-start(bf16[128,1024]{1,0:T(8,128)(2,1)S(1)} %get-tuple-element.51), channel_id=1, source_target_pairs={{0,8},{4,12},{8,0},{12,4},{16,24},{20,28},{24,16},{28,20},{1,9},{5... | collective-permute-start | bytes 786440 | tf_op jit(solution)/shard_map/ppermute | solution.py:19
  96.1 10.3 %grads.1 = (bf16[768,4096]{1,0:T(8,128)(2,1)}, bf16[384,4096]{1,0:T(8,128)(2,1)}) custom-call(s32[3]{0:T(128)} %pad_add_fusion.where_ref, bf16[768,512]{1,0:T(8,128)(2,1)} %get-tuple-element.42.dadb_ref, bf16[384,512]{1,0:T(8,128)(2,1)} %get-tuple-element.36.hid_ref, bf16[272,1024]{1,0:T(8,128)(2,1)} %copy-done, bf16[272,1024]{1,0:T(8,128)(2,1)} %copy-done.7, ...), custom_call_target="tpu_custom_call" | custom-call | flops 4831838208 | bytes 17825792 | tf_op jit(solution)/shard_map/grads/pallas_call | solution.py:435
  108.0 1.8 %collective-permute-done.42.refs_16_ = bf16[128,1024]{1,0:T(8,128)(2,1)S(1)} collective-permute-done((bf16[128,1024]{1,0:T(8,128)(2,1)}, bf16[128,1024]{1,0:T(8,128)(2,1)S(1)}, u32[]{:S(2)}, u32[]{:S(2)}) %collective-permute-start.42) | collective-permute-done | bytes 262176 | tf_op jit(solution)/shard_map/ppermute | solution.py:19
  109.9 1.5 %collective-permute-start.20 = (bf16[128,1024]{1,0:T(8,128)(2,1)S(1)}, bf16[128,1024]{1,0:T(8,128)(2,1)S(1)}, u32[]{:S(2)}, u32[]{:S(2)}) collective-permute-start(bf16[128,1024]{1,0:T(8,128)(2,1)S(1)} %get-tuple-element.50), channel_id=1, source_target_pairs={{0,4},{1,5},{2,6},{3,7},{4,0},{5,1},{6,2},{7,3},{8,12},{9,13},{10,... | collective-permute-start | bytes 786440 | tf_op jit(solution)/shard_map/ppermute | solution.py:25
  115.0 18.5 %far.1 = (bf16[768,4096]{1,0:T(8,128)(2,1)}, bf16[384,4096]{1,0:T(8,128)(2,1)}) custom-call(s32[3]{0:T(128)} %pad_add_fusion.where_ref, bf16[768,4096]{1,0:T(8,128)(2,1)} %bitcast.40, bf16[384,4096]{1,0:T(8,128)(2,1)} %bitcast.42, bf16[272,1024]{1,0:T(8,128)(2,1)} %collective-permute-done.11.refs_0_, bf16[272,1024]{1,0:T(8,128)(2,1)} %copy-done.11, ...), custom_call_target="tpu_custom_call" | custom-call | flops 9663676416 | bytes 36700160 | tf_op jit(solution)/shard_map/far/pallas_call | solution.py:328
  (129 shorter events, 18.5 us)
Async XLA Ops:
  2.4 15.7 %collective-permute-start.1 = (bf16[272,1024]{1,0:T(8,128)(2,1)S(1)}, bf16[272,1024]{1,0:T(8,128)(2,1)S(1)}, u32[]{:S(2)}, u32[]{:S(2)}) collective-permute-start(bf16[272,1024]{1,0:T(8,128)(2,1)S(1)} %fusion.1.refs_0_), channel_id=1, source_target_pairs={{0,2},{1,3},{2,0},{3,1},{4,6},{5,7},{6,4},{7,5},{8,10},{9,11},{10,... | collective-permute-start | bytes 1671176 | tf_op jit(solution)/shard_map/ppermute | solution.py:19
  7.0 25.6 %collective-permute-start.9 = (bf16[272,1024]{1,0:T(8,128)(2,1)S(1)}, bf16[272,1024]{1,0:T(8,128)(2,1)S(1)}, u32[]{:S(2)}, u32[]{:S(2)}) collective-permute-start(bf16[272,1024]{1,0:T(8,128)(2,1)S(1)} %fusion.1.refs_0_), channel_id=1, source_target_pairs={{0,8},{4,12},{8,0},{12,4},{16,24},{20,28},{24,16},{28,20},{1,9},{5... | collective-permute-start | bytes 1671176 | tf_op jit(solution)/shard_map/ppermute | solution.py:19
  8.5 26.5 %collective-permute-start.11 = (bf16[272,1024]{1,0:T(8,128)(2,1)S(1)}, bf16[272,1024]{1,0:T(8,128)(2,1)}, u32[]{:S(2)}, u32[]{:S(2)}) collective-permute-start(bf16[272,1024]{1,0:T(8,128)(2,1)S(1)} %fusion.1.refs_0_), channel_id=1, source_target_pairs={{0,16},{4,20},{8,24},{12,28},{16,0},{20,4},{24,8},{28,12},{1,17},{... | collective-permute-start | bytes 1671176 | tf_op jit(solution)/shard_map/ppermute | solution.py:19
  11.1 25.1 %collective-permute-start = (bf16[272,1024]{1,0:T(8,128)(2,1)S(1)}, bf16[272,1024]{1,0:T(8,128)(2,1)S(1)}, u32[]{:S(2)}, u32[]{:S(2)}) collective-permute-start(bf16[272,1024]{1,0:T(8,128)(2,1)S(1)} %fusion.1.refs_0_), channel_id=1, source_target_pairs={{0,1},{1,0},{2,3},{3,2},{4,5},{5,4},{6,7},{7,6},{8,9},{9,8},{10,11... | collective-permute-start | bytes 1671176 | tf_op jit(solution)/shard_map/ppermute | solution.py:19
  19.5 15.5 %collective-permute-start.5 = (bf16[128,1024]{1,0:T(8,128)(2,1)S(1)}, bf16[128,1024]{1,0:T(8,128)(2,1)S(1)}, u32[]{:S(2)}, u32[]{:S(2)}) collective-permute-start(bf16[128,1024]{1,0:T(8,128)(2,1)S(1)} %slice.56), channel_id=1, source_target_pairs={{0,4},{4,0},{8,12},{12,8},{16,20},{20,16},{24,28},{28,24},{1,5},{5... | collective-permute-start | bytes 786440 | tf_op jit(solution)/shard_map/ppermute | solution.py:19
  21.1 14.5 %collective-permute-start.6 = (bf16[144,1024]{1,0:T(8,128)(2,1)S(1)}, bf16[144,1024]{1,0:T(8,128)(2,1)S(1)}, u32[]{:S(2)}, u32[]{:S(2)}) collective-permute-start(bf16[144,1024]{1,0:T(8,128)(2,1)S(1)} %slice.57), channel_id=1, source_target_pairs={{0,2},{1,3},{2,0},{3,1},{4,6},{5,7},{6,4},{7,5},{8,10},{9,11},{10,... | collective-permute-start | bytes 884744 | tf_op jit(solution)/shard_map/ppermute | solution.py:19
  35.6 15.2 %collective-permute-start.12 = (bf16[272,1024]{1,0:T(8,128)(2,1)S(1)}, bf16[272,1024]{1,0:T(8,128)(2,1)}, u32[]{:S(2)}, u32[]{:S(2)}) collective-permute-start(bf16[272,1024]{1,0:T(8,128)(2,1)S(1)} %collective-permute-done.9.refs_9_), channel_id=1, source_target_pairs={{0,2},{1,3},{2,0},{3,1},{4,6},{5,7},{6,4},{7,5},{8,10},{9,11},{10,... | collective-permute-start | bytes 1671176 | tf_op jit(solution)/shard_map/ppermute | solution.py:19
  36.2 14.9 %collective-permute-start.16 = (bf16[272,1024]{1,0:T(8,128)(2,1)S(1)}, bf16[272,1024]{1,0:T(8,128)(2,1)}, u32[]{:S(2)}, u32[]{:S(2)}) collective-permute-start(bf16[272,1024]{1,0:T(8,128)(2,1)S(1)} %constant_dynamic-update-slice_fusion.refs_6_), channel_id=1, source_target_pairs={{0,8},{4,12},{8,0},{12,4},{16,24},{20,28},{24,16},{28,20},{1,9},{5... | collective-permute-start | bytes 1671176 | tf_op jit(solution)/shard_map/ppermute | solution.py:19
  37.1 14.2 %collective-permute-start.4 = (bf16[272,1024]{1,0:T(8,128)(2,1)S(1)}, bf16[272,1024]{1,0:T(8,128)(2,1)S(1)}, u32[]{:S(2)}, u32[]{:S(2)}) collective-permute-start(bf16[272,1024]{1,0:T(8,128)(2,1)S(1)} %collective-permute-done.3.refs_4_), channel_id=1, source_target_pairs={{0,1},{1,0},{2,3},{3,2},{4,5},{5,4},{6,7},{7,6},{8,9},{9,8},{10,11... | collective-permute-start | bytes 1671176 | tf_op jit(solution)/shard_map/ppermute | solution.py:19
  37.3 15.6 %collective-permute-start.10 = (bf16[272,1024]{1,0:T(8,128)(2,1)S(1)}, bf16[272,1024]{1,0:T(8,128)(2,1)}, u32[]{:S(2)}, u32[]{:S(2)}) collective-permute-start(bf16[272,1024]{1,0:T(8,128)(2,1)S(1)} %collective-permute-done.9.refs_9_), channel_id=1, source_target_pairs={{0,1},{1,0},{2,3},{3,2},{4,5},{5,4},{6,7},{7,6},{8,9},{9,8},{10,11... | collective-permute-start | bytes 1671176 | tf_op jit(solution)/shard_map/ppermute | solution.py:19
  52.8 18.6 %collective-permute-start.28 = (bf16[272,1024]{1,0:T(8,128)(2,1)}, bf16[272,1024]{1,0:T(8,128)(2,1)}, u32[]{:S(2)}, u32[]{:S(2)}) collective-permute-start(bf16[272,1024]{1,0:T(8,128)(2,1)} %collective-permute-done.11.refs_0_), channel_id=1, source_target_pairs={{0,2},{1,3},{2,0},{3,1},{4,6},{5,7},{6,4},{7,5},{8,10},{9,11},{10,... | collective-permute-start | bytes 1671176 | tf_op jit(solution)/shard_map/ppermute | solution.py:19
  54.2 17.3 %collective-permute-start.30 = (bf16[272,1024]{1,0:T(8,128)(2,1)}, bf16[272,1024]{1,0:T(8,128)(2,1)}, u32[]{:S(2)}, u32[]{:S(2)}) collective-permute-start(bf16[272,1024]{1,0:T(8,128)(2,1)} %collective-permute-done.11.refs_0_), channel_id=1, source_target_pairs={{0,4},{4,0},{8,12},{12,8},{16,20},{20,16},{24,28},{28,24},{1,5},{5... | collective-permute-start | bytes 1671176 | tf_op jit(solution)/shard_map/ppermute | solution.py:19
  55.7 15.8 %collective-permute-start.32 = (bf16[272,1024]{1,0:T(8,128)(2,1)}, bf16[272,1024]{1,0:T(8,128)(2,1)}, u32[]{:S(2)}, u32[]{:S(2)}) collective-permute-start(bf16[272,1024]{1,0:T(8,128)(2,1)} %collective-permute-done.11.refs_0_), channel_id=1, source_target_pairs={{0,8},{4,12},{8,0},{12,4},{16,24},{20,28},{24,16},{28,20},{1,9},{5... | collective-permute-start | bytes 1671176 | tf_op jit(solution)/shard_map/ppermute | solution.py:19
  70.9 16.6 %collective-permute-start.18 = (bf16[4,128,1024]{2,1,0:T(8,128)(2,1)}, bf16[4,128,1024]{2,1,0:T(8,128)(2,1)S(1)}, u32[]{:S(2)}, u32[]{:S(2)}) collective-permute-start(bf16[4,128,1024]{2,1,0:T(8,128)(2,1)} %get-tuple-element.31), channel_id=1, source_target_pairs={{0,1},{1,0},{2,3},{3,2},{4,5},{5,4},{6,7},{7,6},{8,9},{9,8},{10,11... | collective-permute-start | bytes 3145736 | tf_op jit(solution)/shard_map/ppermute | solution.py:19
  71.0 16.9 %collective-permute-start.21 = (bf16[4,128,1024]{2,1,0:T(8,128)(2,1)}, bf16[4,128,1024]{2,1,0:T(8,128)(2,1)S(1)}, u32[]{:S(2)}, u32[]{:S(2)}) collective-permute-start(bf16[4,128,1024]{2,1,0:T(8,128)(2,1)} %get-tuple-element.32), channel_id=1, source_target_pairs={{0,1},{1,0},{2,3},{3,2},{4,5},{5,4},{6,7},{7,6},{8,9},{9,8},{10,11... | collective-permute-start | bytes 3145736 | tf_op jit(solution)/shard_map/ppermute | solution.py:19
  71.5 14.9 %collective-permute-start.36 = (bf16[272,1024]{1,0:T(8,128)(2,1)}, bf16[272,1024]{1,0:T(8,128)(2,1)S(1)}, u32[]{:S(2)}, u32[]{:S(2)}) collective-permute-start(bf16[272,1024]{1,0:T(8,128)(2,1)} %collective-permute-done.32.refs_8_), channel_id=1, source_target_pairs={{0,2},{1,3},{2,0},{3,1},{4,6},{5,7},{6,4},{7,5},{8,10},{9,11},{10,... | collective-permute-start | bytes 1671176 | tf_op jit(solution)/shard_map/ppermute | solution.py:19
  72.4 14.5 %collective-permute-start.33 = (bf16[272,1024]{1,0:T(8,128)(2,1)}, bf16[272,1024]{1,0:T(8,128)(2,1)S(1)}, u32[]{:S(2)}, u32[]{:S(2)}) collective-permute-start(bf16[272,1024]{1,0:T(8,128)(2,1)} %collective-permute-done.28.refs_2_), channel_id=1, source_target_pairs={{0,4},{4,0},{8,12},{12,8},{16,20},{20,16},{24,28},{28,24},{1,5},{5... | collective-permute-start | bytes 1671176 | tf_op jit(solution)/shard_map/ppermute | solution.py:19
  72.9 14.3 %collective-permute-start.38 = (bf16[272,1024]{1,0:T(8,128)(2,1)}, bf16[272,1024]{1,0:T(8,128)(2,1)S(1)}, u32[]{:S(2)}, u32[]{:S(2)}) collective-permute-start(bf16[272,1024]{1,0:T(8,128)(2,1)} %collective-permute-done.30.refs_4_), channel_id=1, source_target_pairs={{0,8},{4,12},{8,0},{12,4},{16,24},{20,28},{24,16},{28,20},{1,9},{5... | collective-permute-start | bytes 1671176 | tf_op jit(solution)/shard_map/ppermute | solution.py:19
  87.8 18.6 %collective-permute-start.40 = (bf16[128,1024]{1,0:T(8,128)(2,1)S(1)}, bf16[128,1024]{1,0:T(8,128)(2,1)}, u32[]{:S(2)}, u32[]{:S(2)}) collective-permute-start(bf16[128,1024]{1,0:T(8,128)(2,1)S(1)} %slice.66), channel_id=1, source_target_pairs={{0,4},{4,0},{8,12},{12,8},{16,20},{20,16},{24,28},{28,24},{1,5},{5... | collective-permute-start | bytes 786440 | tf_op jit(solution)/shard_map/ppermute | solution.py:19
  91.9 14.7 %collective-permute-start.41 = (bf16[144,1024]{1,0:T(8,128)(2,1)S(1)}, bf16[144,1024]{1,0:T(8,128)(2,1)S(1)}, u32[]{:S(2)}, u32[]{:S(2)}) collective-permute-start(bf16[144,1024]{1,0:T(8,128)(2,1)S(1)} %slice.67), channel_id=1, source_target_pairs={{0,2},{1,3},{2,0},{3,1},{4,6},{5,7},{6,4},{7,5},{8,10},{9,11},{10,... | collective-permute-start | bytes 884744 | tf_op jit(solution)/shard_map/ppermute | solution.py:19
  109.9 23.6 %collective-permute-start.20 = (bf16[128,1024]{1,0:T(8,128)(2,1)S(1)}, bf16[128,1024]{1,0:T(8,128)(2,1)S(1)}, u32[]{:S(2)}, u32[]{:S(2)}) collective-permute-start(bf16[128,1024]{1,0:T(8,128)(2,1)S(1)} %get-tuple-element.50), channel_id=1, source_target_pairs={{0,4},{1,5},{2,6},{3,7},{4,0},{5,1},{6,2},{7,3},{8,12},{9,13},{10,... | collective-permute-start | bytes 786440 | tf_op jit(solution)/shard_map/ppermute | solution.py:25
  111.4 22.1 %collective-permute-start.19 = (bf16[128,1024]{1,0:T(8,128)(2,1)S(1)}, bf16[128,1024]{1,0:T(8,128)(2,1)S(1)}, u32[]{:S(2)}, u32[]{:S(2)}) collective-permute-start(bf16[128,1024]{1,0:T(8,128)(2,1)S(1)} %get-tuple-element.49), channel_id=1, source_target_pairs={{0,2},{1,3},{2,0},{3,1},{4,6},{5,7},{6,4},{7,5},{8,10},{9,11},{10,... | collective-permute-start | bytes 786440 | tf_op jit(solution)/shard_map/ppermute | solution.py:25
  112.5 21.0 %collective-permute-start.26 = (bf16[128,1024]{1,0:T(8,128)(2,1)S(1)}, bf16[128,1024]{1,0:T(8,128)(2,1)S(1)}, u32[]{:S(2)}, u32[]{:S(2)}) collective-permute-start(bf16[128,1024]{1,0:T(8,128)(2,1)S(1)} %fusion.3), channel_id=1, source_target_pairs={{0,8},{1,9},{2,10},{3,11},{4,12},{5,13},{6,14},{7,15},{8,0},{9,1},... | collective-permute-start | bytes 786440 | tf_op jit(solution)/shard_map/ppermute | solution.py:25
  113.4 20.1 %collective-permute-start.23 = (bf16[128,1024]{1,0:T(8,128)(2,1)S(1)}, bf16[128,1024]{1,0:T(8,128)(2,1)S(1)}, u32[]{:S(2)}, u32[]{:S(2)}) collective-permute-start(bf16[128,1024]{1,0:T(8,128)(2,1)S(1)} %fusion.4), channel_id=1, source_target_pairs={{0,6},{1,7},{2,4},{3,5},{4,2},{5,3},{6,0},{7,1},{8,14},{9,15},{10,... | collective-permute-start | bytes 786440 | tf_op jit(solution)/shard_map/ppermute | solution.py:25
  (43 other events, 453.3 us)

commit v4 on v3

--- a/solution.py
+++ b/solution.py
@@ -323,7 +323,7 @@
     blocks = len(pieces)
     rows, width = blocks * tok, arrays[0].shape[1]
     ffl, depth = w_out.shape
-    tile = min(512, width)
+    tile = width
     hbm = pl.BlockSpec(memory_space=pltpu.HBM)
     return pl.pallas_call(
         functools.partial(far_kernel, n_tp, sizes),

time: 135 us -> 134 us (level)
  no operation moved by 1% of the time
where the time goes in v4:
time: 134 us; the launch traced here: 133 us
  waiting for transfers between devices  50.2 us (37%)
  Pallas kernels  42.5 us (32%)
  starting transfers between devices  32.2 us (24%)
  other arithmetic  6.04 us (5%)
  local copies, waits for them, and re-layouts  1.48 us (1%)
    ppermute x40, waiting for transfers between devices, hop(): return lax.ppermute(block, axis, [(i, i ^ bit) for i in range(count)])  50.2 us
    ppermute x40, starting transfers between devices, hop(): return lax.ppermute(block, axis, [(i, i ^ bit) for i in range(count)])  27.9 us
    pallas_call x1, Pallas kernels, far_call(): pl.pallas_call(functools.partial(far_kernel, n_tp, sizes), out_shape=[jax...  17.5 us
    pallas_call x1, Pallas kernels, rows_call(): pl.pallas_call(functools.partial(rows_kernel, n_tp, sizes, part), out_sha...  14.7 us
    pallas_call x1, Pallas kernels, grads_call(): pl.pallas_call(functools.partial(grads_kernel, steps, sizes, len(base) >...  10.3 us
    ppermute x4, starting transfers between devices, leap(): lax.ppermute(block, ('ep', 'tp'), [(i, i ^ apart) for i in range(count)])  4.33 us
  transfers between devices with their start and end apart: 44, of which 12 were waited for; matrix products, arithmetic and copies ran while one was open for 3% of the time, Pallas kernels for 32%

profile of v4, /device:TPU:0, one launch (start us, length us, event | category | flops | bytes accessed | tf_op | source)
XLA Modules:
  0.0 133.5 jit_solution(5364468626218598376)
XLA Ops:
  2.4 3.0 %collective-permute-start.1 = (bf16[272,1024]{1,0:T(8,128)(2,1)S(1)}, bf16[272,1024]{1,0:T(8,128)(2,1)S(1)}, u32[]{:S(2)}, u32[]{:S(2)}) collective-permute-start(bf16[272,1024]{1,0:T(8,128)(2,1)S(1)} %fusion.1.refs_0_), channel_id=1, source_target_pairs={{0,2},{1,3},{2,0},{3,1},{4,6},{5,7},{6,4},{7,5},{8,10},{9,11},{10,... | collective-permute-start | bytes 1671176 | tf_op jit(solution)/shard_map/ppermute | solution.py:19
  5.5 1.5 %collective-permute-start.3 = (bf16[272,1024]{1,0:T(8,128)(2,1)S(1)}, bf16[272,1024]{1,0:T(8,128)(2,1)S(1)}, u32[]{:S(2)}, u32[]{:S(2)}) collective-permute-start(bf16[272,1024]{1,0:T(8,128)(2,1)S(1)} %fusion.1.refs_0_), channel_id=1, source_target_pairs={{0,4},{4,0},{8,12},{12,8},{16,20},{20,16},{24,28},{28,24},{1,5},{5... | collective-permute-start | bytes 1671176 | tf_op jit(solution)/shard_map/ppermute | solution.py:19
  7.0 1.6 %collective-permute-start.9 = (bf16[272,1024]{1,0:T(8,128)(2,1)S(1)}, bf16[272,1024]{1,0:T(8,128)(2,1)S(1)}, u32[]{:S(2)}, u32[]{:S(2)}) collective-permute-start(bf16[272,1024]{1,0:T(8,128)(2,1)S(1)} %fusion.1.refs_0_), channel_id=1, source_target_pairs={{0,8},{4,12},{8,0},{12,4},{16,24},{20,28},{24,16},{28,20},{1,9},{5... | collective-permute-start | bytes 1671176 | tf_op jit(solution)/shard_map/ppermute | solution.py:19
  8.5 2.6 %collective-permute-start.11 = (bf16[272,1024]{1,0:T(8,128)(2,1)S(1)}, bf16[272,1024]{1,0:T(8,128)(2,1)}, u32[]{:S(2)}, u32[]{:S(2)}) collective-permute-start(bf16[272,1024]{1,0:T(8,128)(2,1)S(1)} %fusion.1.refs_0_), channel_id=1, source_target_pairs={{0,16},{4,20},{8,24},{12,28},{16,0},{20,4},{24,8},{28,12},{1,17},{... | collective-permute-start | bytes 1671176 | tf_op jit(solution)/shard_map/ppermute | solution.py:19
  11.1 7.0 %collective-permute-done.1.refs_2_ = bf16[272,1024]{1,0:T(8,128)(2,1)S(1)} collective-permute-done((bf16[272,1024]{1,0:T(8,128)(2,1)S(1)}, bf16[272,1024]{1,0:T(8,128)(2,1)S(1)}, u32[]{:S(2)}, u32[]{:S(2)}) %collective-permute-start.1) | collective-permute-done | bytes 557088 | tf_op jit(solution)/shard_map/ppermute | solution.py:19
  18.1 1.4 %collective-permute-done.3.refs_4_ = bf16[272,1024]{1,0:T(8,128)(2,1)S(1)} collective-permute-done((bf16[272,1024]{1,0:T(8,128)(2,1)S(1)}, bf16[272,1024]{1,0:T(8,128)(2,1)S(1)}, u32[]{:S(2)}, u32[]{:S(2)}) %collective-permute-start.3) | collective-permute-done | bytes 557088 | tf_op jit(solution)/shard_map/ppermute | solution.py:19
  19.5 1.5 %collective-permute-start.5 = (bf16[128,1024]{1,0:T(8,128)(2,1)S(1)}, bf16[128,1024]{1,0:T(8,128)(2,1)S(1)}, u32[]{:S(2)}, u32[]{:S(2)}) collective-permute-start(bf16[128,1024]{1,0:T(8,128)(2,1)S(1)} %slice.56), channel_id=1, source_target_pairs={{0,4},{4,0},{8,12},{12,8},{16,20},{20,16},{24,28},{28,24},{1,5},{5... | collective-permute-start | bytes 786440 | tf_op jit(solution)/shard_map/ppermute | solution.py:19
  21.6 10.9 %collective-permute-done.9.refs_9_ = bf16[272,1024]{1,0:T(8,128)(2,1)S(1)} collective-permute-done((bf16[272,1024]{1,0:T(8,128)(2,1)S(1)}, bf16[272,1024]{1,0:T(8,128)(2,1)S(1)}, u32[]{:S(2)}, u32[]{:S(2)}) %collective-permute-start.9) | collective-permute-done | bytes 557088 | tf_op jit(solution)/shard_map/ppermute | solution.py:19
  32.6 2.5 %collective-permute-done.11.refs_0_ = bf16[272,1024]{1,0:T(8,128)(2,1)} collective-permute-done((bf16[272,1024]{1,0:T(8,128)(2,1)S(1)}, bf16[272,1024]{1,0:T(8,128)(2,1)}, u32[]{:S(2)}, u32[]{:S(2)}) %collective-permute-start.11) | collective-permute-done | bytes 557088 | tf_op jit(solution)/shard_map/ppermute | solution.py:19
  37.6 10.1 %collective-permute-done.14.refs_13_ = bf16[272,1024]{1,0:T(8,128)(2,1)} collective-permute-done((bf16[272,1024]{1,0:T(8,128)(2,1)S(1)}, bf16[272,1024]{1,0:T(8,128)(2,1)}, u32[]{:S(2)}, u32[]{:S(2)}) %collective-permute-start.14) | collective-permute-done | bytes 557088 | tf_op jit(solution)/shard_map/ppermute | solution.py:19
  47.7 3.1 %collective-permute-done.12.refs_11_ = bf16[272,1024]{1,0:T(8,128)(2,1)} collective-permute-done((bf16[272,1024]{1,0:T(8,128)(2,1)S(1)}, bf16[272,1024]{1,0:T(8,128)(2,1)}, u32[]{:S(2)}, u32[]{:S(2)}) %collective-permute-start.12) | collective-permute-done | bytes 557088 | tf_op jit(solution)/shard_map/ppermute | solution.py:19
  52.8 1.4 %collective-permute-start.28 = (bf16[272,1024]{1,0:T(8,128)(2,1)}, bf16[272,1024]{1,0:T(8,128)(2,1)}, u32[]{:S(2)}, u32[]{:S(2)}) collective-permute-start(bf16[272,1024]{1,0:T(8,128)(2,1)} %collective-permute-done.11.refs_0_), channel_id=1, source_target_pairs={{0,2},{1,3},{2,0},{3,1},{4,6},{5,7},{6,4},{7,5},{8,10},{9,11},{10,... | collective-permute-start | bytes 1671176 | tf_op jit(solution)/shard_map/ppermute | solution.py:19
  54.2 1.5 %collective-permute-start.30 = (bf16[272,1024]{1,0:T(8,128)(2,1)}, bf16[272,1024]{1,0:T(8,128)(2,1)}, u32[]{:S(2)}, u32[]{:S(2)}) collective-permute-start(bf16[272,1024]{1,0:T(8,128)(2,1)} %collective-permute-done.11.refs_0_), channel_id=1, source_target_pairs={{0,4},{4,0},{8,12},{12,8},{16,20},{20,16},{24,28},{28,24},{1,5},{5... | collective-permute-start | bytes 1671176 | tf_op jit(solution)/shard_map/ppermute | solution.py:19
  56.2 14.7 %rows.1 = (bf16[768,512]{1,0:T(8,128)(2,1)}, bf16[384,512]{1,0:T(8,128)(2,1)}, bf16[8,128,1024]{2,1,0:T(8,128)(2,1)}, bf16[4,128,1024]{2,1,0:T(8,128)(2,1)}, bf16[4,128,1024]{2,1,0:T(8,128)(2,1)}) custom-call(s32[3]{0:T(128)} %pad_add_fusion.where_ref, bf16[768,4096]{1,0:T(8,128)(2,1)} %bitcast.39, bf16[384,4096]{1,0:T(8,128)(2,1)} %bitcast.41, ...), custom_call_target="tpu_custom_call" | custom-call | flops 8053063680 | bytes 17825792 | tf_op jit(solution)/shard_map/rows/pallas_call | solution.py:194
  72.9 1.6 %collective-permute-start.38 = (bf16[272,1024]{1,0:T(8,128)(2,1)}, bf16[272,1024]{1,0:T(8,128)(2,1)S(1)}, u32[]{:S(2)}, u32[]{:S(2)}) collective-permute-start(bf16[272,1024]{1,0:T(8,128)(2,1)} %collective-permute-done.30.refs_4_), channel_id=1, source_target_pairs={{0,8},{4,12},{8,0},{12,4},{16,24},{20,28},{24,16},{28,20},{1,9},{5... | collective-permute-start | bytes 1671176 | tf_op jit(solution)/shard_map/ppermute | solution.py:19
  74.5 11.8 %collective-permute-done.36.refs_10_ = bf16[272,1024]{1,0:T(8,128)(2,1)S(1)} collective-permute-done((bf16[272,1024]{1,0:T(8,128)(2,1)}, bf16[272,1024]{1,0:T(8,128)(2,1)S(1)}, u32[]{:S(2)}, u32[]{:S(2)}) %collective-permute-start.36) | collective-permute-done | bytes 557088 | tf_op jit(solution)/shard_map/ppermute | solution.py:19
  87.8 1.5 %collective-permute-start.40 = (bf16[128,1024]{1,0:T(8,128)(2,1)S(1)}, bf16[128,1024]{1,0:T(8,128)(2,1)}, u32[]{:S(2)}, u32[]{:S(2)}) collective-permute-start(bf16[128,1024]{1,0:T(8,128)(2,1)S(1)} %slice.66), channel_id=1, source_target_pairs={{0,4},{4,0},{8,12},{12,8},{16,20},{20,16},{24,28},{28,24},{1,5},{5... | collective-permute-start | bytes 786440 | tf_op jit(solution)/shard_map/ppermute | solution.py:19
  89.3 2.5 %add_convert_fusion.1 = (bf16[4,128,1024]{2,1,0:T(8,128)(2,1)S(1)}, bf16[4,128,1024]{2,1,0:T(8,128)(2,1)S(1)}) fusion(bf16[4,128,1024]{2,1,0:T(8,128)(2,1)S(1)} %collective-permute-done.18, bf16[8,128,1024]{2,1,0:T(8,128)(2,1)} %get-tuple-element.30, bf16[4,128,1024]{2,1,0:T(8,128)(2,1)S(1)} %collective-permute-done.21), kind=kLoop, calls=%fused_computation.1 | loop fusion | flops 4194304 | bytes 6291456 | tf_op jit(solution)/shard_map/convert_element_type | solution.py:538
  91.9 1.2 collective-permute-start.41
  94.6 1.6 %collective-permute-start.22 = (bf16[128,1024]{1,0:T(8,128)(2,1)S(1)}, bf16[128,1024]{1,0:T(8,128)(2,1)S(1)}, u32[]{:S(2)}, u32[]{:S(2)}) collective-permute-start(bf16[128,1024]{1,0:T(8,128)(2,1)S(1)} %get-tuple-element.51), channel_id=1, source_target_pairs={{0,8},{4,12},{8,0},{12,4},{16,24},{20,28},{24,16},{28,20},{1,9},{5... | collective-permute-start | bytes 786440 | tf_op jit(solution)/shard_map/ppermute | solution.py:19
  96.1 10.3 %grads.1 = (bf16[768,4096]{1,0:T(8,128)(2,1)}, bf16[384,4096]{1,0:T(8,128)(2,1)}) custom-call(s32[3]{0:T(128)} %pad_add_fusion.where_ref, bf16[768,512]{1,0:T(8,128)(2,1)} %get-tuple-element.42.dadb_ref, bf16[384,512]{1,0:T(8,128)(2,1)} %get-tuple-element.36.hid_ref, bf16[272,1024]{1,0:T(8,128)(2,1)} %copy-done, bf16[272,1024]{1,0:T(8,128)(2,1)} %copy-done.7, ...), custom_call_target="tpu_custom_call" | custom-call | flops 4831838208 | bytes 17825792 | tf_op jit(solution)/shard_map/grads/pallas_call | solution.py:435
  108.0 1.8 %collective-permute-done.42.refs_16_ = bf16[128,1024]{1,0:T(8,128)(2,1)S(1)} collective-permute-done((bf16[128,1024]{1,0:T(8,128)(2,1)}, bf16[128,1024]{1,0:T(8,128)(2,1)S(1)}, u32[]{:S(2)}, u32[]{:S(2)}) %collective-permute-start.42) | collective-permute-done | bytes 262176 | tf_op jit(solution)/shard_map/ppermute | solution.py:19
  109.9 1.5 %collective-permute-start.20 = (bf16[128,1024]{1,0:T(8,128)(2,1)S(1)}, bf16[128,1024]{1,0:T(8,128)(2,1)S(1)}, u32[]{:S(2)}, u32[]{:S(2)}) collective-permute-start(bf16[128,1024]{1,0:T(8,128)(2,1)S(1)} %get-tuple-element.50), channel_id=1, source_target_pairs={{0,4},{1,5},{2,6},{3,7},{4,0},{5,1},{6,2},{7,3},{8,12},{9,13},{10,... | collective-permute-start | bytes 786440 | tf_op jit(solution)/shard_map/ppermute | solution.py:25
  115.0 17.5 %far.1 = (bf16[768,4096]{1,0:T(8,128)(2,1)}, bf16[384,4096]{1,0:T(8,128)(2,1)}) custom-call(s32[3]{0:T(128)} %pad_add_fusion.where_ref, bf16[768,4096]{1,0:T(8,128)(2,1)} %bitcast.40, bf16[384,4096]{1,0:T(8,128)(2,1)} %bitcast.42, bf16[272,1024]{1,0:T(8,128)(2,1)} %collective-permute-done.11.refs_0_, bf16[272,1024]{1,0:T(8,128)(2,1)} %copy-done.11, ...), custom_call_target="tpu_custom_call" | custom-call | flops 9663676416 | bytes 36700160 | tf_op jit(solution)/shard_map/far/pallas_call | solution.py:328
  (129 shorter events, 18.5 us)
Async XLA Ops:
  2.4 15.7 %collective-permute-start.1 = (bf16[272,1024]{1,0:T(8,128)(2,1)S(1)}, bf16[272,1024]{1,0:T(8,128)(2,1)S(1)}, u32[]{:S(2)}, u32[]{:S(2)}) collective-permute-start(bf16[272,1024]{1,0:T(8,128)(2,1)S(1)} %fusion.1.refs_0_), channel_id=1, source_target_pairs={{0,2},{1,3},{2,0},{3,1},{4,6},{5,7},{6,4},{7,5},{8,10},{9,11},{10,... | collective-permute-start | bytes 1671176 | tf_op jit(solution)/shard_map/ppermute | solution.py:19
  7.0 25.6 %collective-permute-start.9 = (bf16[272,1024]{1,0:T(8,128)(2,1)S(1)}, bf16[272,1024]{1,0:T(8,128)(2,1)S(1)}, u32[]{:S(2)}, u32[]{:S(2)}) collective-permute-start(bf16[272,1024]{1,0:T(8,128)(2,1)S(1)} %fusion.1.refs_0_), channel_id=1, source_target_pairs={{0,8},{4,12},{8,0},{12,4},{16,24},{20,28},{24,16},{28,20},{1,9},{5... | collective-permute-start | bytes 1671176 | tf_op jit(solution)/shard_map/ppermute | solution.py:19
  8.5 26.5 %collective-permute-start.11 = (bf16[272,1024]{1,0:T(8,128)(2,1)S(1)}, bf16[272,1024]{1,0:T(8,128)(2,1)}, u32[]{:S(2)}, u32[]{:S(2)}) collective-permute-start(bf16[272,1024]{1,0:T(8,128)(2,1)S(1)} %fusion.1.refs_0_), channel_id=1, source_target_pairs={{0,16},{4,20},{8,24},{12,28},{16,0},{20,4},{24,8},{28,12},{1,17},{... | collective-permute-start | bytes 1671176 | tf_op jit(solution)/shard_map/ppermute | solution.py:19
  11.1 25.1 %collective-permute-start = (bf16[272,1024]{1,0:T(8,128)(2,1)S(1)}, bf16[272,1024]{1,0:T(8,128)(2,1)S(1)}, u32[]{:S(2)}, u32[]{:S(2)}) collective-permute-start(bf16[272,1024]{1,0:T(8,128)(2,1)S(1)} %fusion.1.refs_0_), channel_id=1, source_target_pairs={{0,1},{1,0},{2,3},{3,2},{4,5},{5,4},{6,7},{7,6},{8,9},{9,8},{10,11... | collective-permute-start | bytes 1671176 | tf_op jit(solution)/shard_map/ppermute | solution.py:19
  19.5 15.5 %collective-permute-start.5 = (bf16[128,1024]{1,0:T(8,128)(2,1)S(1)}, bf16[128,1024]{1,0:T(8,128)(2,1)S(1)}, u32[]{:S(2)}, u32[]{:S(2)}) collective-permute-start(bf16[128,1024]{1,0:T(8,128)(2,1)S(1)} %slice.56), channel_id=1, source_target_pairs={{0,4},{4,0},{8,12},{12,8},{16,20},{20,16},{24,28},{28,24},{1,5},{5... | collective-permute-start | bytes 786440 | tf_op jit(solution)/shard_map/ppermute | solution.py:19
  21.1 14.5 %collective-permute-start.6 = (bf16[144,1024]{1,0:T(8,128)(2,1)S(1)}, bf16[144,1024]{1,0:T(8,128)(2,1)S(1)}, u32[]{:S(2)}, u32[]{:S(2)}) collective-permute-start(bf16[144,1024]{1,0:T(8,128)(2,1)S(1)} %slice.57), channel_id=1, source_target_pairs={{0,2},{1,3},{2,0},{3,1},{4,6},{5,7},{6,4},{7,5},{8,10},{9,11},{10,... | collective-permute-start | bytes 884744 | tf_op jit(solution)/shard_map/ppermute | solution.py:19
  35.6 15.2 %collective-permute-start.12 = (bf16[272,1024]{1,0:T(8,128)(2,1)S(1)}, bf16[272,1024]{1,0:T(8,128)(2,1)}, u32[]{:S(2)}, u32[]{:S(2)}) collective-permute-start(bf16[272,1024]{1,0:T(8,128)(2,1)S(1)} %collective-permute-done.9.refs_9_), channel_id=1, source_target_pairs={{0,2},{1,3},{2,0},{3,1},{4,6},{5,7},{6,4},{7,5},{8,10},{9,11},{10,... | collective-permute-start | bytes 1671176 | tf_op jit(solution)/shard_map/ppermute | solution.py:19
  36.2 14.9 %collective-permute-start.16 = (bf16[272,1024]{1,0:T(8,128)(2,1)S(1)}, bf16[272,1024]{1,0:T(8,128)(2,1)}, u32[]{:S(2)}, u32[]{:S(2)}) collective-permute-start(bf16[272,1024]{1,0:T(8,128)(2,1)S(1)} %constant_dynamic-update-slice_fusion.refs_6_), channel_id=1, source_target_pairs={{0,8},{4,12},{8,0},{12,4},{16,24},{20,28},{24,16},{28,20},{1,9},{5... | collective-permute-start | bytes 1671176 | tf_op jit(solution)/shard_map/ppermute | solution.py:19
  37.1 14.2 %collective-permute-start.4 = (bf16[272,1024]{1,0:T(8,128)(2,1)S(1)}, bf16[272,1024]{1,0:T(8,128)(2,1)S(1)}, u32[]{:S(2)}, u32[]{:S(2)}) collective-permute-start(bf16[272,1024]{1,0:T(8,128)(2,1)S(1)} %collective-permute-done.3.refs_4_), channel_id=1, source_target_pairs={{0,1},{1,0},{2,3},{3,2},{4,5},{5,4},{6,7},{7,6},{8,9},{9,8},{10,11... | collective-permute-start | bytes 1671176 | tf_op jit(solution)/shard_map/ppermute | solution.py:19
  37.3 15.6 %collective-permute-start.10 = (bf16[272,1024]{1,0:T(8,128)(2,1)S(1)}, bf16[272,1024]{1,0:T(8,128)(2,1)}, u32[]{:S(2)}, u32[]{:S(2)}) collective-permute-start(bf16[272,1024]{1,0:T(8,128)(2,1)S(1)} %collective-permute-done.9.refs_9_), channel_id=1, source_target_pairs={{0,1},{1,0},{2,3},{3,2},{4,5},{5,4},{6,7},{7,6},{8,9},{9,8},{10,11... | collective-permute-start | bytes 1671176 | tf_op jit(solution)/shard_map/ppermute | solution.py:19
  52.8 18.6 %collective-permute-start.28 = (bf16[272,1024]{1,0:T(8,128)(2,1)}, bf16[272,1024]{1,0:T(8,128)(2,1)}, u32[]{:S(2)}, u32[]{:S(2)}) collective-permute-start(bf16[272,1024]{1,0:T(8,128)(2,1)} %collective-permute-done.11.refs_0_), channel_id=1, source_target_pairs={{0,2},{1,3},{2,0},{3,1},{4,6},{5,7},{6,4},{7,5},{8,10},{9,11},{10,... | collective-permute-start | bytes 1671176 | tf_op jit(solution)/shard_map/ppermute | solution.py:19
  54.2 17.3 %collective-permute-start.30 = (bf16[272,1024]{1,0:T(8,128)(2,1)}, bf16[272,1024]{1,0:T(8,128)(2,1)}, u32[]{:S(2)}, u32[]{:S(2)}) collective-permute-start(bf16[272,1024]{1,0:T(8,128)(2,1)} %collective-permute-done.11.refs_0_), channel_id=1, source_target_pairs={{0,4},{4,0},{8,12},{12,8},{16,20},{20,16},{24,28},{28,24},{1,5},{5... | collective-permute-start | bytes 1671176 | tf_op jit(solution)/shard_map/ppermute | solution.py:19
  55.7 15.8 %collective-permute-start.32 = (bf16[272,1024]{1,0:T(8,128)(2,1)}, bf16[272,1024]{1,0:T(8,128)(2,1)}, u32[]{:S(2)}, u32[]{:S(2)}) collective-permute-start(bf16[272,1024]{1,0:T(8,128)(2,1)} %collective-permute-done.11.refs_0_), channel_id=1, source_target_pairs={{0,8},{4,12},{8,0},{12,4},{16,24},{20,28},{24,16},{28,20},{1,9},{5... | collective-permute-start | bytes 1671176 | tf_op jit(solution)/shard_map/ppermute | solution.py:19
  70.9 16.6 %collective-permute-start.18 = (bf16[4,128,1024]{2,1,0:T(8,128)(2,1)}, bf16[4,128,1024]{2,1,0:T(8,128)(2,1)S(1)}, u32[]{:S(2)}, u32[]{:S(2)}) collective-permute-start(bf16[4,128,1024]{2,1,0:T(8,128)(2,1)} %get-tuple-element.31), channel_id=1, source_target_pairs={{0,1},{1,0},{2,3},{3,2},{4,5},{5,4},{6,7},{7,6},{8,9},{9,8},{10,11... | collective-permute-start | bytes 3145736 | tf_op jit(solution)/shard_map/ppermute | solution.py:19
  71.0 16.9 %collective-permute-start.21 = (bf16[4,128,1024]{2,1,0:T(8,128)(2,1)}, bf16[4,128,1024]{2,1,0:T(8,128)(2,1)S(1)}, u32[]{:S(2)}, u32[]{:S(2)}) collective-permute-start(bf16[4,128,1024]{2,1,0:T(8,128)(2,1)} %get-tuple-element.32), channel_id=1, source_target_pairs={{0,1},{1,0},{2,3},{3,2},{4,5},{5,4},{6,7},{7,6},{8,9},{9,8},{10,11... | collective-permute-start | bytes 3145736 | tf_op jit(solution)/shard_map/ppermute | solution.py:19
  71.5 14.9 %collective-permute-start.36 = (bf16[272,1024]{1,0:T(8,128)(2,1)}, bf16[272,1024]{1,0:T(8,128)(2,1)S(1)}, u32[]{:S(2)}, u32[]{:S(2)}) collective-permute-start(bf16[272,1024]{1,0:T(8,128)(2,1)} %collective-permute-done.32.refs_8_), channel_id=1, source_target_pairs={{0,2},{1,3},{2,0},{3,1},{4,6},{5,7},{6,4},{7,5},{8,10},{9,11},{10,... | collective-permute-start | bytes 1671176 | tf_op jit(solution)/shard_map/ppermute | solution.py:19
  72.4 14.5 %collective-permute-start.33 = (bf16[272,1024]{1,0:T(8,128)(2,1)}, bf16[272,1024]{1,0:T(8,128)(2,1)S(1)}, u32[]{:S(2)}, u32[]{:S(2)}) collective-permute-start(bf16[272,1024]{1,0:T(8,128)(2,1)} %collective-permute-done.28.refs_2_), channel_id=1, source_target_pairs={{0,4},{4,0},{8,12},{12,8},{16,20},{20,16},{24,28},{28,24},{1,5},{5... | collective-permute-start | bytes 1671176 | tf_op jit(solution)/shard_map/ppermute | solution.py:19
  72.9 14.3 %collective-permute-start.38 = (bf16[272,1024]{1,0:T(8,128)(2,1)}, bf16[272,1024]{1,0:T(8,128)(2,1)S(1)}, u32[]{:S(2)}, u32[]{:S(2)}) collective-permute-start(bf16[272,1024]{1,0:T(8,128)(2,1)} %collective-permute-done.30.refs_4_), channel_id=1, source_target_pairs={{0,8},{4,12},{8,0},{12,4},{16,24},{20,28},{24,16},{28,20},{1,9},{5... | collective-permute-start | bytes 1671176 | tf_op jit(solution)/shard_map/ppermute | solution.py:19
  87.8 18.6 %collective-permute-start.40 = (bf16[128,1024]{1,0:T(8,128)(2,1)S(1)}, bf16[128,1024]{1,0:T(8,128)(2,1)}, u32[]{:S(2)}, u32[]{:S(2)}) collective-permute-start(bf16[128,1024]{1,0:T(8,128)(2,1)S(1)} %slice.66), channel_id=1, source_target_pairs={{0,4},{4,0},{8,12},{12,8},{16,20},{20,16},{24,28},{28,24},{1,5},{5... | collective-permute-start | bytes 786440 | tf_op jit(solution)/shard_map/ppermute | solution.py:19
  91.9 14.7 %collective-permute-start.41 = (bf16[144,1024]{1,0:T(8,128)(2,1)S(1)}, bf16[144,1024]{1,0:T(8,128)(2,1)S(1)}, u32[]{:S(2)}, u32[]{:S(2)}) collective-permute-start(bf16[144,1024]{1,0:T(8,128)(2,1)S(1)} %slice.67), channel_id=1, source_target_pairs={{0,2},{1,3},{2,0},{3,1},{4,6},{5,7},{6,4},{7,5},{8,10},{9,11},{10,... | collective-permute-start | bytes 884744 | tf_op jit(solution)/shard_map/ppermute | solution.py:19
  109.9 22.6 %collective-permute-start.20 = (bf16[128,1024]{1,0:T(8,128)(2,1)S(1)}, bf16[128,1024]{1,0:T(8,128)(2,1)S(1)}, u32[]{:S(2)}, u32[]{:S(2)}) collective-permute-start(bf16[128,1024]{1,0:T(8,128)(2,1)S(1)} %get-tuple-element.50), channel_id=1, source_target_pairs={{0,4},{1,5},{2,6},{3,7},{4,0},{5,1},{6,2},{7,3},{8,12},{9,13},{10,... | collective-permute-start | bytes 786440 | tf_op jit(solution)/shard_map/ppermute | solution.py:25
  111.4 21.2 %collective-permute-start.19 = (bf16[128,1024]{1,0:T(8,128)(2,1)S(1)}, bf16[128,1024]{1,0:T(8,128)(2,1)S(1)}, u32[]{:S(2)}, u32[]{:S(2)}) collective-permute-start(bf16[128,1024]{1,0:T(8,128)(2,1)S(1)} %get-tuple-element.49), channel_id=1, source_target_pairs={{0,2},{1,3},{2,0},{3,1},{4,6},{5,7},{6,4},{7,5},{8,10},{9,11},{10,... | collective-permute-start | bytes 786440 | tf_op jit(solution)/shard_map/ppermute | solution.py:25
  112.5 20.0 %collective-permute-start.26 = (bf16[128,1024]{1,0:T(8,128)(2,1)S(1)}, bf16[128,1024]{1,0:T(8,128)(2,1)S(1)}, u32[]{:S(2)}, u32[]{:S(2)}) collective-permute-start(bf16[128,1024]{1,0:T(8,128)(2,1)S(1)} %fusion.3), channel_id=1, source_target_pairs={{0,8},{1,9},{2,10},{3,11},{4,12},{5,13},{6,14},{7,15},{8,0},{9,1},... | collective-permute-start | bytes 786440 | tf_op jit(solution)/shard_map/ppermute | solution.py:25
  113.4 19.2 %collective-permute-start.23 = (bf16[128,1024]{1,0:T(8,128)(2,1)S(1)}, bf16[128,1024]{1,0:T(8,128)(2,1)S(1)}, u32[]{:S(2)}, u32[]{:S(2)}) collective-permute-start(bf16[128,1024]{1,0:T(8,128)(2,1)S(1)} %fusion.4), channel_id=1, source_target_pairs={{0,6},{1,7},{2,4},{3,5},{4,2},{5,3},{6,0},{7,1},{8,14},{9,15},{10,... | collective-permute-start | bytes 786440 | tf_op jit(solution)/shard_map/ppermute | solution.py:25
  (43 other events, 453.3 us)

commit v5 on v4

--- a/solution.py
+++ b/solution.py
@@ -289,8 +289,6 @@
     dadb_ref[pl.ds(0, ffl)] = jnp.where(named, da, 0.0).astype(BF16)
     dadb_ref[pl.ds(ffl, ffl)] = jnp.where(named, dh * silu, 0.0).astype(BF16)
     hid_ref[...] = jnp.where(named, (0.5 * scale) * (silu * b), 0.0).astype(BF16)
-    for copy in added:
-        copy.wait()
     tile = oi.shape[2]
     tiles = width // tile
     leaving = {}
@@ -302,6 +300,8 @@
             copy.wait()
         gi = jnp.dot(dadb_ref[...], xs[d, :, cols], preferred_element_type=F32)
         go = 2.0 * jnp.dot(hid_ref[...], gs[d, :, cols], preferred_element_type=F32)
+        for copy in added if k == 0 else ():
+            copy.wait()
         oi[slot] = (gi + bi[:, here].astype(F32)).astype(BF16)
         oo[slot] = (go + bo[:, here].astype(F32)).astype(BF16)
         leaving[k] = (

time: 134 us -> 133 us (level)
  no operation moved by 1% of the time
where the time goes in v5:
time: 133 us
  waiting for transfers between devices  50.2 us (38%)
  Pallas kernels  42.2 us (32%)
  starting transfers between devices  32.2 us (24%)
  other arithmetic  6.04 us (5%)
  local copies, waits for them, and re-layouts  1.48 us (1%)
    ppermute x40, waiting for transfers between devices, hop(): return lax.ppermute(block, axis, [(i, i ^ bit) for i in range(count)])  50.2 us
    ppermute x40, starting transfers between devices, hop(): return lax.ppermute(block, axis, [(i, i ^ bit) for i in range(count)])  27.9 us
    pallas_call x1, Pallas kernels, far_call(): pl.pallas_call(functools.partial(far_kernel, n_tp, sizes), out_shape=[jax...  17.2 us
    pallas_call x1, Pallas kernels, rows_call(): pl.pallas_call(functools.partial(rows_kernel, n_tp, sizes, part), out_sha...  14.7 us
    pallas_call x1, Pallas kernels, grads_call(): pl.pallas_call(functools.partial(grads_kernel, steps, sizes, len(base) >...  10.3 us
    ppermute x4, starting transfers between devices, leap(): lax.ppermute(block, ('ep', 'tp'), [(i, i ^ apart) for i in range(count)])  4.33 us
  transfers between devices with their start and end apart: 44, of which 12 were waited for; matrix products, arithmetic and copies ran while one was open for 3% of the time, Pallas kernels for 32%

profile of v5, /device:TPU:0, one launch (start us, length us, event | category | flops | bytes accessed | tf_op | source)
XLA Modules:
  0.0 133.2 jit_solution(7619235794485365375)
XLA Ops:
  2.4 3.0 %collective-permute-start.1 = (bf16[272,1024]{1,0:T(8,128)(2,1)S(1)}, bf16[272,1024]{1,0:T(8,128)(2,1)S(1)}, u32[]{:S(2)}, u32[]{:S(2)}) collective-permute-start(bf16[272,1024]{1,0:T(8,128)(2,1)S(1)} %fusion.1.refs_0_), channel_id=1, source_target_pairs={{0,2},{1,3},{2,0},{3,1},{4,6},{5,7},{6,4},{7,5},{8,10},{9,11},{10,... | collective-permute-start | bytes 1671176 | tf_op jit(solution)/shard_map/ppermute | solution.py:19
  5.5 1.5 %collective-permute-start.3 = (bf16[272,1024]{1,0:T(8,128)(2,1)S(1)}, bf16[272,1024]{1,0:T(8,128)(2,1)S(1)}, u32[]{:S(2)}, u32[]{:S(2)}) collective-permute-start(bf16[272,1024]{1,0:T(8,128)(2,1)S(1)} %fusion.1.refs_0_), channel_id=1, source_target_pairs={{0,4},{4,0},{8,12},{12,8},{16,20},{20,16},{24,28},{28,24},{1,5},{5... | collective-permute-start | bytes 1671176 | tf_op jit(solution)/shard_map/ppermute | solution.py:19
  7.0 1.6 %collective-permute-start.9 = (bf16[272,1024]{1,0:T(8,128)(2,1)S(1)}, bf16[272,1024]{1,0:T(8,128)(2,1)S(1)}, u32[]{:S(2)}, u32[]{:S(2)}) collective-permute-start(bf16[272,1024]{1,0:T(8,128)(2,1)S(1)} %fusion.1.refs_0_), channel_id=1, source_target_pairs={{0,8},{4,12},{8,0},{12,4},{16,24},{20,28},{24,16},{28,20},{1,9},{5... | collective-permute-start | bytes 1671176 | tf_op jit(solution)/shard_map/ppermute | solution.py:19
  8.5 2.6 %collective-permute-start.11 = (bf16[272,1024]{1,0:T(8,128)(2,1)S(1)}, bf16[272,1024]{1,0:T(8,128)(2,1)}, u32[]{:S(2)}, u32[]{:S(2)}) collective-permute-start(bf16[272,1024]{1,0:T(8,128)(2,1)S(1)} %fusion.1.refs_0_), channel_id=1, source_target_pairs={{0,16},{4,20},{8,24},{12,28},{16,0},{20,4},{24,8},{28,12},{1,17},{... | collective-permute-start | bytes 1671176 | tf_op jit(solution)/shard_map/ppermute | solution.py:19
  11.1 7.0 %collective-permute-done.1.refs_2_ = bf16[272,1024]{1,0:T(8,128)(2,1)S(1)} collective-permute-done((bf16[272,1024]{1,0:T(8,128)(2,1)S(1)}, bf16[272,1024]{1,0:T(8,128)(2,1)S(1)}, u32[]{:S(2)}, u32[]{:S(2)}) %collective-permute-start.1) | collective-permute-done | bytes 557088 | tf_op jit(solution)/shard_map/ppermute | solution.py:19
  18.1 1.4 %collective-permute-done.3.refs_4_ = bf16[272,1024]{1,0:T(8,128)(2,1)S(1)} collective-permute-done((bf16[272,1024]{1,0:T(8,128)(2,1)S(1)}, bf16[272,1024]{1,0:T(8,128)(2,1)S(1)}, u32[]{:S(2)}, u32[]{:S(2)}) %collective-permute-start.3) | collective-permute-done | bytes 557088 | tf_op jit(solution)/shard_map/ppermute | solution.py:19
  19.5 1.5 %collective-permute-start.5 = (bf16[128,1024]{1,0:T(8,128)(2,1)S(1)}, bf16[128,1024]{1,0:T(8,128)(2,1)S(1)}, u32[]{:S(2)}, u32[]{:S(2)}) collective-permute-start(bf16[128,1024]{1,0:T(8,128)(2,1)S(1)} %slice.56), channel_id=1, source_target_pairs={{0,4},{4,0},{8,12},{12,8},{16,20},{20,16},{24,28},{28,24},{1,5},{5... | collective-permute-start | bytes 786440 | tf_op jit(solution)/shard_map/ppermute | solution.py:19
  21.6 10.9 %collective-permute-done.9.refs_9_ = bf16[272,1024]{1,0:T(8,128)(2,1)S(1)} collective-permute-done((bf16[272,1024]{1,0:T(8,128)(2,1)S(1)}, bf16[272,1024]{1,0:T(8,128)(2,1)S(1)}, u32[]{:S(2)}, u32[]{:S(2)}) %collective-permute-start.9) | collective-permute-done | bytes 557088 | tf_op jit(solution)/shard_map/ppermute | solution.py:19
  32.6 2.5 %collective-permute-done.11.refs_0_ = bf16[272,1024]{1,0:T(8,128)(2,1)} collective-permute-done((bf16[272,1024]{1,0:T(8,128)(2,1)S(1)}, bf16[272,1024]{1,0:T(8,128)(2,1)}, u32[]{:S(2)}, u32[]{:S(2)}) %collective-permute-start.11) | collective-permute-done | bytes 557088 | tf_op jit(solution)/shard_map/ppermute | solution.py:19
  37.6 10.1 %collective-permute-done.14.refs_13_ = bf16[272,1024]{1,0:T(8,128)(2,1)} collective-permute-done((bf16[272,1024]{1,0:T(8,128)(2,1)S(1)}, bf16[272,1024]{1,0:T(8,128)(2,1)}, u32[]{:S(2)}, u32[]{:S(2)}) %collective-permute-start.14) | collective-permute-done | bytes 557088 | tf_op jit(solution)/shard_map/ppermute | solution.py:19
  47.7 3.1 %collective-permute-done.12.refs_11_ = bf16[272,1024]{1,0:T(8,128)(2,1)} collective-permute-done((bf16[272,1024]{1,0:T(8,128)(2,1)S(1)}, bf16[272,1024]{1,0:T(8,128)(2,1)}, u32[]{:S(2)}, u32[]{:S(2)}) %collective-permute-start.12) | collective-permute-done | bytes 557088 | tf_op jit(solution)/shard_map/ppermute | solution.py:19
  52.8 1.4 %collective-permute-start.28 = (bf16[272,1024]{1,0:T(8,128)(2,1)}, bf16[272,1024]{1,0:T(8,128)(2,1)}, u32[]{:S(2)}, u32[]{:S(2)}) collective-permute-start(bf16[272,1024]{1,0:T(8,128)(2,1)} %collective-permute-done.11.refs_0_), channel_id=1, source_target_pairs={{0,2},{1,3},{2,0},{3,1},{4,6},{5,7},{6,4},{7,5},{8,10},{9,11},{10,... | collective-permute-start | bytes 1671176 | tf_op jit(solution)/shard_map/ppermute | solution.py:19
  54.2 1.5 %collective-permute-start.30 = (bf16[272,1024]{1,0:T(8,128)(2,1)}, bf16[272,1024]{1,0:T(8,128)(2,1)}, u32[]{:S(2)}, u32[]{:S(2)}) collective-permute-start(bf16[272,1024]{1,0:T(8,128)(2,1)} %collective-permute-done.11.refs_0_), channel_id=1, source_target_pairs={{0,4},{4,0},{8,12},{12,8},{16,20},{20,16},{24,28},{28,24},{1,5},{5... | collective-permute-start | bytes 1671176 | tf_op jit(solution)/shard_map/ppermute | solution.py:19
  56.2 14.7 %rows.1 = (bf16[768,512]{1,0:T(8,128)(2,1)}, bf16[384,512]{1,0:T(8,128)(2,1)}, bf16[8,128,1024]{2,1,0:T(8,128)(2,1)}, bf16[4,128,1024]{2,1,0:T(8,128)(2,1)}, bf16[4,128,1024]{2,1,0:T(8,128)(2,1)}) custom-call(s32[3]{0:T(128)} %pad_add_fusion.where_ref, bf16[768,4096]{1,0:T(8,128)(2,1)} %bitcast.39, bf16[384,4096]{1,0:T(8,128)(2,1)} %bitcast.41, ...), custom_call_target="tpu_custom_call" | custom-call | flops 8053063680 | bytes 17825792 | tf_op jit(solution)/shard_map/rows/pallas_call | solution.py:194
  72.9 1.6 %collective-permute-start.38 = (bf16[272,1024]{1,0:T(8,128)(2,1)}, bf16[272,1024]{1,0:T(8,128)(2,1)S(1)}, u32[]{:S(2)}, u32[]{:S(2)}) collective-permute-start(bf16[272,1024]{1,0:T(8,128)(2,1)} %collective-permute-done.30.refs_4_), channel_id=1, source_target_pairs={{0,8},{4,12},{8,0},{12,4},{16,24},{20,28},{24,16},{28,20},{1,9},{5... | collective-permute-start | bytes 1671176 | tf_op jit(solution)/shard_map/ppermute | solution.py:19
  74.5 11.8 %collective-permute-done.36.refs_10_ = bf16[272,1024]{1,0:T(8,128)(2,1)S(1)} collective-permute-done((bf16[272,1024]{1,0:T(8,128)(2,1)}, bf16[272,1024]{1,0:T(8,128)(2,1)S(1)}, u32[]{:S(2)}, u32[]{:S(2)}) %collective-permute-start.36) | collective-permute-done | bytes 557088 | tf_op jit(solution)/shard_map/ppermute | solution.py:19
  87.8 1.5 %collective-permute-start.40 = (bf16[128,1024]{1,0:T(8,128)(2,1)S(1)}, bf16[128,1024]{1,0:T(8,128)(2,1)}, u32[]{:S(2)}, u32[]{:S(2)}) collective-permute-start(bf16[128,1024]{1,0:T(8,128)(2,1)S(1)} %slice.66), channel_id=1, source_target_pairs={{0,4},{4,0},{8,12},{12,8},{16,20},{20,16},{24,28},{28,24},{1,5},{5... | collective-permute-start | bytes 786440 | tf_op jit(solution)/shard_map/ppermute | solution.py:19
  89.3 2.5 %add_convert_fusion.1 = (bf16[4,128,1024]{2,1,0:T(8,128)(2,1)S(1)}, bf16[4,128,1024]{2,1,0:T(8,128)(2,1)S(1)}) fusion(bf16[4,128,1024]{2,1,0:T(8,128)(2,1)S(1)} %collective-permute-done.18, bf16[8,128,1024]{2,1,0:T(8,128)(2,1)} %get-tuple-element.30, bf16[4,128,1024]{2,1,0:T(8,128)(2,1)S(1)} %collective-permute-done.21), kind=kLoop, calls=%fused_computation.1 | loop fusion | flops 4194304 | bytes 6291456 | tf_op jit(solution)/shard_map/convert_element_type | solution.py:538
  91.9 1.2 collective-permute-start.41
  94.6 1.6 %collective-permute-start.22 = (bf16[128,1024]{1,0:T(8,128)(2,1)S(1)}, bf16[128,1024]{1,0:T(8,128)(2,1)S(1)}, u32[]{:S(2)}, u32[]{:S(2)}) collective-permute-start(bf16[128,1024]{1,0:T(8,128)(2,1)S(1)} %get-tuple-element.51), channel_id=1, source_target_pairs={{0,8},{4,12},{8,0},{12,4},{16,24},{20,28},{24,16},{28,20},{1,9},{5... | collective-permute-start | bytes 786440 | tf_op jit(solution)/shard_map/ppermute | solution.py:19
  96.1 10.3 %grads.1 = (bf16[768,4096]{1,0:T(8,128)(2,1)}, bf16[384,4096]{1,0:T(8,128)(2,1)}) custom-call(s32[3]{0:T(128)} %pad_add_fusion.where_ref, bf16[768,512]{1,0:T(8,128)(2,1)} %get-tuple-element.42.dadb_ref, bf16[384,512]{1,0:T(8,128)(2,1)} %get-tuple-element.36.hid_ref, bf16[272,1024]{1,0:T(8,128)(2,1)} %copy-done, bf16[272,1024]{1,0:T(8,128)(2,1)} %copy-done.7, ...), custom_call_target="tpu_custom_call" | custom-call | flops 4831838208 | bytes 17825792 | tf_op jit(solution)/shard_map/grads/pallas_call | solution.py:435
  108.0 1.8 %collective-permute-done.42.refs_16_ = bf16[128,1024]{1,0:T(8,128)(2,1)S(1)} collective-permute-done((bf16[128,1024]{1,0:T(8,128)(2,1)}, bf16[128,1024]{1,0:T(8,128)(2,1)S(1)}, u32[]{:S(2)}, u32[]{:S(2)}) %collective-permute-start.42) | collective-permute-done | bytes 262176 | tf_op jit(solution)/shard_map/ppermute | solution.py:19
  109.9 1.5 %collective-permute-start.20 = (bf16[128,1024]{1,0:T(8,128)(2,1)S(1)}, bf16[128,1024]{1,0:T(8,128)(2,1)S(1)}, u32[]{:S(2)}, u32[]{:S(2)}) collective-permute-start(bf16[128,1024]{1,0:T(8,128)(2,1)S(1)} %get-tuple-element.50), channel_id=1, source_target_pairs={{0,4},{1,5},{2,6},{3,7},{4,0},{5,1},{6,2},{7,3},{8,12},{9,13},{10,... | collective-permute-start | bytes 786440 | tf_op jit(solution)/shard_map/ppermute | solution.py:25
  115.0 17.2 %far.1 = (bf16[768,4096]{1,0:T(8,128)(2,1)}, bf16[384,4096]{1,0:T(8,128)(2,1)}) custom-call(s32[3]{0:T(128)} %pad_add_fusion.where_ref, bf16[768,4096]{1,0:T(8,128)(2,1)} %bitcast.40, bf16[384,4096]{1,0:T(8,128)(2,1)} %bitcast.42, bf16[272,1024]{1,0:T(8,128)(2,1)} %collective-permute-done.11.refs_0_, bf16[272,1024]{1,0:T(8,128)(2,1)} %copy-done.11, ...), custom_call_target="tpu_custom_call" | custom-call | flops 9663676416 | bytes 36700160 | tf_op jit(solution)/shard_map/far/pallas_call | solution.py:328
  (129 shorter events, 18.5 us)
Async XLA Ops:
  2.4 15.7 %collective-permute-start.1 = (bf16[272,1024]{1,0:T(8,128)(2,1)S(1)}, bf16[272,1024]{1,0:T(8,128)(2,1)S(1)}, u32[]{:S(2)}, u32[]{:S(2)}) collective-permute-start(bf16[272,1024]{1,0:T(8,128)(2,1)S(1)} %fusion.1.refs_0_), channel_id=1, source_target_pairs={{0,2},{1,3},{2,0},{3,1},{4,6},{5,7},{6,4},{7,5},{8,10},{9,11},{10,... | collective-permute-start | bytes 1671176 | tf_op jit(solution)/shard_map/ppermute | solution.py:19
  7.0 25.6 %collective-permute-start.9 = (bf16[272,1024]{1,0:T(8,128)(2,1)S(1)}, bf16[272,1024]{1,0:T(8,128)(2,1)S(1)}, u32[]{:S(2)}, u32[]{:S(2)}) collective-permute-start(bf16[272,1024]{1,0:T(8,128)(2,1)S(1)} %fusion.1.refs_0_), channel_id=1, source_target_pairs={{0,8},{4,12},{8,0},{12,4},{16,24},{20,28},{24,16},{28,20},{1,9},{5... | collective-permute-start | bytes 1671176 | tf_op jit(solution)/shard_map/ppermute | solution.py:19
  8.5 26.5 %collective-permute-start.11 = (bf16[272,1024]{1,0:T(8,128)(2,1)S(1)}, bf16[272,1024]{1,0:T(8,128)(2,1)}, u32[]{:S(2)}, u32[]{:S(2)}) collective-permute-start(bf16[272,1024]{1,0:T(8,128)(2,1)S(1)} %fusion.1.refs_0_), channel_id=1, source_target_pairs={{0,16},{4,20},{8,24},{12,28},{16,0},{20,4},{24,8},{28,12},{1,17},{... | collective-permute-start | bytes 1671176 | tf_op jit(solution)/shard_map/ppermute | solution.py:19
  11.1 25.1 %collective-permute-start = (bf16[272,1024]{1,0:T(8,128)(2,1)S(1)}, bf16[272,1024]{1,0:T(8,128)(2,1)S(1)}, u32[]{:S(2)}, u32[]{:S(2)}) collective-permute-start(bf16[272,1024]{1,0:T(8,128)(2,1)S(1)} %fusion.1.refs_0_), channel_id=1, source_target_pairs={{0,1},{1,0},{2,3},{3,2},{4,5},{5,4},{6,7},{7,6},{8,9},{9,8},{10,11... | collective-permute-start | bytes 1671176 | tf_op jit(solution)/shard_map/ppermute | solution.py:19
  19.5 15.5 %collective-permute-start.5 = (bf16[128,1024]{1,0:T(8,128)(2,1)S(1)}, bf16[128,1024]{1,0:T(8,128)(2,1)S(1)}, u32[]{:S(2)}, u32[]{:S(2)}) collective-permute-start(bf16[128,1024]{1,0:T(8,128)(2,1)S(1)} %slice.56), channel_id=1, source_target_pairs={{0,4},{4,0},{8,12},{12,8},{16,20},{20,16},{24,28},{28,24},{1,5},{5... | collective-permute-start | bytes 786440 | tf_op jit(solution)/shard_map/ppermute | solution.py:19
  21.1 14.5 %collective-permute-start.6 = (bf16[144,1024]{1,0:T(8,128)(2,1)S(1)}, bf16[144,1024]{1,0:T(8,128)(2,1)S(1)}, u32[]{:S(2)}, u32[]{:S(2)}) collective-permute-start(bf16[144,1024]{1,0:T(8,128)(2,1)S(1)} %slice.57), channel_id=1, source_target_pairs={{0,2},{1,3},{2,0},{3,1},{4,6},{5,7},{6,4},{7,5},{8,10},{9,11},{10,... | collective-permute-start | bytes 884744 | tf_op jit(solution)/shard_map/ppermute | solution.py:19
  35.6 15.2 %collective-permute-start.12 = (bf16[272,1024]{1,0:T(8,128)(2,1)S(1)}, bf16[272,1024]{1,0:T(8,128)(2,1)}, u32[]{:S(2)}, u32[]{:S(2)}) collective-permute-start(bf16[272,1024]{1,0:T(8,128)(2,1)S(1)} %collective-permute-done.9.refs_9_), channel_id=1, source_target_pairs={{0,2},{1,3},{2,0},{3,1},{4,6},{5,7},{6,4},{7,5},{8,10},{9,11},{10,... | collective-permute-start | bytes 1671176 | tf_op jit(solution)/shard_map/ppermute | solution.py:19
  36.2 14.9 %collective-permute-start.16 = (bf16[272,1024]{1,0:T(8,128)(2,1)S(1)}, bf16[272,1024]{1,0:T(8,128)(2,1)}, u32[]{:S(2)}, u32[]{:S(2)}) collective-permute-start(bf16[272,1024]{1,0:T(8,128)(2,1)S(1)} %constant_dynamic-update-slice_fusion.refs_6_), channel_id=1, source_target_pairs={{0,8},{4,12},{8,0},{12,4},{16,24},{20,28},{24,16},{28,20},{1,9},{5... | collective-permute-start | bytes 1671176 | tf_op jit(solution)/shard_map/ppermute | solution.py:19
  37.1 14.2 %collective-permute-start.4 = (bf16[272,1024]{1,0:T(8,128)(2,1)S(1)}, bf16[272,1024]{1,0:T(8,128)(2,1)S(1)}, u32[]{:S(2)}, u32[]{:S(2)}) collective-permute-start(bf16[272,1024]{1,0:T(8,128)(2,1)S(1)} %collective-permute-done.3.refs_4_), channel_id=1, source_target_pairs={{0,1},{1,0},{2,3},{3,2},{4,5},{5,4},{6,7},{7,6},{8,9},{9,8},{10,11... | collective-permute-start | bytes 1671176 | tf_op jit(solution)/shard_map/ppermute | solution.py:19
  37.3 15.6 %collective-permute-start.10 = (bf16[272,1024]{1,0:T(8,128)(2,1)S(1)}, bf16[272,1024]{1,0:T(8,128)(2,1)}, u32[]{:S(2)}, u32[]{:S(2)}) collective-permute-start(bf16[272,1024]{1,0:T(8,128)(2,1)S(1)} %collective-permute-done.9.refs_9_), channel_id=1, source_target_pairs={{0,1},{1,0},{2,3},{3,2},{4,5},{5,4},{6,7},{7,6},{8,9},{9,8},{10,11... | collective-permute-start | bytes 1671176 | tf_op jit(solution)/shard_map/ppermute | solution.py:19
  52.8 18.6 %collective-permute-start.28 = (bf16[272,1024]{1,0:T(8,128)(2,1)}, bf16[272,1024]{1,0:T(8,128)(2,1)}, u32[]{:S(2)}, u32[]{:S(2)}) collective-permute-start(bf16[272,1024]{1,0:T(8,128)(2,1)} %collective-permute-done.11.refs_0_), channel_id=1, source_target_pairs={{0,2},{1,3},{2,0},{3,1},{4,6},{5,7},{6,4},{7,5},{8,10},{9,11},{10,... | collective-permute-start | bytes 1671176 | tf_op jit(solution)/shard_map/ppermute | solution.py:19
  54.2 17.3 %collective-permute-start.30 = (bf16[272,1024]{1,0:T(8,128)(2,1)}, bf16[272,1024]{1,0:T(8,128)(2,1)}, u32[]{:S(2)}, u32[]{:S(2)}) collective-permute-start(bf16[272,1024]{1,0:T(8,128)(2,1)} %collective-permute-done.11.refs_0_), channel_id=1, source_target_pairs={{0,4},{4,0},{8,12},{12,8},{16,20},{20,16},{24,28},{28,24},{1,5},{5... | collective-permute-start | bytes 1671176 | tf_op jit(solution)/shard_map/ppermute | solution.py:19
  55.7 15.8 %collective-permute-start.32 = (bf16[272,1024]{1,0:T(8,128)(2,1)}, bf16[272,1024]{1,0:T(8,128)(2,1)}, u32[]{:S(2)}, u32[]{:S(2)}) collective-permute-start(bf16[272,1024]{1,0:T(8,128)(2,1)} %collective-permute-done.11.refs_0_), channel_id=1, source_target_pairs={{0,8},{4,12},{8,0},{12,4},{16,24},{20,28},{24,16},{28,20},{1,9},{5... | collective-permute-start | bytes 1671176 | tf_op jit(solution)/shard_map/ppermute | solution.py:19
  70.9 16.6 %collective-permute-start.18 = (bf16[4,128,1024]{2,1,0:T(8,128)(2,1)}, bf16[4,128,1024]{2,1,0:T(8,128)(2,1)S(1)}, u32[]{:S(2)}, u32[]{:S(2)}) collective-permute-start(bf16[4,128,1024]{2,1,0:T(8,128)(2,1)} %get-tuple-element.31), channel_id=1, source_target_pairs={{0,1},{1,0},{2,3},{3,2},{4,5},{5,4},{6,7},{7,6},{8,9},{9,8},{10,11... | collective-permute-start | bytes 3145736 | tf_op jit(solution)/shard_map/ppermute | solution.py:19
  71.0 16.9 %collective-permute-start.21 = (bf16[4,128,1024]{2,1,0:T(8,128)(2,1)}, bf16[4,128,1024]{2,1,0:T(8,128)(2,1)S(1)}, u32[]{:S(2)}, u32[]{:S(2)}) collective-permute-start(bf16[4,128,1024]{2,1,0:T(8,128)(2,1)} %get-tuple-element.32), channel_id=1, source_target_pairs={{0,1},{1,0},{2,3},{3,2},{4,5},{5,4},{6,7},{7,6},{8,9},{9,8},{10,11... | collective-permute-start | bytes 3145736 | tf_op jit(solution)/shard_map/ppermute | solution.py:19
  71.5 14.9 %collective-permute-start.36 = (bf16[272,1024]{1,0:T(8,128)(2,1)}, bf16[272,1024]{1,0:T(8,128)(2,1)S(1)}, u32[]{:S(2)}, u32[]{:S(2)}) collective-permute-start(bf16[272,1024]{1,0:T(8,128)(2,1)} %collective-permute-done.32.refs_8_), channel_id=1, source_target_pairs={{0,2},{1,3},{2,0},{3,1},{4,6},{5,7},{6,4},{7,5},{8,10},{9,11},{10,... | collective-permute-start | bytes 1671176 | tf_op jit(solution)/shard_map/ppermute | solution.py:19
  72.4 14.5 %collective-permute-start.33 = (bf16[272,1024]{1,0:T(8,128)(2,1)}, bf16[272,1024]{1,0:T(8,128)(2,1)S(1)}, u32[]{:S(2)}, u32[]{:S(2)}) collective-permute-start(bf16[272,1024]{1,0:T(8,128)(2,1)} %collective-permute-done.28.refs_2_), channel_id=1, source_target_pairs={{0,4},{4,0},{8,12},{12,8},{16,20},{20,16},{24,28},{28,24},{1,5},{5... | collective-permute-start | bytes 1671176 | tf_op jit(solution)/shard_map/ppermute | solution.py:19
  72.9 14.3 %collective-permute-start.38 = (bf16[272,1024]{1,0:T(8,128)(2,1)}, bf16[272,1024]{1,0:T(8,128)(2,1)S(1)}, u32[]{:S(2)}, u32[]{:S(2)}) collective-permute-start(bf16[272,1024]{1,0:T(8,128)(2,1)} %collective-permute-done.30.refs_4_), channel_id=1, source_target_pairs={{0,8},{4,12},{8,0},{12,4},{16,24},{20,28},{24,16},{28,20},{1,9},{5... | collective-permute-start | bytes 1671176 | tf_op jit(solution)/shard_map/ppermute | solution.py:19
  87.8 18.6 %collective-permute-start.40 = (bf16[128,1024]{1,0:T(8,128)(2,1)S(1)}, bf16[128,1024]{1,0:T(8,128)(2,1)}, u32[]{:S(2)}, u32[]{:S(2)}) collective-permute-start(bf16[128,1024]{1,0:T(8,128)(2,1)S(1)} %slice.66), channel_id=1, source_target_pairs={{0,4},{4,0},{8,12},{12,8},{16,20},{20,16},{24,28},{28,24},{1,5},{5... | collective-permute-start | bytes 786440 | tf_op jit(solution)/shard_map/ppermute | solution.py:19
  91.9 14.7 %collective-permute-start.41 = (bf16[144,1024]{1,0:T(8,128)(2,1)S(1)}, bf16[144,1024]{1,0:T(8,128)(2,1)S(1)}, u32[]{:S(2)}, u32[]{:S(2)}) collective-permute-start(bf16[144,1024]{1,0:T(8,128)(2,1)S(1)} %slice.67), channel_id=1, source_target_pairs={{0,2},{1,3},{2,0},{3,1},{4,6},{5,7},{6,4},{7,5},{8,10},{9,11},{10,... | collective-permute-start | bytes 884744 | tf_op jit(solution)/shard_map/ppermute | solution.py:19
  109.9 22.4 %collective-permute-start.20 = (bf16[128,1024]{1,0:T(8,128)(2,1)S(1)}, bf16[128,1024]{1,0:T(8,128)(2,1)S(1)}, u32[]{:S(2)}, u32[]{:S(2)}) collective-permute-start(bf16[128,1024]{1,0:T(8,128)(2,1)S(1)} %get-tuple-element.50), channel_id=1, source_target_pairs={{0,4},{1,5},{2,6},{3,7},{4,0},{5,1},{6,2},{7,3},{8,12},{9,13},{10,... | collective-permute-start | bytes 786440 | tf_op jit(solution)/shard_map/ppermute | solution.py:25
  111.4 20.9 %collective-permute-start.19 = (bf16[128,1024]{1,0:T(8,128)(2,1)S(1)}, bf16[128,1024]{1,0:T(8,128)(2,1)S(1)}, u32[]{:S(2)}, u32[]{:S(2)}) collective-permute-start(bf16[128,1024]{1,0:T(8,128)(2,1)S(1)} %get-tuple-element.49), channel_id=1, source_target_pairs={{0,2},{1,3},{2,0},{3,1},{4,6},{5,7},{6,4},{7,5},{8,10},{9,11},{10,... | collective-permute-start | bytes 786440 | tf_op jit(solution)/shard_map/ppermute | solution.py:25
  112.5 19.7 %collective-permute-start.26 = (bf16[128,1024]{1,0:T(8,128)(2,1)S(1)}, bf16[128,1024]{1,0:T(8,128)(2,1)S(1)}, u32[]{:S(2)}, u32[]{:S(2)}) collective-permute-start(bf16[128,1024]{1,0:T(8,128)(2,1)S(1)} %fusion.3), channel_id=1, source_target_pairs={{0,8},{1,9},{2,10},{3,11},{4,12},{5,13},{6,14},{7,15},{8,0},{9,1},... | collective-permute-start | bytes 786440 | tf_op jit(solution)/shard_map/ppermute | solution.py:25
  113.4 18.9 %collective-permute-start.23 = (bf16[128,1024]{1,0:T(8,128)(2,1)S(1)}, bf16[128,1024]{1,0:T(8,128)(2,1)S(1)}, u32[]{:S(2)}, u32[]{:S(2)}) collective-permute-start(bf16[128,1024]{1,0:T(8,128)(2,1)S(1)} %fusion.4), channel_id=1, source_target_pairs={{0,6},{1,7},{2,4},{3,5},{4,2},{5,3},{6,0},{7,1},{8,14},{9,15},{10,... | collective-permute-start | bytes 786440 | tf_op jit(solution)/shard_map/ppermute | solution.py:25
  (43 other events, 453.3 us)
